TPU v7x, 128 devices: a whole 4x4x4 slice. The times are simulated.
128 devices in a mesh: shots: 32 (over y, z, core), depth: 4 (over x).
Axes of the slice: x: 4, y: 4, z: 4, core: 2. Of those that a mesh axis runs over, the one named last changes fastest.
Arguments:
- partials: float32 [512, 32, 4096], P('shots', 'depth'), may hold values from -6 to 6
- aperture: int32 [512], P('shots'), may hold values from -1 to 127, as said below
- owner_map: int32 [128], replicated, may hold values from 0 to 127, as said below
- dip_class: int32 [128], replicated, may hold values from 0 to 7
Outputs:
- smoothed: float32 [128, 32, 4096], P('shots', 'depth')
Inputs may be any that keep to these rules, and one draw needn't show every extreme that they name: `aperture`: ids within one shot group are distinct; at most 1 of a group's bricks have storage rows r with the same r div 4, and some group reaches 1; some group fills all 16 slots; empty slots come after live ones. `owner_map`: A permutation of the bricks.
All inputs are finite; a program needn't handle non-finite values.
Results may differ from a plain program's by a relative error of at most 0.0003.
Values sent between devices are 32-bit elements; how exact they have to be, the bound alone decides.
No kernel may reach another device: no remote copies, remote signals or barrier semaphores. Data moves between devices by JAX's collectives and lax.ppermute only.
A program may use at most 128 MiB of HBM per device.

v0:
```python
import math

import jax
import jax.numpy as jnp
from jax import lax
from jax.sharding import PartitionSpec as P

BY = 64
ITERS = 3


smoothing_rate = 0.15
tiny_value = 1e-06


def extended_2(cells, sides, width):
    for axis, dim in sides:
        count = lax.axis_size(axis)
        ends = count - 1
        head = lax.slice_in_dim(cells, 0, width, axis=dim)
        tail = lax.slice_in_dim(cells, cells.shape[dim] - width, cells.shape[dim], axis=dim)
        cells = jnp.concatenate(
            [
                lax.ppermute(tail, axis, [(i, (i + 1) % count) for i in range(ends)]),
                cells,
                lax.ppermute(head, axis, [((i + 1) % count, i) for i in range(ends)]),
            ],
            axis=dim,
        )
    return cells


def shifted(volume, step_x, step_y, row_width):
    count = volume.shape[-1]
    margin = row_width + 1
    padded = jnp.pad(volume, [(0, 0)] * (volume.ndim - 1) + [(margin, margin)])
    begin = margin + step_x * row_width + step_y
    moved = lax.slice_in_dim(padded, begin, begin + count, axis=volume.ndim - 1)
    column = jnp.arange(count) % row_width + step_y
    return jnp.where((column >= 0) & (column < row_width), moved, jnp.float32(0.0))


def smooth_x(volume, row_width):
    return (
        shifted(volume, -1, 0, row_width) + 2.0 * volume + shifted(volume, 1, 0, row_width)
    ) * 0.25


def smooth_y(volume, row_width):
    return (
        shifted(volume, 0, -1, row_width) + 2.0 * volume + shifted(volume, 0, 1, row_width)
    ) * 0.25


def derive_x(volume, row_width):
    return (shifted(volume, 1, 0, row_width) - shifted(volume, -1, 0, row_width)) * 0.5


def derive_y(volume, row_width):
    return (shifted(volume, 0, 1, row_width) - shifted(volume, 0, -1, row_width)) * 0.5


def depth_slice(extended, start, axis):
    length = extended.shape[axis] - 2
    return lax.slice_in_dim(extended, start, start + length, axis=axis)


def gradient_products(extended, row_width):
    lower_plane = depth_slice(extended, 0, 1)
    centre = depth_slice(extended, 1, 1)
    upper_plane = depth_slice(extended, 2, 1)
    along_depth = (lower_plane + 2.0 * centre + upper_plane) * 0.25
    grad_z = smooth_x(smooth_y((upper_plane - lower_plane) * 0.5, row_width), row_width)
    grad_x = smooth_y(derive_x(along_depth, row_width), row_width)
    grad_y = smooth_x(derive_y(along_depth, row_width), row_width)
    return jnp.stack(
        [
            grad_z * grad_z,
            grad_x * grad_x,
            grad_y * grad_y,
            grad_z * grad_x,
            grad_z * grad_y,
            grad_x * grad_y,
        ]
    )


def brick_normal(classes):
    tilt_angle = 0.2 + 0.1 * (classes % 4).astype(jnp.float32)
    azimuth = 0.3 + math.pi / 2.0 * (classes // 4).astype(jnp.float32)
    norm_z = jnp.cos(tilt_angle)[:, None, None]
    norm_x = (jnp.sin(tilt_angle) * jnp.cos(azimuth))[:, None, None]
    norm_y = (jnp.sin(tilt_angle) * jnp.sin(azimuth))[:, None, None]
    return (norm_z, norm_x, norm_y)


def smooth_update(extended, tensor_ext, normal, row_width):
    tensor = (
        depth_slice(tensor_ext, 0, 2)
        + 2.0 * depth_slice(tensor_ext, 1, 2)
        + depth_slice(tensor_ext, 2, 2)
    ) * 0.25
    tensor = smooth_x(smooth_y(tensor, row_width), row_width)
    lower_plane = depth_slice(extended, 0, 1)
    centre = depth_slice(extended, 1, 1)
    upper_plane = depth_slice(extended, 2, 1)
    second_zz = upper_plane + lower_plane - 2.0 * centre
    second_xx = shifted(centre, 1, 0, row_width) + shifted(centre, -1, 0, row_width) - 2.0 * centre
    second_yy = shifted(centre, 0, 1, row_width) + shifted(centre, 0, -1, row_width) - 2.0 * centre
    second_zx = (derive_x(upper_plane, row_width) - derive_x(lower_plane, row_width)) * 0.5
    second_zy = (derive_y(upper_plane, row_width) - derive_y(lower_plane, row_width)) * 0.5
    second_xy = derive_y(derive_x(centre, row_width), row_width)
    norm_z, norm_x, norm_y = normal
    curvature = (
        norm_z * norm_z * second_zz
        + norm_x * norm_x * second_xx
        + norm_y * norm_y * second_yy
        + 2.0 * norm_z * norm_x * second_zx
        + 2.0 * norm_z * norm_y * second_zy
        + 2.0 * norm_x * norm_y * second_xy
    )
    aligned = (
        norm_z * norm_z * tensor[0]
        + norm_x * norm_x * tensor[1]
        + norm_y * norm_y * tensor[2]
        + 2.0 * norm_z * norm_x * tensor[3]
        + 2.0 * norm_z * norm_y * tensor[4]
        + 2.0 * norm_x * norm_y * tensor[5]
    )
    weight = aligned / (tensor[0] + tensor[1] + tensor[2] + tiny_value)
    return centre + smoothing_rate * weight * (second_zz + second_xx + second_yy - curvature)


def local(partials, aperture, owner_map, dip_class):
    slot_count, planes, columns = partials.shape
    senders = lax.axis_size("shots")
    owned = owner_map.shape[0] // senders
    active = aperture >= 0
    slot_of = jnp.take(owner_map, jnp.maximum(aperture, 0))
    flattened = partials.reshape(slot_count, planes * columns)
    wanted = jnp.arange(owned * lax.axis_size("shots"))
    matches = (wanted[:, None] == slot_of[None, :]) & active[None, :]
    migrated = lax.psum_scatter(
        jnp.dot(
            matches.astype(jnp.float32),
            flattened,
            precision=lax.Precision.HIGHEST,
            preferred_element_type=jnp.float32,
        ),
        "shots",
        scatter_dimension=0,
        tiled=True,
    )
    migrated = migrated.reshape(owned, planes, columns)
    mine = lax.axis_index("shots") * owned + jnp.arange(owned)
    classes = jnp.sum(jnp.where(owner_map[None, :] == mine[:, None], dip_class[None, :], 0), axis=1)
    normal = brick_normal(classes)
    for sweep in range(ITERS):
        extended = extended_2(migrated, (("depth", 1),), 1)
        products = gradient_products(extended, BY)
        tensor_ext = extended_2(products, (("depth", 2),), 1)
        migrated = smooth_update(extended, tensor_ext, normal, BY)
    return migrated


def solution(mesh):
    placed = (P("shots", "depth", None), P("shots"), P(), P())
    return jax.shard_map(
        local, mesh=mesh, in_specs=placed, out_specs=P("shots", "depth", None), check_vma=False
    )
```

profile of v0, /device:TPU:34, one launch (start us, length us, event | category | flops | bytes accessed | tf_op | source)
XLA Modules:
  0.0 313.7 jit_solution(16074934823266151567)
XLA Ops:
  7.9 2.8 copy.5
  11.4 9.4 %fusion.157 = f32[128,32768]{1,0:T(8,128)} fusion(f32[16,32768]{1,0:T(8,128)S(1)} %bitcast.168, s32[16]{0:T(128)S(1)} %compare_select_fusion, pred[16]{0:T(512)(128)(4,1)S(1)} %broadcast_compare_fusion), kind=kOutput, calls=%fused_computation.295 | convolution fusion | flops 805310464 | bytes 18874448 | tf_op jit(solution)/shard_map/dot_general | solution.py:144
  23.0 178.0 %all-reduce.36.cloned.1.call-done = f32[128,32768]{1,0:T(8,128)} async-done(((f32[128,32768]{1,0:T(8,128)}), f32[128,32768]{1,0:T(8,128)}) %all-reduce.36.cloned.1.call-update) | async-done | bytes 16777232
  202.8 3.4 %collective-permute-start.1 = (f32[4,1,4096]{2,1,0:T(1,128)S(1)}, f32[4,1,4096]{2,1,0:T(1,128)S(1)}, u32[]{:S(2)}, u32[]{:S(2)}) collective-permute-start(f32[4,1,4096]{2,1,0:T(1,128)S(1)} %get-tuple-element.74), channel_id=1, source_target_pairs={{0,1},{1,2},{2,3},{4,5},{5,6},{6,7},{8,9},{9,10},{10,11},{12,13},{... | collective-permute-start | bytes 196616 | tf_op jit(solution)/shard_map/ppermute | solution.py:24
  206.2 2.5 collective-permute-start
  209.3 3.1 collective-permute-done
  216.6 2.5 collective-permute-start.3
  219.0 3.6 %collective-permute-start.2 = (f32[6,4,1,4096]{3,2,1,0:T(1,128)S(1)}, f32[6,4,1,4096]{3,2,1,0:T(1,128)S(1)}, u32[]{:S(2)}, u32[]{:S(2)}) collective-permute-start(f32[6,4,1,4096]{3,2,1,0:T(1,128)S(1)} %get-tuple-element.49), channel_id=1, source_target_pairs={{0,1},{1,2},{2,3},{4,5},{5,6},{6,7},{8,9},{9,10},{10,11},{12,13},{... | collective-permute-start | bytes 1179656 | tf_op jit(solution)/shard_map/ppermute | solution.py:24
  222.7 6.3 %collective-permute-done.3 = f32[6,4,1,4096]{3,2,1,0:T(1,128)S(1)} collective-permute-done((f32[6,4,1,4096]{3,2,1,0:T(1,128)S(1)}, f32[6,4,1,4096]{3,2,1,0:T(1,128)S(1)}, u32[]{:S(2)}, u32[]{:S(2)}) %collective-permute-start.3) | collective-permute-done | bytes 393248 | tf_op jit(solution)/shard_map/ppermute | solution.py:26
  232.7 2.4 broadcast_multiply_fusion.4
  239.0 3.4 %collective-permute-start.5 = (f32[4,1,4096]{2,1,0:T(1,128)S(1)}, f32[4,1,4096]{2,1,0:T(1,128)S(1)}, u32[]{:S(2)}, u32[]{:S(2)}) collective-permute-start(f32[4,1,4096]{2,1,0:T(1,128)S(1)} %get-tuple-element.70), channel_id=1, source_target_pairs={{0,1},{1,2},{2,3},{4,5},{5,6},{6,7},{8,9},{9,10},{10,11},{12,13},{... | collective-permute-start | bytes 196616 | tf_op jit(solution)/shard_map/ppermute | solution.py:24
  242.4 2.5 collective-permute-start.4
  245.2 3.4 %collective-permute-done.4 = f32[4,1,4096]{2,1,0:T(1,128)S(1)} collective-permute-done((f32[4,1,4096]{2,1,0:T(1,128)S(1)}, f32[4,1,4096]{2,1,0:T(1,128)S(1)}, u32[]{:S(2)}, u32[]{:S(2)}) %collective-permute-start.4) | collective-permute-done | bytes 65568 | tf_op jit(solution)/shard_map/ppermute | solution.py:26
  252.7 2.5 collective-permute-start.7
  255.2 3.6 %collective-permute-start.6 = (f32[6,4,1,4096]{3,2,1,0:T(1,128)S(1)}, f32[6,4,1,4096]{3,2,1,0:T(1,128)S(1)}, u32[]{:S(2)}, u32[]{:S(2)}) collective-permute-start(f32[6,4,1,4096]{3,2,1,0:T(1,128)S(1)} %get-tuple-element.47), channel_id=1, source_target_pairs={{0,1},{1,2},{2,3},{4,5},{5,6},{6,7},{8,9},{9,10},{10,11},{12,13},{... | collective-permute-start | bytes 1179656 | tf_op jit(solution)/shard_map/ppermute | solution.py:24
  258.8 3.8 %collective-permute-done.7 = f32[6,4,1,4096]{3,2,1,0:T(1,128)S(1)} collective-permute-done((f32[6,4,1,4096]{3,2,1,0:T(1,128)S(1)}, f32[6,4,1,4096]{3,2,1,0:T(1,128)S(1)}, u32[]{:S(2)}, u32[]{:S(2)}) %collective-permute-start.7) | collective-permute-done | bytes 393248 | tf_op jit(solution)/shard_map/ppermute | solution.py:26
  272.6 3.4 %collective-permute-start.9 = (f32[4,1,4096]{2,1,0:T(1,128)S(1)}, f32[4,1,4096]{2,1,0:T(1,128)S(1)}, u32[]{:S(2)}, u32[]{:S(2)}) collective-permute-start(f32[4,1,4096]{2,1,0:T(1,128)S(1)} %get-tuple-element.66), channel_id=1, source_target_pairs={{0,1},{1,2},{2,3},{4,5},{5,6},{6,7},{8,9},{9,10},{10,11},{12,13},{... | collective-permute-start | bytes 196616 | tf_op jit(solution)/shard_map/ppermute | solution.py:24
  276.0 2.5 collective-permute-start.8
  278.8 3.4 %collective-permute-done.8 = f32[4,1,4096]{2,1,0:T(1,128)S(1)} collective-permute-done((f32[4,1,4096]{2,1,0:T(1,128)S(1)}, f32[4,1,4096]{2,1,0:T(1,128)S(1)}, u32[]{:S(2)}, u32[]{:S(2)}) %collective-permute-start.8) | collective-permute-done | bytes 65568 | tf_op jit(solution)/shard_map/ppermute | solution.py:26
  286.3 2.5 collective-permute-start.11
  288.7 3.6 %collective-permute-start.10 = (f32[6,4,1,4096]{3,2,1,0:T(1,128)S(1)}, f32[6,4,1,4096]{3,2,1,0:T(1,128)S(1)}, u32[]{:S(2)}, u32[]{:S(2)}) collective-permute-start(f32[6,4,1,4096]{3,2,1,0:T(1,128)S(1)} %get-tuple-element.45), channel_id=1, source_target_pairs={{0,1},{1,2},{2,3},{4,5},{5,6},{6,7},{8,9},{9,10},{10,11},{12,13},{... | collective-permute-start | bytes 1179656 | tf_op jit(solution)/shard_map/ppermute | solution.py:24
  292.4 3.6 %collective-permute-done.11 = f32[6,4,1,4096]{3,2,1,0:T(1,128)S(1)} collective-permute-done((f32[6,4,1,4096]{3,2,1,0:T(1,128)S(1)}, f32[6,4,1,4096]{3,2,1,0:T(1,128)S(1)}, u32[]{:S(2)}, u32[]{:S(2)}) %collective-permute-start.11) | collective-permute-done | bytes 393248 | tf_op jit(solution)/shard_map/ppermute | solution.py:26
  295.9 2.5 collective-permute-done.10
  303.9 2.9 fusion.112
  (74 shorter events, 41.9 us)
Async XLA Ops:
  6.5 4.9 %copy-start.2 = (s32[16]{0:T(128)S(1)}, s32[16]{0:T(128)}, u32[]{:S(2)}) copy-start(s32[16]{0:T(128)} %param.5) | copy-start | bytes 196
  6.5 4.2 %copy-start = (s32[128]{0:T(128)S(1)}, s32[128]{0:T(128)}, u32[]{:S(2)}) copy-start(s32[128]{0:T(128)} %param.6) | copy-start | bytes 1540
  6.5 194.5 %all-reduce.36.cloned.1.call-start = ((), (), s32[]{:S(2)}) async-start(), calls=%async_computation | async-start | bytes 33554432
  20.8 0.7 copy-start.1
  20.8 0.9 copy-start.3
  202.8 6.6 %collective-permute-start.1 = (f32[4,1,4096]{2,1,0:T(1,128)S(1)}, f32[4,1,4096]{2,1,0:T(1,128)S(1)}, u32[]{:S(2)}, u32[]{:S(2)}) collective-permute-start(f32[4,1,4096]{2,1,0:T(1,128)S(1)} %get-tuple-element.74), channel_id=1, source_target_pairs={{0,1},{1,2},{2,3},{4,5},{5,6},{6,7},{8,9},{9,10},{10,11},{12,13},{... | collective-permute-start | bytes 196616 | tf_op jit(solution)/shard_map/ppermute | solution.py:24
  206.2 6.3 %collective-permute-start = (f32[4,1,4096]{2,1,0:T(1,128)S(1)}, f32[4,1,4096]{2,1,0:T(1,128)S(1)}, u32[]{:S(2)}, u32[]{:S(2)}) collective-permute-start(f32[4,1,4096]{2,1,0:T(1,128)S(1)} %get-tuple-element.73), channel_id=1, source_target_pairs={{1,0},{2,1},{3,2},{5,4},{6,5},{7,6},{9,8},{10,9},{11,10},{13,12},{... | collective-permute-start | bytes 196616 | tf_op jit(solution)/shard_map/ppermute | solution.py:26
  216.6 12.5 %collective-permute-start.3 = (f32[6,4,1,4096]{3,2,1,0:T(1,128)S(1)}, f32[6,4,1,4096]{3,2,1,0:T(1,128)S(1)}, u32[]{:S(2)}, u32[]{:S(2)}) collective-permute-start(f32[6,4,1,4096]{3,2,1,0:T(1,128)S(1)} %get-tuple-element.50), channel_id=1, source_target_pairs={{1,0},{2,1},{3,2},{5,4},{6,5},{7,6},{9,8},{10,9},{11,10},{13,12},{... | collective-permute-start | bytes 1179656 | tf_op jit(solution)/shard_map/ppermute | solution.py:26
  219.0 12.2 %collective-permute-start.2 = (f32[6,4,1,4096]{3,2,1,0:T(1,128)S(1)}, f32[6,4,1,4096]{3,2,1,0:T(1,128)S(1)}, u32[]{:S(2)}, u32[]{:S(2)}) collective-permute-start(f32[6,4,1,4096]{3,2,1,0:T(1,128)S(1)} %get-tuple-element.49), channel_id=1, source_target_pairs={{0,1},{1,2},{2,3},{4,5},{5,6},{6,7},{8,9},{9,10},{10,11},{12,13},{... | collective-permute-start | bytes 1179656 | tf_op jit(solution)/shard_map/ppermute | solution.py:24
  239.0 6.2 %collective-permute-start.5 = (f32[4,1,4096]{2,1,0:T(1,128)S(1)}, f32[4,1,4096]{2,1,0:T(1,128)S(1)}, u32[]{:S(2)}, u32[]{:S(2)}) collective-permute-start(f32[4,1,4096]{2,1,0:T(1,128)S(1)} %get-tuple-element.70), channel_id=1, source_target_pairs={{0,1},{1,2},{2,3},{4,5},{5,6},{6,7},{8,9},{9,10},{10,11},{12,13},{... | collective-permute-start | bytes 196616 | tf_op jit(solution)/shard_map/ppermute | solution.py:24
  242.4 6.2 %collective-permute-start.4 = (f32[4,1,4096]{2,1,0:T(1,128)S(1)}, f32[4,1,4096]{2,1,0:T(1,128)S(1)}, u32[]{:S(2)}, u32[]{:S(2)}) collective-permute-start(f32[4,1,4096]{2,1,0:T(1,128)S(1)} %get-tuple-element.69), channel_id=1, source_target_pairs={{1,0},{2,1},{3,2},{5,4},{6,5},{7,6},{9,8},{10,9},{11,10},{13,12},{... | collective-permute-start | bytes 196616 | tf_op jit(solution)/shard_map/ppermute | solution.py:26
  252.7 9.8 %collective-permute-start.7 = (f32[6,4,1,4096]{3,2,1,0:T(1,128)S(1)}, f32[6,4,1,4096]{3,2,1,0:T(1,128)S(1)}, u32[]{:S(2)}, u32[]{:S(2)}) collective-permute-start(f32[6,4,1,4096]{3,2,1,0:T(1,128)S(1)} %get-tuple-element.48), channel_id=1, source_target_pairs={{1,0},{2,1},{3,2},{5,4},{6,5},{7,6},{9,8},{10,9},{11,10},{13,12},{... | collective-permute-start | bytes 1179656 | tf_op jit(solution)/shard_map/ppermute | solution.py:26
  255.2 9.7 %collective-permute-start.6 = (f32[6,4,1,4096]{3,2,1,0:T(1,128)S(1)}, f32[6,4,1,4096]{3,2,1,0:T(1,128)S(1)}, u32[]{:S(2)}, u32[]{:S(2)}) collective-permute-start(f32[6,4,1,4096]{3,2,1,0:T(1,128)S(1)} %get-tuple-element.47), channel_id=1, source_target_pairs={{0,1},{1,2},{2,3},{4,5},{5,6},{6,7},{8,9},{9,10},{10,11},{12,13},{... | collective-permute-start | bytes 1179656 | tf_op jit(solution)/shard_map/ppermute | solution.py:24
  272.6 6.2 %collective-permute-start.9 = (f32[4,1,4096]{2,1,0:T(1,128)S(1)}, f32[4,1,4096]{2,1,0:T(1,128)S(1)}, u32[]{:S(2)}, u32[]{:S(2)}) collective-permute-start(f32[4,1,4096]{2,1,0:T(1,128)S(1)} %get-tuple-element.66), channel_id=1, source_target_pairs={{0,1},{1,2},{2,3},{4,5},{5,6},{6,7},{8,9},{9,10},{10,11},{12,13},{... | collective-permute-start | bytes 196616 | tf_op jit(solution)/shard_map/ppermute | solution.py:24
  276.0 6.2 %collective-permute-start.8 = (f32[4,1,4096]{2,1,0:T(1,128)S(1)}, f32[4,1,4096]{2,1,0:T(1,128)S(1)}, u32[]{:S(2)}, u32[]{:S(2)}) collective-permute-start(f32[4,1,4096]{2,1,0:T(1,128)S(1)} %get-tuple-element.65), channel_id=1, source_target_pairs={{1,0},{2,1},{3,2},{5,4},{6,5},{7,6},{9,8},{10,9},{11,10},{13,12},{... | collective-permute-start | bytes 196616 | tf_op jit(solution)/shard_map/ppermute | solution.py:26
  286.3 9.7 %collective-permute-start.11 = (f32[6,4,1,4096]{3,2,1,0:T(1,128)S(1)}, f32[6,4,1,4096]{3,2,1,0:T(1,128)S(1)}, u32[]{:S(2)}, u32[]{:S(2)}) collective-permute-start(f32[6,4,1,4096]{3,2,1,0:T(1,128)S(1)} %get-tuple-element.46), channel_id=1, source_target_pairs={{1,0},{2,1},{3,2},{5,4},{6,5},{7,6},{9,8},{10,9},{11,10},{13,12},{... | collective-permute-start | bytes 1179656 | tf_op jit(solution)/shard_map/ppermute | solution.py:26
  288.7 9.7 %collective-permute-start.10 = (f32[6,4,1,4096]{3,2,1,0:T(1,128)S(1)}, f32[6,4,1,4096]{3,2,1,0:T(1,128)S(1)}, u32[]{:S(2)}, u32[]{:S(2)}) collective-permute-start(f32[6,4,1,4096]{3,2,1,0:T(1,128)S(1)} %get-tuple-element.45), channel_id=1, source_target_pairs={{0,1},{1,2},{2,3},{4,5},{5,6},{6,7},{8,9},{9,10},{10,11},{12,13},{... | collective-permute-start | bytes 1179656 | tf_op jit(solution)/shard_map/ppermute | solution.py:24
Sparse Core Ops, SparseCore 0:
  21.0 180.0 all-reduce.35
where the time goes:
time: 316 us; the launch traced here: 314 us
  waiting for transfers between devices  210 us (66%)
  starting transfers between devices  35.7 us (11%)
  other arithmetic  35.2 us (11%)
  between operations  14.5 us (5%)
  matrix products  9.39 us (3%)
  local copies, waits for them, and re-layouts  9 us (3%)
    unnamed x2, waiting for transfers between devices  178 us
    ppermute x6, waiting for transfers between devices, extended_2(): lax.ppermute(head, axis, [((i + 1) % count, i) for i in range(ends)])  23.5 us
    ppermute x6, starting transfers between devices, extended_2(): lax.ppermute(tail, axis, [(i, (i + 1) % count) for i in range(ends)])  20.9 us
    ppermute x6, starting transfers between devices, extended_2(): lax.ppermute(head, axis, [((i + 1) % count, i) for i in range(ends)])  14.8 us
    dot_general x1, matrix products, local(): jnp.dot(matches.astype(jnp.float32), flattened, precision=lax.Precision.H...  9.39 us
    mul x6, other arithmetic, smooth_y(): (shifted(volume, 0, -1, row_width) + 2.0 * volume + shifted(volume, 0, 1,...  9.24 us
    ppermute x6, waiting for transfers between devices, extended_2(): lax.ppermute(tail, axis, [(i, (i + 1) % count) for i in range(ends)])  8.23 us
    add x3, other arithmetic, smooth_update(): centre + smoothing_rate * weight * (second_zz + second_xx + second_yy - c...  7.22 us
  transfers between devices with their start and end apart: 13, of which 13 were waited for; matrix products, arithmetic and copies ran while one was open for 0% of the time, Pallas kernels for 0%

commit v1 on v0

v1 whole, which is shorter than its diff:
```python
import math

import jax
import jax.numpy as jnp
from jax import lax
from jax.experimental import pallas as pl
from jax.experimental.pallas import tpu as pltpu
from jax.sharding import PartitionSpec as P

STEPS = 16
HALO = 6
PLANES = 8
DEEP = PLANES + 2 * HALO
ITERS = 3
RATE = 0.15
TINY = 1e-6
TILES = 32


def lanes():
    return lax.broadcasted_iota(jnp.int32, (8, 128), 1)


def rows():
    return lax.broadcasted_iota(jnp.int32, (8, 128), 0)


def pack_kernel(aperture, owner_map, partials, out, slot_of, place_of):
    step = pl.program_id(0)
    owners = slot_of.shape[0]
    slots = partials.shape[0]
    per_step = out.shape[0]

    @pl.when(step == 0)
    def _():
        for owner in range(owners):
            slot_of[owner] = -1
        for slot in range(slots):
            brick = aperture[slot]

            @pl.when(brick >= 0)
            def _():
                row = owner_map[brick]
                slot_of[row // 4] = slot
                place_of[row // 4] = row % 4

    for j in range(per_step):
        owner = step * per_step + j
        slot = slot_of[owner]

        @pl.when(slot >= 0)
        def _():
            for tile in range(TILES):
                out[j, (tile % 8) * 4 + tile // 8] = partials[slot, :, tile * 128 : tile * 128 + 128]
            out[j, TILES] = jnp.full((8, 128), place_of[owner], jnp.int32).astype(jnp.float32)

        @pl.when(slot < 0)
        def _():
            for tile in range(TILES):
                out[j, tile] = jnp.zeros((8, 128), jnp.float32)
            out[j, TILES] = jnp.full((8, 128), -1.0, jnp.float32)


def pack(aperture, owner_map, partials, owners):
    slots, planes, columns = partials.shape
    per_step = 4
    return pl.pallas_call(
        pack_kernel,
        grid=(owners // per_step,),
        in_specs=[
            pl.BlockSpec(memory_space=pltpu.SMEM),
            pl.BlockSpec(memory_space=pltpu.SMEM),
            pl.BlockSpec((slots, planes, columns), lambda i: (0, 0, 0)),
        ],
        out_specs=pl.BlockSpec((per_step, TILES + 1, 8, 128), lambda i: (i, 0, 0, 0)),
        out_shape=jax.ShapeDtypeStruct((owners, TILES + 1, 8, 128), jnp.float32),
        scratch_shapes=[pltpu.SMEM((owners,), jnp.int32), pltpu.SMEM((owners,), jnp.int32)],
        compiler_params=pltpu.CompilerParams(vmem_limit_bytes=24 << 20),
        name="pack_blocks",
    )(aperture, owner_map, partials)


def merge_kernel(blocks, places, out):
    step = pl.program_id(0)
    senders = blocks.shape[0]
    low = lanes() < 64
    for half in range(2):

        def add(sender, sums):
            place = places[sender, 0]
            hits = [place == float(b) for b in range(4)]
            new = []
            for quarter in range(4):
                block = blocks[sender, half * 4 + quarter]
                for b in range(4):
                    new.append(sums[quarter * 4 + b] + jnp.where(hits[b], block, 0.0))
            return tuple(new)

        zero = jnp.zeros((8, 128), jnp.float32)
        sums = lax.fori_loop(0, senders, add, (zero,) * 16, unroll=4)
        for b in range(4):
            for upper in range(2):
                even = sums[(2 * upper) * 4 + b]
                odd = sums[(2 * upper + 1) * 4 + b]
                first = jnp.where(low, even, pltpu.roll(odd, 64, 1))
                second = jnp.where(low, pltpu.roll(even, 64, 1), odd)
                base = (step * 2 + half) * 16 + b * 2 + upper
                out[pl.ds(base, 8, stride=128), :] = first
                out[pl.ds(base + 8, 8, stride=128), :] = second


def merge(received):
    senders = received.shape[0]
    return pl.pallas_call(
        merge_kernel,
        grid=(4,),
        in_specs=[
            pl.BlockSpec((senders, 8, 8, 128), lambda i: (0, i, 0, 0)),
            pl.BlockSpec((senders, 1, 8, 128), lambda i: (0, TILES, 0, 0)),
        ],
        out_specs=pl.BlockSpec((PLANES * STEPS * 8, 128), lambda i: (0, 0)),
        out_shape=jax.ShapeDtypeStruct((PLANES * STEPS * 8, 128), jnp.float32),
        compiler_params=pltpu.CompilerParams(vmem_limit_bytes=24 << 20),
        name="merge_blocks",
    )(received, received)


def set_edges(field, plane, first, last):
    left_half = lanes() < 64
    lower_row = rows() % 2 == 0
    turned = pltpu.roll(last, 64, 1)
    below = jnp.where(lower_row, 0.0, pltpu.roll(turned, 1, 0))
    field[plane, 0] = jnp.where(left_half, below, turned)
    turned = pltpu.roll(first, 64, 1)
    above = jnp.where(lower_row, pltpu.roll(turned, 7, 0), 0.0)
    field[plane, STEPS + 1] = jnp.where(left_half, turned, above)


def smooth_kernel(bounds, coefs, lower, own, upper, out, image, other, along, total, final):
    column = lanes() % 64
    first_y = column == 0
    last_y = column == 63

    def after(f):
        return jnp.where(last_y, 0.0, pltpu.roll(f, 127, 1))

    def before(f):
        return jnp.where(first_y, 0.0, pltpu.roll(f, 1, 1))

    def blur_y(f):
        pair = f + after(f)
        return pair + jnp.where(first_y, f, pltpu.roll(pair, 1, 1))

    zero = jnp.zeros((8, 128), jnp.float32)
    for plane in (HALO - 1, HALO + PLANES):
        for step in range(STEPS + 2):
            other[plane, step] = zero
            along[plane, step] = zero
            total[plane, step] = zero

    def load(source, count, offset):
        @pl.loop(0, count)
        def _(plane):
            cells = [source[plane, step] for step in range(STEPS)]
            for step in range(STEPS):
                image[plane + offset, step + 1] = cells[step]
            set_edges(image, plane + offset, cells[0], cells[-1])

    load(lower, HALO, 0)
    load(own, PLANES, HALO)
    load(upper, HALO, HALO + PLANES)

    first_plane = bounds[0]
    end_plane = bounds[1]

    for sweep in range(ITERS):
        source = image if sweep % 2 == 0 else other
        target = other if sweep % 2 == 0 else image
        margin = 2 * sweep + 1

        @pl.loop(jnp.maximum(margin, first_plane), jnp.minimum(DEEP - margin, end_plane))
        def _(plane):
            norm_z, norm_x, norm_y = coefs[0], coefs[1], coefs[2]

            def depth_pair(step):
                low, mid, high = source[plane - 1, step], source[plane, step], source[plane + 1, step]
                return (low + mid) + (mid + high), high - low

            blurred, slopes = {}, {}
            blurred[0], slopes[0] = depth_pair(0)
            blurred[1], slopes[1] = depth_pair(1)
            slope_pair = slopes[0] + slopes[1]
            blur_pair = blurred[0] + blurred[1]
            ends = []
            for step in range(1, STEPS + 1):
                blurred[step + 1], slopes[step + 1] = depth_pair(step + 1)
                next_slope = slopes[step] + slopes[step + 1]
                next_blur = blurred[step] + blurred[step + 1]
                grad_z = blur_y(slope_pair + next_slope)
                grad_x = blur_y(blurred[step + 1] - blurred[step - 1])
                wide = blur_pair + next_blur
                grad_y = after(wide) - before(wide)
                slope_pair, blur_pair = next_slope, next_blur
                aligned = norm_z * grad_z + norm_x * grad_x + norm_y * grad_y
                aligned = aligned * aligned
                whole = grad_z * grad_z + grad_x * grad_x + grad_y * grad_y
                along[plane, step] = aligned
                total[plane, step] = whole
                if step in (1, STEPS):
                    ends.append((aligned, whole))
            set_edges(along, plane, ends[0][0], ends[1][0])
            set_edges(total, plane, ends[0][1], ends[1][1])

        margin += 1

        @pl.loop(jnp.maximum(margin, first_plane), jnp.minimum(DEEP - margin, end_plane))
        def _(plane):
            c_mid, c_zz, c_xx, c_yy, c_zx, c_zy, c_xy = [coefs[3 + i] for i in range(7)]

            def blur_z(field, step):
                low, mid, high = field[plane - 1, step], field[plane, step], field[plane + 1, step]
                return (low + mid) + (mid + high)

            def both(step):
                return blur_z(along, step), blur_z(total, step)

            def depth(step):
                return source[plane - 1, step], source[plane + 1, step]

            a_now, t_now = both(0)
            a_next, t_next = both(1)
            a_pair, t_pair = a_now + a_next, t_now + t_next
            low, high = depth(0)
            slope_before = high - low
            low, high = depth(1)
            slope, stack = high - low, high + low
            u_before, u_now = source[plane, 0], source[plane, 1]
            ends = []
            for step in range(1, STEPS + 1):
                a_now, t_now = a_next, t_next
                a_next, t_next = both(step + 1)
                a_new, t_new = a_now + a_next, t_now + t_next
                aligned = blur_y(a_pair + a_new)
                whole = blur_y(t_pair + t_new)
                a_pair, t_pair = a_new, t_new
                weight = aligned / (whole + jnp.float32(TINY * 65536.0))
                low, high = depth(step + 1)
                slope_after, stack_after = high - low, high + low
                u_after = source[plane, step + 1]
                side = u_after - u_before
                skew = c_zy * slope + c_xy * side
                level = c_yy * u_now
                change = (
                    c_mid * u_now
                    + c_zz * stack
                    + c_xx * (u_after + u_before)
                    + c_zx * (slope_after - slope_before)
                    + after(level + skew)
                    + before(level - skew)
                )
                new = u_now + weight * change
                slope_before, slope, stack = slope, slope_after, stack_after
                u_before, u_now = u_now, u_after
                if sweep == ITERS - 1:
                    base = pl.multiple_of((plane - HALO) * 128, 128) + (step - 1) * 8
                    final[pl.ds(base, 8), :] = new
                else:
                    target[plane, step] = new
                    if step in (1, STEPS):
                        ends.append(new)
            if sweep < ITERS - 1:
                set_edges(target, plane, ends[0], ends[1])

    low_half = lanes() < 64
    for b in range(4):
        for upper_half in range(2):
            for k in range(8):
                base = k * 16 + b * 2 + upper_half
                first = final[pl.ds(base, 8, stride=128), :]
                second = final[pl.ds(base + 8, 8, stride=128), :]
                tile = upper_half * 16 + k
                out[b, :, tile * 128 : tile * 128 + 128] = jnp.where(low_half, first, pltpu.roll(second, 64, 1))
                tile += 8
                out[b, :, tile * 128 : tile * 128 + 128] = jnp.where(low_half, pltpu.roll(first, 64, 1), second)


def smooth(bounds, coefs, lower, own, upper, interpret=False):
    field = pltpu.VMEM((DEEP, STEPS + 2, 8, 128), jnp.float32)
    vmem = pl.BlockSpec(memory_space=pltpu.VMEM)
    return pl.pallas_call(
        smooth_kernel,
        in_specs=[pl.BlockSpec(memory_space=pltpu.SMEM), vmem, vmem, vmem, vmem],
        out_specs=vmem,
        out_shape=jax.ShapeDtypeStruct((4, PLANES, STEPS * 256), jnp.float32),
        scratch_shapes=[field, field, field, field, pltpu.VMEM((PLANES * STEPS * 8, 128), jnp.float32)],
        compiler_params=pltpu.CompilerParams(vmem_limit_bytes=32 << 20),
        name="smooth_image",
        interpret=interpret,
    )(bounds, coefs, lower, own, upper)


def coefficients(classes):
    tilt = 0.2 + 0.1 * (classes % 4).astype(jnp.float32)
    azimuth = 0.3 + math.pi / 2.0 * (classes // 4).astype(jnp.float32)
    norm_z = jnp.cos(tilt)
    norm_x = jnp.sin(tilt) * jnp.cos(azimuth)
    norm_y = jnp.sin(tilt) * jnp.sin(azimuth)
    c_zz = RATE * (1.0 - norm_z * norm_z)
    c_xx = RATE * (1.0 - norm_x * norm_x)
    c_yy = RATE * (1.0 - norm_y * norm_y)
    cross = -0.5 * RATE
    values = jnp.stack(
        [
            norm_z,
            norm_x,
            norm_y,
            -2.0 * (c_zz + c_xx + c_yy),
            c_zz,
            c_xx,
            c_yy,
            cross * norm_z * norm_x,
            cross * norm_z * norm_y,
            cross * norm_x * norm_y,
        ]
    )
    return jnp.broadcast_to(jnp.repeat(values, 2, axis=1)[:, :, None], (10, 8, 128))


def local(partials, aperture, owner_map, dip_class):
    senders = lax.axis_size("shots")
    owned = owner_map.shape[0] // senders
    sent = pack(aperture, owner_map, partials, senders)
    received = lax.all_to_all(sent, "shots", 0, 0, tiled=True)
    image = merge(received).reshape(PLANES, STEPS, 8, 128)
    depth_count = lax.axis_size("depth")
    lower = lax.ppermute(image[PLANES - HALO :], "depth", [(i, i + 1) for i in range(depth_count - 1)])
    upper = lax.ppermute(image[:HALO], "depth", [(i + 1, i) for i in range(depth_count - 1)])
    mine = lax.axis_index("shots") * owned + jnp.arange(owned)
    classes = jnp.sum(jnp.where(owner_map[None, :] == mine[:, None], dip_class[None, :], 0), axis=1)
    place = lax.axis_index("depth")
    bounds = jnp.stack([HALO - place * PLANES, HALO + (depth_count - place) * PLANES]).astype(jnp.int32)
    return smooth(bounds, coefficients(classes), lower, image, upper)


def solution(mesh):
    placed = (P("shots", "depth", None), P("shots"), P(), P())
    return jax.shard_map(
        local, mesh=mesh, in_specs=placed, out_specs=P("shots", "depth", None), check_vma=False
    )
```

time: 316 us -> 115 us (0.36)
  waiting for transfers between devices: 210 us -> 65.2 us
  other arithmetic: 35.2 us -> 0.33 us
  Pallas kernels: 0 us -> 28.5 us
  starting transfers between devices: 35.7 us -> 14.1 us
  between operations: 14.5 us -> 0.12 us
  matrix products: 9.39 us -> 0 us
    unnamed x2 -> x0, waiting for transfers between devices: 178 us -> none
    all_to_all x0 -> x1, waiting for transfers between devices: none -> 56.9 us  [local(): received = lax.all_to_all(sent, 'shots', 0, 0, tiled=True)]
    ppermute x12 -> x2, starting transfers between devices: 35.7 us -> 5.86 us  [the longest x1 3.4 us: local(): lax.ppermute(image[PLANES - HALO:], 'depth', [(i, i + 1) for i in range(d...]
    pallas_call x0 -> x3, Pallas kernels: none -> 28.5 us  [the longest x1 22.7 us: smooth(): pl.pallas_call(smooth_kernel, in_specs=[pl.BlockSpec(memory_space=pltpu.S...]
    ppermute x12 -> x2, waiting for transfers between devices: 31.8 us -> 8.33 us  [the longest x1 5.2 us: local(): lax.ppermute(image[PLANES - HALO:], 'depth', [(i, i + 1) for i in range(d...]
    mul x20 -> x1, other arithmetic: 21.1 us -> 0.07 us  [coefficients(): cross * norm_x * norm_y]
    dot_general x1 -> x0, matrix products: 9.39 us -> none  [local(): jnp.dot(matches.astype(jnp.float32), flattened, precision=lax.Precision.H...]
    all_to_all x0 -> x1, starting transfers between devices: none -> 8.25 us  [local(): received = lax.all_to_all(sent, 'shots', 0, 0, tiled=True)]
  transfers between devices with their start and end apart: 13 -> 3, of which waited for: 13 -> 3; matrix products, arithmetic and copies ran while one was open for 0% -> 1% of each run, Pallas kernels for 0% -> 0%
where the time goes in v1:
time: 115 us; the launch traced here: 114 us
  waiting for transfers between devices  65.2 us (57%)
  Pallas kernels  28.5 us (25%)
  starting transfers between devices  14.1 us (12%)
  local copies, waits for them, and re-layouts  6.19 us (5%)
    all_to_all x1, waiting for transfers between devices, local(): received = lax.all_to_all(sent, 'shots', 0, 0, tiled=True)  56.9 us
    pallas_call x1, Pallas kernels, smooth(): pl.pallas_call(smooth_kernel, in_specs=[pl.BlockSpec(memory_space=pltpu.S...  22.7 us
    all_to_all x1, starting transfers between devices, local(): received = lax.all_to_all(sent, 'shots', 0, 0, tiled=True)  8.25 us
    ppermute x1, waiting for transfers between devices, local(): lax.ppermute(image[PLANES - HALO:], 'depth', [(i, i + 1) for i in range(d...  5.2 us
    unnamed x12, local copies, waits for them, and re-layouts  4.95 us
    pallas_call x1, Pallas kernels, merge(): pl.pallas_call(merge_kernel, grid=(4,), in_specs=[pl.BlockSpec((senders,...  4.36 us
    ppermute x1, starting transfers between devices, local(): lax.ppermute(image[PLANES - HALO:], 'depth', [(i, i + 1) for i in range(d...  3.4 us
    ppermute x1, waiting for transfers between devices, local(): lax.ppermute(image[:HALO], 'depth', [(i + 1, i) for i in range(depth_coun...  3.13 us
  transfers between devices with their start and end apart: 3, of which 3 were waited for; matrix products, arithmetic and copies ran while one was open for 1% of the time, Pallas kernels for 0%

profile of v1, /device:TPU:34, one launch (start us, length us, event | category | flops | bytes accessed | tf_op | source)
XLA Modules:
  0.0 114.5 jit_solution(680753713160542989)
XLA Ops:
  0.0 1.6 %copy-done.1 = f32[16,8,4096]{2,1,0:T(8,128)S(1)} copy-done((f32[16,8,4096]{2,1,0:T(8,128)S(1)}, f32[16,8,4096]{2,1,0:T(8,128)}, u32[]{:S(2)}) %copy-start.1) | copy-done | bytes 2097176
  1.6 0.7 copy-done.2
  2.2 0.7 copy-done.4
  2.9 1.5 %pack_blocks.1 = f32[32,33,8,128]{3,2,1,0:T(8,128)S(1)} custom-call(s32[16]{0:T(128)S(1)} %copy-done.4, s32[128]{0:T(128)S(1)} %copy-done.2, f32[16,8,4096]{2,1,0:T(8,128)S(1)} %copy-done.1), custom_call_target="tpu_custom_call" | custom-call | tf_op jit(solution)/shard_map/pack_blocks/pallas_call | solution.py:67
  4.4 2.0 %copy-done = f32[32,33,8,128]{3,2,1,0:T(8,128)} copy-done((f32[32,33,8,128]{3,2,1,0:T(8,128)}, f32[32,33,8,128]{3,2,1,0:T(8,128)S(1)}, u32[]{:S(2)}) %copy-start) | copy-done | bytes 4325400
  6.5 8.3 %all-to-all-start = ((f32[32,33,8,128]{3,2,1,0:T(8,128)}), f32[32,33,8,128]{3,2,1,0:T(8,128)}, u32[]{:S(2)}, u32[]{:S(2)}) async-start(f32[32,33,8,128]{3,2,1,0:T(8,128)} %copy-done), calls=%async_computation | async-start | bytes 8650752 | tf_op jit(solution)/shard_map/all_to_all | solution.py:333
  14.8 56.9 %all-to-all-done.blocks.places = f32[32,33,8,128]{3,2,1,0:T(8,128)} async-done(((f32[32,33,8,128]{3,2,1,0:T(8,128)}), f32[32,33,8,128]{3,2,1,0:T(8,128)}, u32[]{:S(2)}, u32[]{:S(2)}) %all-to-all-start) | async-done | bytes 4325408 | tf_op jit(solution)/shard_map/all_to_all | solution.py:333
  71.6 4.4 %merge_blocks.1 = f32[1024,128]{1,0:T(8,128)S(1)} custom-call(f32[32,33,8,128]{3,2,1,0:T(8,128)} %all-to-all-done.blocks.places, f32[32,33,8,128]{3,2,1,0:T(8,128)} %all-to-all-done.blocks.places), custom_call_target="tpu_custom_call" | custom-call | tf_op jit(solution)/shard_map/merge_blocks/pallas_call | solution.py:114
  76.1 3.4 %collective-permute-start = (f32[6,16,8,128]{3,2,1,0:T(8,128)S(1)}, f32[6,16,8,128]{3,2,1,0:T(8,128)S(1)}, u32[]{:S(2)}, u32[]{:S(2)}) collective-permute-start(f32[6,16,8,128]{3,2,1,0:T(8,128)S(1)} %bitcast.61), channel_id=1, source_target_pairs={{0,1},{1,2},{2,3},{4,5},{5,6},{6,7},{8,9},{9,10},{10,11},{12,13},{... | collective-permute-start | bytes 1179656 | tf_op jit(solution)/shard_map/ppermute | solution.py:336
  79.5 2.5 %collective-permute-start.1 = (f32[6,16,8,128]{3,2,1,0:T(8,128)S(1)}, f32[6,16,8,128]{3,2,1,0:T(8,128)S(1)}, u32[]{:S(2)}, u32[]{:S(2)}) collective-permute-start(f32[6,16,8,128]{3,2,1,0:T(8,128)S(1)} %bitcast.60), channel_id=1, source_target_pairs={{1,0},{2,1},{3,2},{5,4},{6,5},{7,6},{9,8},{10,9},{11,10},{13,12},{... | collective-permute-start | bytes 1179656 | tf_op jit(solution)/shard_map/ppermute | solution.py:337
  82.0 0.2 select_reduce_fusion
  82.2 0.1 copy.27
  82.3 0.1 copy.24
  82.4 0.1 copy.23
  82.5 0.1 copy.22
  82.6 0.1 copy.25
  82.7 0.1 copy.26
  82.8 0.1 copy.21
  82.9 0.1 copy.20
  83.0 0.1 copy.19
  83.1 0.1 stack.11
  83.4 5.2 %collective-permute-done.lower = f32[6,16,8,128]{3,2,1,0:T(8,128)S(1)} collective-permute-done((f32[6,16,8,128]{3,2,1,0:T(8,128)S(1)}, f32[6,16,8,128]{3,2,1,0:T(8,128)S(1)}, u32[]{:S(2)}, u32[]{:S(2)}) %collective-permute-start) | collective-permute-done | bytes 393248 | tf_op jit(solution)/shard_map/ppermute | solution.py:336
  88.6 3.1 %collective-permute-done.1.upper = f32[6,16,8,128]{3,2,1,0:T(8,128)S(1)} collective-permute-done((f32[6,16,8,128]{3,2,1,0:T(8,128)S(1)}, f32[6,16,8,128]{3,2,1,0:T(8,128)S(1)}, u32[]{:S(2)}, u32[]{:S(2)}) %collective-permute-start.1) | collective-permute-done | bytes 393248 | tf_op jit(solution)/shard_map/ppermute | solution.py:337
  91.8 22.7 %smooth_image.1 = f32[4,8,4096]{2,1,0:T(8,128)} custom-call(s32[2]{0:T(128)S(1)} %pad_add_fusion.bounds, f32[10,8,128]{2,1,0:T(8,128)S(1)} %broadcast_in_dim.29.coefs, f32[6,16,8,128]{3,2,1,0:T(8,128)S(1)} %collective-permute-done.lower, f32[8,16,8,128]{3,2,1,0:T(8,128)S(1)} %bitcast.59, f32[6,16,8,128]{3,2,1,0:T(8,128)S(1)} %collective-permute-done.1.upper), custom_call_target="tpu_custom_call" | custom-call | tf_op jit(solution)/shard_map/smooth_image/pallas_call | solution.py:290
  (16 shorter events, 0.5 us)
Async XLA Ops:
  0.0 1.6 %copy-start.1 = (f32[16,8,4096]{2,1,0:T(8,128)S(1)}, f32[16,8,4096]{2,1,0:T(8,128)}, u32[]{:S(2)}) copy-start(f32[16,8,4096]{2,1,0:T(8,128)} %partials.1) | copy-start | bytes 6291460
  1.6 0.7 copy-start.2
  2.2 0.7 copy-start.4
  4.4 2.0 %copy-start = (f32[32,33,8,128]{3,2,1,0:T(8,128)}, f32[32,33,8,128]{3,2,1,0:T(8,128)S(1)}, u32[]{:S(2)}) copy-start(f32[32,33,8,128]{3,2,1,0:T(8,128)S(1)} %pack_blocks.1) | copy-start | bytes 12976132
  6.5 65.2 %all-to-all-start = ((f32[32,33,8,128]{3,2,1,0:T(8,128)}), f32[32,33,8,128]{3,2,1,0:T(8,128)}, u32[]{:S(2)}, u32[]{:S(2)}) async-start(f32[32,33,8,128]{3,2,1,0:T(8,128)} %copy-done), calls=%async_computation | async-start | bytes 8650752 | tf_op jit(solution)/shard_map/all_to_all | solution.py:333
  14.7 67.2 %copy-start.3 = (s32[128]{0:T(128)S(1)}, s32[128]{0:T(128)}, u32[]{:S(2)}) copy-start(s32[128]{0:T(128)} %owner_map.1) | copy-start | bytes 1540
  14.7 67.2 %copy-start.5 = (s32[128]{0:T(128)S(1)}, s32[128]{0:T(128)}, u32[]{:S(2)}) copy-start(s32[128]{0:T(128)} %param.7) | copy-start | bytes 1540
  76.1 12.6 %collective-permute-start = (f32[6,16,8,128]{3,2,1,0:T(8,128)S(1)}, f32[6,16,8,128]{3,2,1,0:T(8,128)S(1)}, u32[]{:S(2)}, u32[]{:S(2)}) collective-permute-start(f32[6,16,8,128]{3,2,1,0:T(8,128)S(1)} %bitcast.61), channel_id=1, source_target_pairs={{0,1},{1,2},{2,3},{4,5},{5,6},{6,7},{8,9},{9,10},{10,11},{12,13},{... | collective-permute-start | bytes 1179656 | tf_op jit(solution)/shard_map/ppermute | solution.py:336
  79.5 12.3 %collective-permute-start.1 = (f32[6,16,8,128]{3,2,1,0:T(8,128)S(1)}, f32[6,16,8,128]{3,2,1,0:T(8,128)S(1)}, u32[]{:S(2)}, u32[]{:S(2)}) collective-permute-start(f32[6,16,8,128]{3,2,1,0:T(8,128)S(1)} %bitcast.60), channel_id=1, source_target_pairs={{1,0},{2,1},{3,2},{5,4},{6,5},{7,6},{9,8},{10,9},{11,10},{13,12},{... | collective-permute-start | bytes 1179656 | tf_op jit(solution)/shard_map/ppermute | solution.py:337

commit v2 on v1

--- a/solution.py
+++ b/solution.py
@@ -15,6 +15,7 @@
 RATE = 0.15
 TINY = 1e-6
 TILES = 32
+GROUP = 2
 
 
 def lanes():
@@ -136,7 +137,7 @@
     field[plane, STEPS + 1] = jnp.where(left_half, turned, above)
 
 
-def smooth_kernel(bounds, coefs, lower, own, upper, out, image, other, along, total, final):
+def smooth_kernel(bounds, coefs, lower, own, upper, out, image, other, blur, slope, along, total, final):
     column = lanes() % 64
     first_y = column == 0
     last_y = column == 63
@@ -148,15 +149,16 @@
         return jnp.where(first_y, 0.0, pltpu.roll(f, 1, 1))
 
     def blur_y(f):
-        pair = f + after(f)
-        return pair + jnp.where(first_y, f, pltpu.roll(pair, 1, 1))
+        return (f + after(f)) + (f + before(f))
 
     zero = jnp.zeros((8, 128), jnp.float32)
+
+    def clear(field, plane):
+        for step in range(STEPS + 2):
+            field[plane, step] = zero
+
     for plane in (HALO - 1, HALO + PLANES):
-        for step in range(STEPS + 2):
-            other[plane, step] = zero
-            along[plane, step] = zero
-            total[plane, step] = zero
+        clear(other, plane)
 
     def load(source, count, offset):
         @pl.loop(0, count)
@@ -173,103 +175,126 @@
     first_plane = bounds[0]
     end_plane = bounds[1]
 
+    def along_y(source, plane):
+        for step in range(STEPS + 2):
+            cells = source[plane, step]
+            up, down = after(cells), before(cells)
+            blur[plane, step] = (cells + cells) + (up + down)
+            slope[plane, step] = up - down
+
+    def depth_blur(field, plane, step):
+        deep = [field[plane - 1 + k, step] for k in range(GROUP + 2)]
+        pairs = [deep[k] + deep[k + 1] for k in range(GROUP + 1)]
+        return [pairs[k] + pairs[k + 1] for k in range(GROUP)], deep
+
+    def depth_slope(deep):
+        return [deep[k + 2] - deep[k] for k in range(GROUP)]
+
     for sweep in range(ITERS):
         source = image if sweep % 2 == 0 else other
         target = other if sweep % 2 == 0 else image
         margin = 2 * sweep + 1
-
-        @pl.loop(jnp.maximum(margin, first_plane), jnp.minimum(DEEP - margin, end_plane))
-        def _(plane):
+        start = jnp.maximum(margin, first_plane - 1)
+        stop = jnp.minimum(DEEP - margin, end_plane + 1)
+
+        for k in range(GROUP + 1):
+            along_y(source, start - 1 + k)
+
+        @pl.loop(0, (stop - start) // GROUP)
+        def _(group):
+            plane = start + group * GROUP
+            for k in range(GROUP):
+                along_y(source, plane + GROUP + k)
             norm_z, norm_x, norm_y = coefs[0], coefs[1], coefs[2]
 
-            def depth_pair(step):
-                low, mid, high = source[plane - 1, step], source[plane, step], source[plane + 1, step]
-                return (low + mid) + (mid + high), high - low
-
-            blurred, slopes = {}, {}
-            blurred[0], slopes[0] = depth_pair(0)
-            blurred[1], slopes[1] = depth_pair(1)
-            slope_pair = slopes[0] + slopes[1]
-            blur_pair = blurred[0] + blurred[1]
-            ends = []
+            flat, steep, wide = {}, {}, {}
+
+            def prepare(step):
+                flat[step], deep = depth_blur(blur, plane, step)
+                steep[step] = depth_slope(deep)
+                wide[step], _ = depth_blur(slope, plane, step)
+
+            prepare(0)
+            prepare(1)
+            steep_pair = [steep[0][k] + steep[1][k] for k in range(GROUP)]
+            wide_pair = [wide[0][k] + wide[1][k] for k in range(GROUP)]
+            ends = {}
             for step in range(1, STEPS + 1):
-                blurred[step + 1], slopes[step + 1] = depth_pair(step + 1)
-                next_slope = slopes[step] + slopes[step + 1]
-                next_blur = blurred[step] + blurred[step + 1]
-                grad_z = blur_y(slope_pair + next_slope)
-                grad_x = blur_y(blurred[step + 1] - blurred[step - 1])
-                wide = blur_pair + next_blur
-                grad_y = after(wide) - before(wide)
-                slope_pair, blur_pair = next_slope, next_blur
-                aligned = norm_z * grad_z + norm_x * grad_x + norm_y * grad_y
-                aligned = aligned * aligned
-                whole = grad_z * grad_z + grad_x * grad_x + grad_y * grad_y
-                along[plane, step] = aligned
-                total[plane, step] = whole
-                if step in (1, STEPS):
-                    ends.append((aligned, whole))
-            set_edges(along, plane, ends[0][0], ends[1][0])
-            set_edges(total, plane, ends[0][1], ends[1][1])
+                prepare(step + 1)
+                for k in range(GROUP):
+                    steep_next = steep[step][k] + steep[step + 1][k]
+                    wide_next = wide[step][k] + wide[step + 1][k]
+                    grad_z = steep_pair[k] + steep_next
+                    grad_x = flat[step + 1][k] - flat[step - 1][k]
+                    grad_y = wide_pair[k] + wide_next
+                    steep_pair[k], wide_pair[k] = steep_next, wide_next
+                    aligned = norm_z * grad_z + norm_x * grad_x + norm_y * grad_y
+                    aligned = aligned * aligned
+                    whole = grad_z * grad_z + grad_x * grad_x + grad_y * grad_y
+                    along[plane + k, step] = aligned
+                    total[plane + k, step] = whole
+                    if step in (1, STEPS):
+                        ends[step, k] = (aligned, whole)
+            for k in range(GROUP):
+                set_edges(along, plane + k, ends[1, k][0], ends[STEPS, k][0])
+                set_edges(total, plane + k, ends[1, k][1], ends[STEPS, k][1])
+
+        for outside, edge in ((first_plane == HALO, HALO - 1), (end_plane == HALO + PLANES, HALO + PLANES)):
+
+            @pl.when(outside)
+            def _():
+                clear(along, edge)
+                clear(total, edge)
 
         margin += 1
-
-        @pl.loop(jnp.maximum(margin, first_plane), jnp.minimum(DEEP - margin, end_plane))
-        def _(plane):
+        begin = jnp.maximum(margin, first_plane)
+        finish = jnp.minimum(DEEP - margin, end_plane)
+
+        @pl.loop(0, (finish - begin) // GROUP)
+        def _(group):
+            plane = begin + group * GROUP
             c_mid, c_zz, c_xx, c_yy, c_zx, c_zy, c_xy = [coefs[3 + i] for i in range(7)]
-
-            def blur_z(field, step):
-                low, mid, high = field[plane - 1, step], field[plane, step], field[plane + 1, step]
-                return (low + mid) + (mid + high)
-
-            def both(step):
-                return blur_z(along, step), blur_z(total, step)
-
-            def depth(step):
-                return source[plane - 1, step], source[plane + 1, step]
-
-            a_now, t_now = both(0)
-            a_next, t_next = both(1)
-            a_pair, t_pair = a_now + a_next, t_now + t_next
-            low, high = depth(0)
-            slope_before = high - low
-            low, high = depth(1)
-            slope, stack = high - low, high + low
-            u_before, u_now = source[plane, 0], source[plane, 1]
-            ends = []
+            a_cells, t_cells, deep, tilted = {}, {}, {}, {}
+
+            def prepare(step):
+                a_cells[step], _ = depth_blur(along, plane, step)
+                t_cells[step], _ = depth_blur(total, plane, step)
+                deep[step] = [source[plane - 1 + k, step] for k in range(GROUP + 2)]
+                steep = depth_slope(deep[step])
+                tilted[step] = [c_zx * steep[k] + c_xy * slope[plane + k, step] for k in range(GROUP)]
+
+            prepare(0)
+            prepare(1)
+            a_pair = [a_cells[0][k] + a_cells[1][k] for k in range(GROUP)]
+            t_pair = [t_cells[0][k] + t_cells[1][k] for k in range(GROUP)]
+            ends = {}
             for step in range(1, STEPS + 1):
-                a_now, t_now = a_next, t_next
-                a_next, t_next = both(step + 1)
-                a_new, t_new = a_now + a_next, t_now + t_next
-                aligned = blur_y(a_pair + a_new)
-                whole = blur_y(t_pair + t_new)
-                a_pair, t_pair = a_new, t_new
-                weight = aligned / (whole + jnp.float32(TINY * 65536.0))
-                low, high = depth(step + 1)
-                slope_after, stack_after = high - low, high + low
-                u_after = source[plane, step + 1]
-                side = u_after - u_before
-                skew = c_zy * slope + c_xy * side
-                level = c_yy * u_now
-                change = (
-                    c_mid * u_now
-                    + c_zz * stack
-                    + c_xx * (u_after + u_before)
-                    + c_zx * (slope_after - slope_before)
-                    + after(level + skew)
-                    + before(level - skew)
-                )
-                new = u_now + weight * change
-                slope_before, slope, stack = slope, slope_after, stack_after
-                u_before, u_now = u_now, u_after
-                if sweep == ITERS - 1:
-                    base = pl.multiple_of((plane - HALO) * 128, 128) + (step - 1) * 8
-                    final[pl.ds(base, 8), :] = new
-                else:
-                    target[plane, step] = new
-                    if step in (1, STEPS):
-                        ends.append(new)
+                prepare(step + 1)
+                lean = depth_slope([slope[plane - 1 + k, step] for k in range(GROUP + 2)])
+                for k in range(GROUP):
+                    a_new = a_cells[step][k] + a_cells[step + 1][k]
+                    t_new = t_cells[step][k] + t_cells[step + 1][k]
+                    aligned = blur_y(a_pair[k] + a_new)
+                    whole = blur_y(t_pair[k] + t_new)
+                    a_pair[k], t_pair[k] = a_new, t_new
+                    weight = aligned / (whole + jnp.float32(TINY * 65536.0))
+                    now = deep[step][k + 1]
+                    change = (
+                        (c_mid * now + c_zz * (deep[step][k] + deep[step][k + 2]))
+                        + (c_xx * (deep[step - 1][k + 1] + deep[step + 1][k + 1]) + c_yy * blur[plane + k, step])
+                        + ((tilted[step + 1][k] - tilted[step - 1][k]) + c_zy * lean[k])
+                    )
+                    new = now + weight * change
+                    if sweep == ITERS - 1:
+                        base = pl.multiple_of((plane + k - HALO) * 128, 128) + (step - 1) * 8
+                        final[pl.ds(base, 8), :] = new
+                    else:
+                        target[plane + k, step] = new
+                        if step in (1, STEPS):
+                            ends[step, k] = new
             if sweep < ITERS - 1:
-                set_edges(target, plane, ends[0], ends[1])
+                for k in range(GROUP):
+                    set_edges(target, plane + k, ends[1, k], ends[STEPS, k])
 
     low_half = lanes() < 64
     for b in range(4):
@@ -285,14 +310,14 @@
 
 
 def smooth(bounds, coefs, lower, own, upper, interpret=False):
-    field = pltpu.VMEM((DEEP, STEPS + 2, 8, 128), jnp.float32)
+    field = pltpu.VMEM((DEEP + GROUP, STEPS + 2, 8, 128), jnp.float32)
     vmem = pl.BlockSpec(memory_space=pltpu.VMEM)
     return pl.pallas_call(
         smooth_kernel,
         in_specs=[pl.BlockSpec(memory_space=pltpu.SMEM), vmem, vmem, vmem, vmem],
         out_specs=vmem,
         out_shape=jax.ShapeDtypeStruct((4, PLANES, STEPS * 256), jnp.float32),
-        scratch_shapes=[field, field, field, field, pltpu.VMEM((PLANES * STEPS * 8, 128), jnp.float32)],
+        scratch_shapes=[field] * 6 + [pltpu.VMEM((PLANES * STEPS * 8, 128), jnp.float32)],
         compiler_params=pltpu.CompilerParams(vmem_limit_bytes=32 << 20),
         name="smooth_image",
         interpret=interpret,
@@ -314,7 +339,7 @@
             norm_z,
             norm_x,
             norm_y,
-            -2.0 * (c_zz + c_xx + c_yy),
+            -2.0 * (c_zz + c_xx + 2.0 * c_yy),
             c_zz,
             c_xx,
             c_yy,

time: 115 us -> 106 us (0.922)
  Pallas kernels: 28.5 us -> 19.9 us
    pallas_call x1, Pallas kernels: 22.7 us -> 14.1 us  [smooth(): pl.pallas_call(smooth_kernel, in_specs=[pl.BlockSpec(memory_space=pltpu.S...]
where the time goes in v2:
time: 106 us
  waiting for transfers between devices  65.2 us (62%)
  Pallas kernels  19.9 us (19%)
  starting transfers between devices  14.1 us (13%)
  local copies, waits for them, and re-layouts  6.19 us (6%)
    all_to_all x1, waiting for transfers between devices, local(): received = lax.all_to_all(sent, 'shots', 0, 0, tiled=True)  56.9 us
    pallas_call x1, Pallas kernels, smooth(): pl.pallas_call(smooth_kernel, in_specs=[pl.BlockSpec(memory_space=pltpu.S...  14.1 us
    all_to_all x1, starting transfers between devices, local(): received = lax.all_to_all(sent, 'shots', 0, 0, tiled=True)  8.25 us
    ppermute x1, waiting for transfers between devices, local(): lax.ppermute(image[PLANES - HALO:], 'depth', [(i, i + 1) for i in range(d...  5.2 us
    unnamed x12, local copies, waits for them, and re-layouts  4.95 us
    pallas_call x1, Pallas kernels, merge(): pl.pallas_call(merge_kernel, grid=(4,), in_specs=[pl.BlockSpec((senders,...  4.36 us
    ppermute x1, starting transfers between devices, local(): lax.ppermute(image[PLANES - HALO:], 'depth', [(i, i + 1) for i in range(d...  3.4 us
    ppermute x1, waiting for transfers between devices, local(): lax.ppermute(image[:HALO], 'depth', [(i + 1, i) for i in range(depth_coun...  3.13 us
  transfers between devices with their start and end apart: 3, of which 3 were waited for; matrix products, arithmetic and copies ran while one was open for 1% of the time, Pallas kernels for 0%

profile of v2, /device:TPU:34, one launch (start us, length us, event | category | flops | bytes accessed | tf_op | source)
XLA Modules:
  0.0 105.9 jit_solution(16320196851975349603)
XLA Ops:
  0.0 1.6 %copy-done.1 = f32[16,8,4096]{2,1,0:T(8,128)S(1)} copy-done((f32[16,8,4096]{2,1,0:T(8,128)S(1)}, f32[16,8,4096]{2,1,0:T(8,128)}, u32[]{:S(2)}) %copy-start.1) | copy-done | bytes 2097176
  1.6 0.7 copy-done.2
  2.2 0.7 copy-done.4
  2.9 1.5 %pack_blocks.1 = f32[32,33,8,128]{3,2,1,0:T(8,128)S(1)} custom-call(s32[16]{0:T(128)S(1)} %copy-done.4, s32[128]{0:T(128)S(1)} %copy-done.2, f32[16,8,4096]{2,1,0:T(8,128)S(1)} %copy-done.1), custom_call_target="tpu_custom_call" | custom-call | tf_op jit(solution)/shard_map/pack_blocks/pallas_call | solution.py:68
  4.4 2.0 %copy-done = f32[32,33,8,128]{3,2,1,0:T(8,128)} copy-done((f32[32,33,8,128]{3,2,1,0:T(8,128)}, f32[32,33,8,128]{3,2,1,0:T(8,128)S(1)}, u32[]{:S(2)}) %copy-start) | copy-done | bytes 4325400
  6.5 8.3 %all-to-all-start = ((f32[32,33,8,128]{3,2,1,0:T(8,128)}), f32[32,33,8,128]{3,2,1,0:T(8,128)}, u32[]{:S(2)}, u32[]{:S(2)}) async-start(f32[32,33,8,128]{3,2,1,0:T(8,128)} %copy-done), calls=%async_computation | async-start | bytes 8650752 | tf_op jit(solution)/shard_map/all_to_all | solution.py:358
  14.8 56.9 %all-to-all-done.blocks.places = f32[32,33,8,128]{3,2,1,0:T(8,128)} async-done(((f32[32,33,8,128]{3,2,1,0:T(8,128)}), f32[32,33,8,128]{3,2,1,0:T(8,128)}, u32[]{:S(2)}, u32[]{:S(2)}) %all-to-all-start) | async-done | bytes 4325408 | tf_op jit(solution)/shard_map/all_to_all | solution.py:358
  71.6 4.4 %merge_blocks.1 = f32[1024,128]{1,0:T(8,128)S(1)} custom-call(f32[32,33,8,128]{3,2,1,0:T(8,128)} %all-to-all-done.blocks.places, f32[32,33,8,128]{3,2,1,0:T(8,128)} %all-to-all-done.blocks.places), custom_call_target="tpu_custom_call" | custom-call | tf_op jit(solution)/shard_map/merge_blocks/pallas_call | solution.py:115
  76.1 3.4 %collective-permute-start = (f32[6,16,8,128]{3,2,1,0:T(8,128)S(1)}, f32[6,16,8,128]{3,2,1,0:T(8,128)S(1)}, u32[]{:S(2)}, u32[]{:S(2)}) collective-permute-start(f32[6,16,8,128]{3,2,1,0:T(8,128)S(1)} %bitcast.61), channel_id=1, source_target_pairs={{0,1},{1,2},{2,3},{4,5},{5,6},{6,7},{8,9},{9,10},{10,11},{12,13},{... | collective-permute-start | bytes 1179656 | tf_op jit(solution)/shard_map/ppermute | solution.py:361
  79.5 2.5 %collective-permute-start.1 = (f32[6,16,8,128]{3,2,1,0:T(8,128)S(1)}, f32[6,16,8,128]{3,2,1,0:T(8,128)S(1)}, u32[]{:S(2)}, u32[]{:S(2)}) collective-permute-start(f32[6,16,8,128]{3,2,1,0:T(8,128)S(1)} %bitcast.60), channel_id=1, source_target_pairs={{1,0},{2,1},{3,2},{5,4},{6,5},{7,6},{9,8},{10,9},{11,10},{13,12},{... | collective-permute-start | bytes 1179656 | tf_op jit(solution)/shard_map/ppermute | solution.py:362
  82.0 0.2 select_reduce_fusion
  82.2 0.1 copy.27
  82.3 0.1 copy.24
  82.4 0.1 copy.23
  82.5 0.1 copy.22
  82.6 0.1 copy.25
  82.7 0.1 copy.26
  82.8 0.1 copy.21
  82.9 0.1 copy.20
  83.0 0.1 copy.19
  83.2 0.1 stack.11
  83.4 5.2 %collective-permute-done.lower = f32[6,16,8,128]{3,2,1,0:T(8,128)S(1)} collective-permute-done((f32[6,16,8,128]{3,2,1,0:T(8,128)S(1)}, f32[6,16,8,128]{3,2,1,0:T(8,128)S(1)}, u32[]{:S(2)}, u32[]{:S(2)}) %collective-permute-start) | collective-permute-done | bytes 393248 | tf_op jit(solution)/shard_map/ppermute | solution.py:361
  88.6 3.1 %collective-permute-done.1.upper = f32[6,16,8,128]{3,2,1,0:T(8,128)S(1)} collective-permute-done((f32[6,16,8,128]{3,2,1,0:T(8,128)S(1)}, f32[6,16,8,128]{3,2,1,0:T(8,128)S(1)}, u32[]{:S(2)}, u32[]{:S(2)}) %collective-permute-start.1) | collective-permute-done | bytes 393248 | tf_op jit(solution)/shard_map/ppermute | solution.py:362
  91.8 14.1 %smooth_image.1 = f32[4,8,4096]{2,1,0:T(8,128)} custom-call(s32[2]{0:T(128)S(1)} %pad_add_fusion.bounds, f32[10,8,128]{2,1,0:T(8,128)S(1)} %broadcast_in_dim.29.coefs, f32[6,16,8,128]{3,2,1,0:T(8,128)S(1)} %collective-permute-done.lower, f32[8,16,8,128]{3,2,1,0:T(8,128)S(1)} %bitcast.59, f32[6,16,8,128]{3,2,1,0:T(8,128)S(1)} %collective-permute-done.1.upper), custom_call_target="tpu_custom_call" | custom-call | tf_op jit(solution)/shard_map/smooth_image/pallas_call | solution.py:315
  (16 shorter events, 0.5 us)
Async XLA Ops:
  0.0 1.6 %copy-start.1 = (f32[16,8,4096]{2,1,0:T(8,128)S(1)}, f32[16,8,4096]{2,1,0:T(8,128)}, u32[]{:S(2)}) copy-start(f32[16,8,4096]{2,1,0:T(8,128)} %partials.1) | copy-start | bytes 6291460
  1.6 0.7 copy-start.2
  2.2 0.7 copy-start.4
  4.4 2.0 %copy-start = (f32[32,33,8,128]{3,2,1,0:T(8,128)}, f32[32,33,8,128]{3,2,1,0:T(8,128)S(1)}, u32[]{:S(2)}) copy-start(f32[32,33,8,128]{3,2,1,0:T(8,128)S(1)} %pack_blocks.1) | copy-start | bytes 12976132
  6.5 65.2 %all-to-all-start = ((f32[32,33,8,128]{3,2,1,0:T(8,128)}), f32[32,33,8,128]{3,2,1,0:T(8,128)}, u32[]{:S(2)}, u32[]{:S(2)}) async-start(f32[32,33,8,128]{3,2,1,0:T(8,128)} %copy-done), calls=%async_computation | async-start | bytes 8650752 | tf_op jit(solution)/shard_map/all_to_all | solution.py:358
  14.7 67.2 %copy-start.3 = (s32[128]{0:T(128)S(1)}, s32[128]{0:T(128)}, u32[]{:S(2)}) copy-start(s32[128]{0:T(128)} %owner_map.1) | copy-start | bytes 1540
  14.8 67.2 %copy-start.5 = (s32[128]{0:T(128)S(1)}, s32[128]{0:T(128)}, u32[]{:S(2)}) copy-start(s32[128]{0:T(128)} %param.7) | copy-start | bytes 1540
  76.1 12.6 %collective-permute-start = (f32[6,16,8,128]{3,2,1,0:T(8,128)S(1)}, f32[6,16,8,128]{3,2,1,0:T(8,128)S(1)}, u32[]{:S(2)}, u32[]{:S(2)}) collective-permute-start(f32[6,16,8,128]{3,2,1,0:T(8,128)S(1)} %bitcast.61), channel_id=1, source_target_pairs={{0,1},{1,2},{2,3},{4,5},{5,6},{6,7},{8,9},{9,10},{10,11},{12,13},{... | collective-permute-start | bytes 1179656 | tf_op jit(solution)/shard_map/ppermute | solution.py:361
  79.5 12.3 %collective-permute-start.1 = (f32[6,16,8,128]{3,2,1,0:T(8,128)S(1)}, f32[6,16,8,128]{3,2,1,0:T(8,128)S(1)}, u32[]{:S(2)}, u32[]{:S(2)}) collective-permute-start(f32[6,16,8,128]{3,2,1,0:T(8,128)S(1)} %bitcast.60), channel_id=1, source_target_pairs={{1,0},{2,1},{3,2},{5,4},{6,5},{7,6},{9,8},{10,9},{11,10},{13,12},{... | collective-permute-start | bytes 1179656 | tf_op jit(solution)/shard_map/ppermute | solution.py:362

commit v3 on v2

--- a/solution.py
+++ b/solution.py
@@ -26,104 +26,123 @@
     return lax.broadcasted_iota(jnp.int32, (8, 128), 0)
 
 
-def pack_kernel(aperture, owner_map, partials, out, slot_of, place_of):
-    step = pl.program_id(0)
-    owners = slot_of.shape[0]
+def pack_kernel(aperture_hbm, owner_map_hbm, partials, out, aperture, owner_map, places, table_sems, block_sems, place_sem):
     slots = partials.shape[0]
-    per_step = out.shape[0]
-
-    @pl.when(step == 0)
-    def _():
-        for owner in range(owners):
-            slot_of[owner] = -1
-        for slot in range(slots):
-            brick = aperture[slot]
-
-            @pl.when(brick >= 0)
-            def _():
-                row = owner_map[brick]
-                slot_of[row // 4] = slot
-                place_of[row // 4] = row % 4
-
-    for j in range(per_step):
-        owner = step * per_step + j
-        slot = slot_of[owner]
-
-        @pl.when(slot >= 0)
+    columns = partials.shape[2]
+    tables = [
+        pltpu.make_async_copy(aperture_hbm, aperture, table_sems.at[0]),
+        pltpu.make_async_copy(owner_map_hbm, owner_map, table_sems.at[1]),
+    ]
+    for copy in tables:
+        copy.start()
+    for owner in range(places.shape[0]):
+        places[owner] = jnp.full((8, 128), -1.0, jnp.float32)
+    for copy in tables:
+        copy.wait()
+
+    def block(slot, owner):
+        return pltpu.make_async_copy(partials.at[slot], out.at[owner, :, 0:columns], block_sems.at[slot])
+
+    for slot in range(slots):
+        brick = aperture[slot]
+
+        @pl.when(brick >= 0)
         def _():
-            for tile in range(TILES):
-                out[j, (tile % 8) * 4 + tile // 8] = partials[slot, :, tile * 128 : tile * 128 + 128]
-            out[j, TILES] = jnp.full((8, 128), place_of[owner], jnp.int32).astype(jnp.float32)
-
-        @pl.when(slot < 0)
+            row = owner_map[brick]
+            owner = row // 4
+            block(slot, owner).start()
+            places[owner] = jnp.full((8, 128), row % 4, jnp.int32).astype(jnp.float32)
+
+    labels = pltpu.make_async_copy(places, out.at[:, :, columns : columns + 128], place_sem)
+    labels.start()
+    for slot in range(slots):
+
+        @pl.when(aperture[slot] >= 0)
         def _():
-            for tile in range(TILES):
-                out[j, tile] = jnp.zeros((8, 128), jnp.float32)
-            out[j, TILES] = jnp.full((8, 128), -1.0, jnp.float32)
+            block(slot, 0).wait()
+
+    labels.wait()
 
 
 def pack(aperture, owner_map, partials, owners):
     slots, planes, columns = partials.shape
-    per_step = 4
+    hbm = pl.BlockSpec(memory_space=pltpu.HBM)
     return pl.pallas_call(
         pack_kernel,
-        grid=(owners // per_step,),
-        in_specs=[
-            pl.BlockSpec(memory_space=pltpu.SMEM),
-            pl.BlockSpec(memory_space=pltpu.SMEM),
-            pl.BlockSpec((slots, planes, columns), lambda i: (0, 0, 0)),
+        in_specs=[hbm, hbm, hbm],
+        out_specs=hbm,
+        out_shape=jax.ShapeDtypeStruct((owners, planes, columns + 128), jnp.float32),
+        scratch_shapes=[
+            pltpu.SMEM(aperture.shape, jnp.int32),
+            pltpu.SMEM(owner_map.shape, jnp.int32),
+            pltpu.VMEM((owners, planes, 128), jnp.float32),
+            pltpu.SemaphoreType.DMA((2,)),
+            pltpu.SemaphoreType.DMA((slots,)),
+            pltpu.SemaphoreType.DMA,
         ],
-        out_specs=pl.BlockSpec((per_step, TILES + 1, 8, 128), lambda i: (i, 0, 0, 0)),
-        out_shape=jax.ShapeDtypeStruct((owners, TILES + 1, 8, 128), jnp.float32),
-        scratch_shapes=[pltpu.SMEM((owners,), jnp.int32), pltpu.SMEM((owners,), jnp.int32)],
-        compiler_params=pltpu.CompilerParams(vmem_limit_bytes=24 << 20),
+        compiler_params=pltpu.CompilerParams(vmem_limit_bytes=60 << 20),
         name="pack_blocks",
     )(aperture, owner_map, partials)
 
 
-def merge_kernel(blocks, places, out):
-    step = pl.program_id(0)
-    senders = blocks.shape[0]
+def merge_kernel(received, out, places, blocks, sums, place_sem, block_sems):
+    senders, planes, columns = blocks.shape
+    labels = pltpu.make_async_copy(received.at[:, 0:1, columns : columns + 128], places, place_sem)
+    labels.start()
+    for brick in range(4):
+        for tile in range(TILES):
+            sums[brick, tile] = jnp.zeros((8, 128), jnp.float32)
+    labels.wait()
+
+    def block(sender):
+        return pltpu.make_async_copy(
+            received.at[sender, :, 0:columns], blocks.at[sender], block_sems.at[sender]
+        )
+
+    for sender in range(senders):
+
+        @pl.when(places[sender, 0, 0] >= 0.0)
+        def _():
+            block(sender).start()
+
+    for sender in range(senders):
+        place = places[sender, 0, 0].astype(jnp.int32)
+
+        @pl.when(place >= 0)
+        def _():
+            block(sender).wait()
+            for tile in range(TILES):
+                sums[place, tile] += blocks[sender, :, tile * 128 : tile * 128 + 128]
+
     low = lanes() < 64
-    for half in range(2):
-
-        def add(sender, sums):
-            place = places[sender, 0]
-            hits = [place == float(b) for b in range(4)]
-            new = []
-            for quarter in range(4):
-                block = blocks[sender, half * 4 + quarter]
-                for b in range(4):
-                    new.append(sums[quarter * 4 + b] + jnp.where(hits[b], block, 0.0))
-            return tuple(new)
-
-        zero = jnp.zeros((8, 128), jnp.float32)
-        sums = lax.fori_loop(0, senders, add, (zero,) * 16, unroll=4)
-        for b in range(4):
-            for upper in range(2):
-                even = sums[(2 * upper) * 4 + b]
-                odd = sums[(2 * upper + 1) * 4 + b]
-                first = jnp.where(low, even, pltpu.roll(odd, 64, 1))
-                second = jnp.where(low, pltpu.roll(even, 64, 1), odd)
-                base = (step * 2 + half) * 16 + b * 2 + upper
-                out[pl.ds(base, 8, stride=128), :] = first
-                out[pl.ds(base + 8, 8, stride=128), :] = second
+    for b in range(4):
+        for upper in range(2):
+            for k in range(8):
+                even = sums[b, upper * 16 + k]
+                odd = sums[b, upper * 16 + 8 + k]
+                base = k * 16 + b * 2 + upper
+                out[pl.ds(base, 8, stride=128), :] = jnp.where(low, even, pltpu.roll(odd, 64, 1))
+                out[pl.ds(base + 8, 8, stride=128), :] = jnp.where(low, pltpu.roll(even, 64, 1), odd)
 
 
 def merge(received):
-    senders = received.shape[0]
+    senders, planes, columns = received.shape
+    columns -= 128
     return pl.pallas_call(
         merge_kernel,
-        grid=(4,),
-        in_specs=[
-            pl.BlockSpec((senders, 8, 8, 128), lambda i: (0, i, 0, 0)),
-            pl.BlockSpec((senders, 1, 8, 128), lambda i: (0, TILES, 0, 0)),
+        in_specs=[pl.BlockSpec(memory_space=pltpu.HBM)],
+        out_specs=pl.BlockSpec(memory_space=pltpu.VMEM),
+        out_shape=jax.ShapeDtypeStruct((PLANES * STEPS * 8, 128), jnp.float32),
+        scratch_shapes=[
+            pltpu.SMEM((senders, 1, 128), jnp.float32),
+            pltpu.VMEM((senders, planes, columns), jnp.float32),
+            pltpu.VMEM((4, TILES, 8, 128), jnp.float32),
+            pltpu.SemaphoreType.DMA,
+            pltpu.SemaphoreType.DMA((senders,)),
         ],
-        out_specs=pl.BlockSpec((PLANES * STEPS * 8, 128), lambda i: (0, 0)),
-        out_shape=jax.ShapeDtypeStruct((PLANES * STEPS * 8, 128), jnp.float32),
-        compiler_params=pltpu.CompilerParams(vmem_limit_bytes=24 << 20),
+        compiler_params=pltpu.CompilerParams(vmem_limit_bytes=48 << 20),
         name="merge_blocks",
-    )(received, received)
+    )(received)
 
 
 def set_edges(field, plane, first, last):

time: 106 us -> 163 us (1.54)
  Pallas kernels: 19.9 us -> 82.7 us
  local copies, waits for them, and re-layouts: 6.19 us -> 1.25 us
    pallas_call x2, Pallas kernels: 5.86 us -> 68.6 us  [the longest x1 65.5 us: pack(): pl.pallas_call(pack_kernel, in_specs=[hbm, hbm, hbm], out_specs=hbm, out_...]
    unnamed x12 -> x4, local copies, waits for them, and re-layouts: 4.95 us -> 0.01 us
where the time goes in v3:
time: 163 us
  Pallas kernels  82.7 us (51%)
  waiting for transfers between devices  65.2 us (40%)
  starting transfers between devices  13.6 us (8%)
    pallas_call x1, Pallas kernels, pack(): pl.pallas_call(pack_kernel, in_specs=[hbm, hbm, hbm], out_specs=hbm, out_...  65.5 us
    all_to_all x1, waiting for transfers between devices, local(): received = lax.all_to_all(sent, 'shots', 0, 0, tiled=True)  56.9 us
    pallas_call x1, Pallas kernels, smooth(): pl.pallas_call(smooth_kernel, in_specs=[pl.BlockSpec(memory_space=pltpu.S...  14.2 us
    all_to_all x1, starting transfers between devices, local(): received = lax.all_to_all(sent, 'shots', 0, 0, tiled=True)  7.71 us
    ppermute x1, waiting for transfers between devices, local(): lax.ppermute(image[PLANES - HALO:], 'depth', [(i, i + 1) for i in range(d...  5.24 us
    ppermute x1, starting transfers between devices, local(): lax.ppermute(image[PLANES - HALO:], 'depth', [(i, i + 1) for i in range(d...  3.4 us
  transfers between devices with their start and end apart: 3, of which 3 were waited for; matrix products, arithmetic and copies ran while one was open for 1% of the time, Pallas kernels for 0%

profile of v3, /device:TPU:34, one launch (start us, length us, event | category | flops | bytes accessed | tf_op | source)
XLA Modules:
  0.0 163.2 jit_solution(5625197760875595213)
XLA Ops:
  0.0 65.5 %pack_blocks.1 = f32[32,8,4224]{2,1,0:T(8,128)} custom-call(s32[16]{0:T(128)} %aperture_hbm.1, s32[128]{0:T(128)} %owner_map_hbm.1, f32[16,8,4096]{2,1,0:T(8,128)} %partials.1), custom_call_target="tpu_custom_call" | custom-call | tf_op jit(solution)/shard_map/pack_blocks/pallas_call | solution.py:70
  65.5 7.7 %all-to-all-start = ((f32[32,8,4224]{2,1,0:T(8,128)}), f32[32,8,4224]{2,1,0:T(8,128)}, u32[]{:S(2)}, u32[]{:S(2)}) async-start(f32[32,8,4224]{2,1,0:T(8,128)} %pack_blocks.1), calls=%async_computation | async-start | bytes 8650752 | tf_op jit(solution)/shard_map/all_to_all | solution.py:377
  73.2 56.9 %all-to-all-done.received = f32[32,8,4224]{2,1,0:T(8,128)} async-done(((f32[32,8,4224]{2,1,0:T(8,128)}), f32[32,8,4224]{2,1,0:T(8,128)}, u32[]{:S(2)}, u32[]{:S(2)}) %all-to-all-start) | async-done | bytes 4325408 | tf_op jit(solution)/shard_map/all_to_all | solution.py:377
  130.1 3.1 %merge_blocks.1 = f32[1024,128]{1,0:T(8,128)S(1)} custom-call(f32[32,8,4224]{2,1,0:T(8,128)} %all-to-all-done.received), custom_call_target="tpu_custom_call" | custom-call | tf_op jit(solution)/shard_map/merge_blocks/pallas_call | solution.py:131
  133.3 3.4 %collective-permute-start = (f32[6,16,8,128]{3,2,1,0:T(8,128)S(1)}, f32[6,16,8,128]{3,2,1,0:T(8,128)S(1)}, u32[]{:S(2)}, u32[]{:S(2)}) collective-permute-start(f32[6,16,8,128]{3,2,1,0:T(8,128)S(1)} %bitcast.61), channel_id=1, source_target_pairs={{0,1},{1,2},{2,3},{4,5},{5,6},{6,7},{8,9},{9,10},{10,11},{12,13},{... | collective-permute-start | bytes 1179656 | tf_op jit(solution)/shard_map/ppermute | solution.py:380
  136.7 2.5 %collective-permute-start.1 = (f32[6,16,8,128]{3,2,1,0:T(8,128)S(1)}, f32[6,16,8,128]{3,2,1,0:T(8,128)S(1)}, u32[]{:S(2)}, u32[]{:S(2)}) collective-permute-start(f32[6,16,8,128]{3,2,1,0:T(8,128)S(1)} %bitcast.60), channel_id=1, source_target_pairs={{1,0},{2,1},{3,2},{5,4},{6,5},{7,6},{9,8},{10,9},{11,10},{13,12},{... | collective-permute-start | bytes 1179656 | tf_op jit(solution)/shard_map/ppermute | solution.py:381
  139.2 0.2 select_reduce_fusion
  139.4 0.1 copy.27
  139.5 0.1 copy.24
  139.6 0.1 copy.23
  139.7 0.1 copy.22
  139.8 0.1 copy.25
  139.9 0.1 copy.26
  140.0 0.1 copy.21
  140.1 0.1 copy.20
  140.2 0.1 copy.19
  140.3 0.1 copy.18
  140.4 0.1 stack.11
  140.5 0.1 copy.28
  140.5 0.1 pad_add_fusion.bounds
  140.6 5.2 %collective-permute-done.lower = f32[6,16,8,128]{3,2,1,0:T(8,128)S(1)} collective-permute-done((f32[6,16,8,128]{3,2,1,0:T(8,128)S(1)}, f32[6,16,8,128]{3,2,1,0:T(8,128)S(1)}, u32[]{:S(2)}, u32[]{:S(2)}) %collective-permute-start) | collective-permute-done | bytes 393248 | tf_op jit(solution)/shard_map/ppermute | solution.py:380
  145.9 3.1 %collective-permute-done.1.upper = f32[6,16,8,128]{3,2,1,0:T(8,128)S(1)} collective-permute-done((f32[6,16,8,128]{3,2,1,0:T(8,128)S(1)}, f32[6,16,8,128]{3,2,1,0:T(8,128)S(1)}, u32[]{:S(2)}, u32[]{:S(2)}) %collective-permute-start.1) | collective-permute-done | bytes 393248 | tf_op jit(solution)/shard_map/ppermute | solution.py:381
  149.0 0.1 broadcast_in_dim.29.coefs
  149.1 14.2 %smooth_image.1 = f32[4,8,4096]{2,1,0:T(8,128)} custom-call(s32[2]{0:T(128)S(1)} %pad_add_fusion.bounds, f32[10,8,128]{2,1,0:T(8,128)S(1)} %broadcast_in_dim.29.coefs, f32[6,16,8,128]{3,2,1,0:T(8,128)S(1)} %collective-permute-done.lower, f32[8,16,8,128]{3,2,1,0:T(8,128)S(1)} %bitcast.59, f32[6,16,8,128]{3,2,1,0:T(8,128)S(1)} %collective-permute-done.1.upper), custom_call_target="tpu_custom_call" | custom-call | tf_op jit(solution)/shard_map/smooth_image/pallas_call | solution.py:334
  (8 shorter events, 0.1 us)
Async XLA Ops:
  65.5 64.6 %all-to-all-start = ((f32[32,8,4224]{2,1,0:T(8,128)}), f32[32,8,4224]{2,1,0:T(8,128)}, u32[]{:S(2)}, u32[]{:S(2)}) async-start(f32[32,8,4224]{2,1,0:T(8,128)} %pack_blocks.1), calls=%async_computation | async-start | bytes 8650752 | tf_op jit(solution)/shard_map/all_to_all | solution.py:377
  73.2 65.9 %copy-start = (s32[128]{0:T(128)S(1)}, s32[128]{0:T(128)}, u32[]{:S(2)}) copy-start(s32[128]{0:T(128)} %owner_map_hbm.1) | copy-start | bytes 1540
  73.2 65.9 %copy-start.1 = (s32[128]{0:T(128)S(1)}, s32[128]{0:T(128)}, u32[]{:S(2)}) copy-start(s32[128]{0:T(128)} %param.7) | copy-start | bytes 1540
  133.3 12.6 %collective-permute-start = (f32[6,16,8,128]{3,2,1,0:T(8,128)S(1)}, f32[6,16,8,128]{3,2,1,0:T(8,128)S(1)}, u32[]{:S(2)}, u32[]{:S(2)}) collective-permute-start(f32[6,16,8,128]{3,2,1,0:T(8,128)S(1)} %bitcast.61), channel_id=1, source_target_pairs={{0,1},{1,2},{2,3},{4,5},{5,6},{6,7},{8,9},{9,10},{10,11},{12,13},{... | collective-permute-start | bytes 1179656 | tf_op jit(solution)/shard_map/ppermute | solution.py:380
  136.7 12.3 %collective-permute-start.1 = (f32[6,16,8,128]{3,2,1,0:T(8,128)S(1)}, f32[6,16,8,128]{3,2,1,0:T(8,128)S(1)}, u32[]{:S(2)}, u32[]{:S(2)}) collective-permute-start(f32[6,16,8,128]{3,2,1,0:T(8,128)S(1)} %bitcast.60), channel_id=1, source_target_pairs={{1,0},{2,1},{3,2},{5,4},{6,5},{7,6},{9,8},{10,9},{11,10},{13,12},{... | collective-permute-start | bytes 1179656 | tf_op jit(solution)/shard_map/ppermute | solution.py:381

commit v4 on v3

--- a/solution.py
+++ b/solution.py
@@ -26,7 +26,9 @@
     return lax.broadcasted_iota(jnp.int32, (8, 128), 0)
 
 
-def pack_kernel(aperture_hbm, owner_map_hbm, partials, out, aperture, owner_map, places, table_sems, block_sems, place_sem):
+def pack_kernel(
+    aperture_hbm, owner_map_hbm, partials, out, aperture, owner_map, blocks, places, table_sems, in_sems, out_sems, place_sem
+):
     slots = partials.shape[0]
     columns = partials.shape[2]
     tables = [
@@ -35,15 +37,19 @@
     ]
     for copy in tables:
         copy.start()
+    fetches = [pltpu.make_async_copy(partials.at[slot], blocks.at[slot], in_sems.at[slot]) for slot in range(slots)]
+    for fetch in fetches:
+        fetch.start()
     for owner in range(places.shape[0]):
         places[owner] = jnp.full((8, 128), -1.0, jnp.float32)
     for copy in tables:
         copy.wait()
 
     def block(slot, owner):
-        return pltpu.make_async_copy(partials.at[slot], out.at[owner, :, 0:columns], block_sems.at[slot])
+        return pltpu.make_async_copy(blocks.at[slot], out.at[owner, :, 0:columns], out_sems.at[slot])
 
     for slot in range(slots):
+        fetches[slot].wait()
         brick = aperture[slot]
 
         @pl.when(brick >= 0)
@@ -75,8 +81,10 @@
         scratch_shapes=[
             pltpu.SMEM(aperture.shape, jnp.int32),
             pltpu.SMEM(owner_map.shape, jnp.int32),
+            pltpu.VMEM(partials.shape, jnp.float32),
             pltpu.VMEM((owners, planes, 128), jnp.float32),
             pltpu.SemaphoreType.DMA((2,)),
+            pltpu.SemaphoreType.DMA((slots,)),
             pltpu.SemaphoreType.DMA((slots,)),
             pltpu.SemaphoreType.DMA,
         ],

time: 163 us -> 101 us (0.62)
  Pallas kernels: 82.7 us -> 19.9 us
    pallas_call x1, Pallas kernels: 65.5 us -> 2.63 us  [pack(): pl.pallas_call(pack_kernel, in_specs=[hbm, hbm, hbm], out_specs=hbm, out_...]
where the time goes in v4:
time: 101 us
  waiting for transfers between devices  65.4 us (65%)
  Pallas kernels  19.9 us (20%)
  starting transfers between devices  14.1 us (14%)
  local copies, waits for them, and re-layouts  1.25 us (1%)
    all_to_all x1, waiting for transfers between devices, local(): received = lax.all_to_all(sent, 'shots', 0, 0, tiled=True)  56.9 us
    pallas_call x1, Pallas kernels, smooth(): pl.pallas_call(smooth_kernel, in_specs=[pl.BlockSpec(memory_space=pltpu.S...  14.2 us
    all_to_all x1, starting transfers between devices, local(): received = lax.all_to_all(sent, 'shots', 0, 0, tiled=True)  8.22 us
    ppermute x1, waiting for transfers between devices, local(): lax.ppermute(image[PLANES - HALO:], 'depth', [(i, i + 1) for i in range(d...  5.36 us
    ppermute x1, starting transfers between devices, local(): lax.ppermute(image[PLANES - HALO:], 'depth', [(i, i + 1) for i in range(d...  3.4 us
    pallas_call x1, Pallas kernels, merge(): pl.pallas_call(merge_kernel, in_specs=[pl.BlockSpec(memory_space=pltpu.HB...  3.14 us
    ppermute x1, waiting for transfers between devices, local(): lax.ppermute(image[:HALO], 'depth', [(i + 1, i) for i in range(depth_coun...  3.13 us
    pallas_call x1, Pallas kernels, pack(): pl.pallas_call(pack_kernel, in_specs=[hbm, hbm, hbm], out_specs=hbm, out_...  2.63 us
  transfers between devices with their start and end apart: 3, of which 3 were waited for; matrix products, arithmetic and copies ran while one was open for 1% of the time, Pallas kernels for 0%

profile of v4, /device:TPU:34, one launch (start us, length us, event | category | flops | bytes accessed | tf_op | source)
XLA Modules:
  0.0 101.0 jit_solution(4028803509894938350)
XLA Ops:
  0.0 2.6 %pack_blocks.1 = f32[32,8,4224]{2,1,0:T(8,128)} custom-call(s32[16]{0:T(128)} %aperture_hbm.1, s32[128]{0:T(128)} %owner_map_hbm.1, f32[16,8,4096]{2,1,0:T(8,128)} %partials.1), custom_call_target="tpu_custom_call" | custom-call | tf_op jit(solution)/shard_map/pack_blocks/pallas_call | solution.py:76
  2.6 8.2 %all-to-all-start = ((f32[32,8,4224]{2,1,0:T(8,128)}), f32[32,8,4224]{2,1,0:T(8,128)}, u32[]{:S(2)}, u32[]{:S(2)}) async-start(f32[32,8,4224]{2,1,0:T(8,128)} %pack_blocks.1), calls=%async_computation | async-start | bytes 8650752 | tf_op jit(solution)/shard_map/all_to_all | solution.py:385
  10.9 56.9 %all-to-all-done.received = f32[32,8,4224]{2,1,0:T(8,128)} async-done(((f32[32,8,4224]{2,1,0:T(8,128)}), f32[32,8,4224]{2,1,0:T(8,128)}, u32[]{:S(2)}, u32[]{:S(2)}) %all-to-all-start) | async-done | bytes 4325408 | tf_op jit(solution)/shard_map/all_to_all | solution.py:385
  67.8 3.1 %merge_blocks.1 = f32[1024,128]{1,0:T(8,128)S(1)} custom-call(f32[32,8,4224]{2,1,0:T(8,128)} %all-to-all-done.received), custom_call_target="tpu_custom_call" | custom-call | tf_op jit(solution)/shard_map/merge_blocks/pallas_call | solution.py:139
  71.0 3.4 %collective-permute-start = (f32[6,16,8,128]{3,2,1,0:T(8,128)S(1)}, f32[6,16,8,128]{3,2,1,0:T(8,128)S(1)}, u32[]{:S(2)}, u32[]{:S(2)}) collective-permute-start(f32[6,16,8,128]{3,2,1,0:T(8,128)S(1)} %bitcast.61), channel_id=1, source_target_pairs={{0,1},{1,2},{2,3},{4,5},{5,6},{6,7},{8,9},{9,10},{10,11},{12,13},{... | collective-permute-start | bytes 1179656 | tf_op jit(solution)/shard_map/ppermute | solution.py:388
  74.4 2.5 %collective-permute-start.1 = (f32[6,16,8,128]{3,2,1,0:T(8,128)S(1)}, f32[6,16,8,128]{3,2,1,0:T(8,128)S(1)}, u32[]{:S(2)}, u32[]{:S(2)}) collective-permute-start(f32[6,16,8,128]{3,2,1,0:T(8,128)S(1)} %bitcast.60), channel_id=1, source_target_pairs={{1,0},{2,1},{3,2},{5,4},{6,5},{7,6},{9,8},{10,9},{11,10},{13,12},{... | collective-permute-start | bytes 1179656 | tf_op jit(solution)/shard_map/ppermute | solution.py:389
  76.9 0.2 select_reduce_fusion
  77.1 0.1 copy.27
  77.2 0.1 copy.24
  77.3 0.1 copy.23
  77.4 0.1 copy.22
  77.5 0.1 copy.25
  77.6 0.1 copy.26
  77.7 0.1 copy.21
  77.8 0.1 copy.20
  77.9 0.1 copy.19
  78.0 0.1 copy.18
  78.1 0.1 stack.11
  78.2 0.1 copy.28
  78.3 0.1 pad_add_fusion.bounds
  78.3 5.4 %collective-permute-done.lower = f32[6,16,8,128]{3,2,1,0:T(8,128)S(1)} collective-permute-done((f32[6,16,8,128]{3,2,1,0:T(8,128)S(1)}, f32[6,16,8,128]{3,2,1,0:T(8,128)S(1)}, u32[]{:S(2)}, u32[]{:S(2)}) %collective-permute-start) | collective-permute-done | bytes 393248 | tf_op jit(solution)/shard_map/ppermute | solution.py:388
  83.7 3.1 %collective-permute-done.1.upper = f32[6,16,8,128]{3,2,1,0:T(8,128)S(1)} collective-permute-done((f32[6,16,8,128]{3,2,1,0:T(8,128)S(1)}, f32[6,16,8,128]{3,2,1,0:T(8,128)S(1)}, u32[]{:S(2)}, u32[]{:S(2)}) %collective-permute-start.1) | collective-permute-done | bytes 393248 | tf_op jit(solution)/shard_map/ppermute | solution.py:389
  86.8 0.1 broadcast_in_dim.29.coefs
  86.9 14.2 %smooth_image.1 = f32[4,8,4096]{2,1,0:T(8,128)} custom-call(s32[2]{0:T(128)S(1)} %pad_add_fusion.bounds, f32[10,8,128]{2,1,0:T(8,128)S(1)} %broadcast_in_dim.29.coefs, f32[6,16,8,128]{3,2,1,0:T(8,128)S(1)} %collective-permute-done.lower, f32[8,16,8,128]{3,2,1,0:T(8,128)S(1)} %bitcast.59, f32[6,16,8,128]{3,2,1,0:T(8,128)S(1)} %collective-permute-done.1.upper), custom_call_target="tpu_custom_call" | custom-call | tf_op jit(solution)/shard_map/smooth_image/pallas_call | solution.py:342
  (8 shorter events, 0.1 us)
Async XLA Ops:
  2.6 65.1 %all-to-all-start = ((f32[32,8,4224]{2,1,0:T(8,128)}), f32[32,8,4224]{2,1,0:T(8,128)}, u32[]{:S(2)}, u32[]{:S(2)}) async-start(f32[32,8,4224]{2,1,0:T(8,128)} %pack_blocks.1), calls=%async_computation | async-start | bytes 8650752 | tf_op jit(solution)/shard_map/all_to_all | solution.py:385
  10.9 66.0 %copy-start = (s32[128]{0:T(128)S(1)}, s32[128]{0:T(128)}, u32[]{:S(2)}) copy-start(s32[128]{0:T(128)} %owner_map_hbm.1) | copy-start | bytes 1540
  10.9 66.0 %copy-start.1 = (s32[128]{0:T(128)S(1)}, s32[128]{0:T(128)}, u32[]{:S(2)}) copy-start(s32[128]{0:T(128)} %param.7) | copy-start | bytes 1540
  71.0 12.7 %collective-permute-start = (f32[6,16,8,128]{3,2,1,0:T(8,128)S(1)}, f32[6,16,8,128]{3,2,1,0:T(8,128)S(1)}, u32[]{:S(2)}, u32[]{:S(2)}) collective-permute-start(f32[6,16,8,128]{3,2,1,0:T(8,128)S(1)} %bitcast.61), channel_id=1, source_target_pairs={{0,1},{1,2},{2,3},{4,5},{5,6},{6,7},{8,9},{9,10},{10,11},{12,13},{... | collective-permute-start | bytes 1179656 | tf_op jit(solution)/shard_map/ppermute | solution.py:388
  74.4 12.4 %collective-permute-start.1 = (f32[6,16,8,128]{3,2,1,0:T(8,128)S(1)}, f32[6,16,8,128]{3,2,1,0:T(8,128)S(1)}, u32[]{:S(2)}, u32[]{:S(2)}) collective-permute-start(f32[6,16,8,128]{3,2,1,0:T(8,128)S(1)} %bitcast.60), channel_id=1, source_target_pairs={{1,0},{2,1},{3,2},{5,4},{6,5},{7,6},{9,8},{10,9},{11,10},{13,12},{... | collective-permute-start | bytes 1179656 | tf_op jit(solution)/shard_map/ppermute | solution.py:389

commit v5 on v4

--- a/solution.py
+++ b/solution.py
@@ -153,15 +153,16 @@
     )(received)
 
 
-def set_edges(field, plane, first, last):
-    left_half = lanes() < 64
-    lower_row = rows() % 2 == 0
+def left_edge(last):
     turned = pltpu.roll(last, 64, 1)
-    below = jnp.where(lower_row, 0.0, pltpu.roll(turned, 1, 0))
-    field[plane, 0] = jnp.where(left_half, below, turned)
+    below = jnp.where(rows() % 2 == 0, 0.0, pltpu.roll(turned, 1, 0))
+    return jnp.where(lanes() < 64, below, turned)
+
+
+def right_edge(first):
     turned = pltpu.roll(first, 64, 1)
-    above = jnp.where(lower_row, pltpu.roll(turned, 7, 0), 0.0)
-    field[plane, STEPS + 1] = jnp.where(left_half, turned, above)
+    above = jnp.where(rows() % 2 == 0, pltpu.roll(turned, 7, 0), 0.0)
+    return jnp.where(lanes() < 64, turned, above)
 
 
 def smooth_kernel(bounds, coefs, lower, own, upper, out, image, other, blur, slope, along, total, final):
@@ -181,19 +182,18 @@
     zero = jnp.zeros((8, 128), jnp.float32)
 
     def clear(field, plane):
-        for step in range(STEPS + 2):
+        for step in range(1, STEPS + 1):
             field[plane, step] = zero
 
     for plane in (HALO - 1, HALO + PLANES):
         clear(other, plane)
 
     def load(source, count, offset):
-        @pl.loop(0, count)
-        def _(plane):
-            cells = [source[plane, step] for step in range(STEPS)]
-            for step in range(STEPS):
-                image[plane + offset, step + 1] = cells[step]
-            set_edges(image, plane + offset, cells[0], cells[-1])
+        @pl.loop(0, count // 2)
+        def _(pair):
+            for plane in (2 * pair, 2 * pair + 1):
+                for step in range(STEPS):
+                    image[plane + offset, step + 1] = source[plane, step]
 
     load(lower, HALO, 0)
     load(own, PLANES, HALO)
@@ -202,12 +202,18 @@
     first_plane = bounds[0]
     end_plane = bounds[1]
 
-    def along_y(source, plane):
-        for step in range(STEPS + 2):
+    def along_y(source, plane, step):
+        if step == 0:
+            cells = left_edge(source[plane, STEPS])
+        elif step == STEPS + 1:
+            cells = right_edge(source[plane, 1])
+        else:
             cells = source[plane, step]
-            up, down = after(cells), before(cells)
-            blur[plane, step] = (cells + cells) + (up + down)
-            slope[plane, step] = up - down
+        if step in (0, STEPS + 1):
+            source[plane, step] = cells
+        up, down = after(cells), before(cells)
+        blur[plane, step] = (cells + cells) + (up + down)
+        slope[plane, step] = up - down
 
     def depth_blur(field, plane, step):
         deep = [field[plane - 1 + k, step] for k in range(GROUP + 2)]
@@ -225,18 +231,19 @@
         stop = jnp.minimum(DEEP - margin, end_plane + 1)
 
         for k in range(GROUP + 1):
-            along_y(source, start - 1 + k)
+            for step in range(STEPS + 2):
+                along_y(source, start - 1 + k, step)
 
         @pl.loop(0, (stop - start) // GROUP)
         def _(group):
             plane = start + group * GROUP
-            for k in range(GROUP):
-                along_y(source, plane + GROUP + k)
             norm_z, norm_x, norm_y = coefs[0], coefs[1], coefs[2]
 
             flat, steep, wide = {}, {}, {}
 
             def prepare(step):
+                for k in range(GROUP):
+                    along_y(source, plane + GROUP + k, step)
                 flat[step], deep = depth_blur(blur, plane, step)
                 steep[step] = depth_slope(deep)
                 wide[step], _ = depth_blur(slope, plane, step)
@@ -245,7 +252,6 @@
             prepare(1)
             steep_pair = [steep[0][k] + steep[1][k] for k in range(GROUP)]
             wide_pair = [wide[0][k] + wide[1][k] for k in range(GROUP)]
-            ends = {}
             for step in range(1, STEPS + 1):
                 prepare(step + 1)
                 for k in range(GROUP):
@@ -260,11 +266,6 @@
                     whole = grad_z * grad_z + grad_x * grad_x + grad_y * grad_y
                     along[plane + k, step] = aligned
                     total[plane + k, step] = whole
-                    if step in (1, STEPS):
-                        ends[step, k] = (aligned, whole)
-            for k in range(GROUP):
-                set_edges(along, plane + k, ends[1, k][0], ends[STEPS, k][0])
-                set_edges(total, plane + k, ends[1, k][1], ends[STEPS, k][1])
 
         for outside, edge in ((first_plane == HALO, HALO - 1), (end_plane == HALO + PLANES, HALO + PLANES)):
 
@@ -284,8 +285,12 @@
             a_cells, t_cells, deep, tilted = {}, {}, {}, {}
 
             def prepare(step):
-                a_cells[step], _ = depth_blur(along, plane, step)
-                t_cells[step], _ = depth_blur(total, plane, step)
+                for field, cells in ((along, a_cells), (total, t_cells)):
+                    if step == 0:
+                        cells[0] = [left_edge(f) for f in depth_blur(field, plane, STEPS)[0]]
+                        cells[STEPS + 1] = [right_edge(f) for f in depth_blur(field, plane, 1)[0]]
+                    elif step <= STEPS:
+                        cells[step], _ = depth_blur(field, plane, step)
                 deep[step] = [source[plane - 1 + k, step] for k in range(GROUP + 2)]
                 steep = depth_slope(deep[step])
                 tilted[step] = [c_zx * steep[k] + c_xy * slope[plane + k, step] for k in range(GROUP)]
@@ -294,7 +299,6 @@
             prepare(1)
             a_pair = [a_cells[0][k] + a_cells[1][k] for k in range(GROUP)]
             t_pair = [t_cells[0][k] + t_cells[1][k] for k in range(GROUP)]
-            ends = {}
             for step in range(1, STEPS + 1):
                 prepare(step + 1)
                 lean = depth_slope([slope[plane - 1 + k, step] for k in range(GROUP + 2)])
@@ -312,25 +316,20 @@
                         + ((tilted[step + 1][k] - tilted[step - 1][k]) + c_zy * lean[k])
                     )
                     new = now + weight * change
-                    if sweep == ITERS - 1:
+                    if sweep < ITERS - 1:
+                        target[plane + k, step] = new
+                    else:
                         base = pl.multiple_of((plane + k - HALO) * 128, 128) + (step - 1) * 8
                         final[pl.ds(base, 8), :] = new
-                    else:
-                        target[plane + k, step] = new
-                        if step in (1, STEPS):
-                            ends[step, k] = new
-            if sweep < ITERS - 1:
-                for k in range(GROUP):
-                    set_edges(target, plane + k, ends[1, k], ends[STEPS, k])
 
     low_half = lanes() < 64
     for b in range(4):
-        for upper_half in range(2):
+        for half in range(2):
             for k in range(8):
-                base = k * 16 + b * 2 + upper_half
+                base = k * 16 + b * 2 + half
                 first = final[pl.ds(base, 8, stride=128), :]
                 second = final[pl.ds(base + 8, 8, stride=128), :]
-                tile = upper_half * 16 + k
+                tile = half * 16 + k
                 out[b, :, tile * 128 : tile * 128 + 128] = jnp.where(low_half, first, pltpu.roll(second, 64, 1))
                 tile += 8
                 out[b, :, tile * 128 : tile * 128 + 128] = jnp.where(low_half, pltpu.roll(first, 64, 1), second)

time: 101 us -> 99.7 us (0.987)
  Pallas kernels: 19.9 us -> 18.2 us
    pallas_call x1, Pallas kernels: 14.2 us -> 12.6 us  [smooth(): pl.pallas_call(smooth_kernel, in_specs=[pl.BlockSpec(memory_space=pltpu.S...]
where the time goes in v5:
time: 99.7 us; the launch traced here: 99.3 us
  waiting for transfers between devices  65.3 us (65%)
  Pallas kernels  18.2 us (18%)
  starting transfers between devices  14.1 us (14%)
  local copies, waits for them, and re-layouts  1.25 us (1%)
    all_to_all x1, waiting for transfers between devices, local(): received = lax.all_to_all(sent, 'shots', 0, 0, tiled=True)  56.9 us
    pallas_call x1, Pallas kernels, smooth(): pl.pallas_call(smooth_kernel, in_specs=[pl.BlockSpec(memory_space=pltpu.S...  12.6 us
    all_to_all x1, starting transfers between devices, local(): received = lax.all_to_all(sent, 'shots', 0, 0, tiled=True)  8.27 us
    ppermute x1, waiting for transfers between devices, local(): lax.ppermute(image[PLANES - HALO:], 'depth', [(i, i + 1) for i in range(d...  5.31 us
    ppermute x1, starting transfers between devices, local(): lax.ppermute(image[PLANES - HALO:], 'depth', [(i, i + 1) for i in range(d...  3.4 us
    ppermute x1, waiting for transfers between devices, local(): lax.ppermute(image[:HALO], 'depth', [(i + 1, i) for i in range(depth_coun...  3.13 us
    pallas_call x1, Pallas kernels, merge(): pl.pallas_call(merge_kernel, in_specs=[pl.BlockSpec(memory_space=pltpu.HB...  3.04 us
    pallas_call x1, Pallas kernels, pack(): pl.pallas_call(pack_kernel, in_specs=[hbm, hbm, hbm], out_specs=hbm, out_...  2.58 us
  transfers between devices with their start and end apart: 3, of which 3 were waited for; matrix products, arithmetic and copies ran while one was open for 1% of the time, Pallas kernels for 0%

profile of v5, /device:TPU:34, one launch (start us, length us, event | category | flops | bytes accessed | tf_op | source)
XLA Modules:
  0.0 99.3 jit_solution(9501770409795032922)
XLA Ops:
  0.0 2.6 %pack_blocks.1 = f32[32,8,4224]{2,1,0:T(8,128)} custom-call(s32[16]{0:T(128)} %aperture_hbm.1, s32[128]{0:T(128)} %owner_map_hbm.1, f32[16,8,4096]{2,1,0:T(8,128)} %partials.1), custom_call_target="tpu_custom_call" | custom-call | tf_op jit(solution)/shard_map/pack_blocks/pallas_call | solution.py:76
  2.6 8.3 %all-to-all-start = ((f32[32,8,4224]{2,1,0:T(8,128)}), f32[32,8,4224]{2,1,0:T(8,128)}, u32[]{:S(2)}, u32[]{:S(2)}) async-start(f32[32,8,4224]{2,1,0:T(8,128)} %pack_blocks.1), calls=%async_computation | async-start | bytes 8650752 | tf_op jit(solution)/shard_map/all_to_all | solution.py:384
  10.9 56.9 %all-to-all-done.received = f32[32,8,4224]{2,1,0:T(8,128)} async-done(((f32[32,8,4224]{2,1,0:T(8,128)}), f32[32,8,4224]{2,1,0:T(8,128)}, u32[]{:S(2)}, u32[]{:S(2)}) %all-to-all-start) | async-done | bytes 4325408 | tf_op jit(solution)/shard_map/all_to_all | solution.py:384
  67.8 3.0 %merge_blocks.1 = f32[1024,128]{1,0:T(8,128)S(1)} custom-call(f32[32,8,4224]{2,1,0:T(8,128)} %all-to-all-done.received), custom_call_target="tpu_custom_call" | custom-call | tf_op jit(solution)/shard_map/merge_blocks/pallas_call | solution.py:139
  70.9 3.4 %collective-permute-start = (f32[6,16,8,128]{3,2,1,0:T(8,128)S(1)}, f32[6,16,8,128]{3,2,1,0:T(8,128)S(1)}, u32[]{:S(2)}, u32[]{:S(2)}) collective-permute-start(f32[6,16,8,128]{3,2,1,0:T(8,128)S(1)} %bitcast.61), channel_id=1, source_target_pairs={{0,1},{1,2},{2,3},{4,5},{5,6},{6,7},{8,9},{9,10},{10,11},{12,13},{... | collective-permute-start | bytes 1179656 | tf_op jit(solution)/shard_map/ppermute | solution.py:387
  74.3 2.5 %collective-permute-start.1 = (f32[6,16,8,128]{3,2,1,0:T(8,128)S(1)}, f32[6,16,8,128]{3,2,1,0:T(8,128)S(1)}, u32[]{:S(2)}, u32[]{:S(2)}) collective-permute-start(f32[6,16,8,128]{3,2,1,0:T(8,128)S(1)} %bitcast.60), channel_id=1, source_target_pairs={{1,0},{2,1},{3,2},{5,4},{6,5},{7,6},{9,8},{10,9},{11,10},{13,12},{... | collective-permute-start | bytes 1179656 | tf_op jit(solution)/shard_map/ppermute | solution.py:388
  76.8 0.2 select_reduce_fusion
  77.0 0.1 copy.27
  77.1 0.1 copy.24
  77.2 0.1 copy.23
  77.3 0.1 copy.22
  77.4 0.1 copy.25
  77.5 0.1 copy.26
  77.6 0.1 copy.21
  77.7 0.1 copy.20
  77.8 0.1 copy.19
  77.9 0.1 copy.18
  78.0 0.1 stack.11
  78.1 0.1 copy.28
  78.2 0.1 pad_add_fusion.bounds
  78.2 5.3 %collective-permute-done.lower = f32[6,16,8,128]{3,2,1,0:T(8,128)S(1)} collective-permute-done((f32[6,16,8,128]{3,2,1,0:T(8,128)S(1)}, f32[6,16,8,128]{3,2,1,0:T(8,128)S(1)}, u32[]{:S(2)}, u32[]{:S(2)}) %collective-permute-start) | collective-permute-done | bytes 393248 | tf_op jit(solution)/shard_map/ppermute | solution.py:387
  83.6 3.1 %collective-permute-done.1.upper = f32[6,16,8,128]{3,2,1,0:T(8,128)S(1)} collective-permute-done((f32[6,16,8,128]{3,2,1,0:T(8,128)S(1)}, f32[6,16,8,128]{3,2,1,0:T(8,128)S(1)}, u32[]{:S(2)}, u32[]{:S(2)}) %collective-permute-start.1) | collective-permute-done | bytes 393248 | tf_op jit(solution)/shard_map/ppermute | solution.py:388
  86.7 0.1 broadcast_in_dim.29.coefs
  86.8 12.6 %smooth_image.1 = f32[4,8,4096]{2,1,0:T(8,128)} custom-call(s32[2]{0:T(128)S(1)} %pad_add_fusion.bounds, f32[10,8,128]{2,1,0:T(8,128)S(1)} %broadcast_in_dim.29.coefs, f32[6,16,8,128]{3,2,1,0:T(8,128)S(1)} %collective-permute-done.lower, f32[8,16,8,128]{3,2,1,0:T(8,128)S(1)} %bitcast.59, f32[6,16,8,128]{3,2,1,0:T(8,128)S(1)} %collective-permute-done.1.upper), custom_call_target="tpu_custom_call" | custom-call | tf_op jit(solution)/shard_map/smooth_image/pallas_call | solution.py:341
  (8 shorter events, 0.1 us)
Async XLA Ops:
  2.6 65.2 %all-to-all-start = ((f32[32,8,4224]{2,1,0:T(8,128)}), f32[32,8,4224]{2,1,0:T(8,128)}, u32[]{:S(2)}, u32[]{:S(2)}) async-start(f32[32,8,4224]{2,1,0:T(8,128)} %pack_blocks.1), calls=%async_computation | async-start | bytes 8650752 | tf_op jit(solution)/shard_map/all_to_all | solution.py:384
  10.9 65.9 %copy-start = (s32[128]{0:T(128)S(1)}, s32[128]{0:T(128)}, u32[]{:S(2)}) copy-start(s32[128]{0:T(128)} %owner_map_hbm.1) | copy-start | bytes 1540
  10.9 65.9 %copy-start.1 = (s32[128]{0:T(128)S(1)}, s32[128]{0:T(128)}, u32[]{:S(2)}) copy-start(s32[128]{0:T(128)} %param.7) | copy-start | bytes 1540
  70.9 12.7 %collective-permute-start = (f32[6,16,8,128]{3,2,1,0:T(8,128)S(1)}, f32[6,16,8,128]{3,2,1,0:T(8,128)S(1)}, u32[]{:S(2)}, u32[]{:S(2)}) collective-permute-start(f32[6,16,8,128]{3,2,1,0:T(8,128)S(1)} %bitcast.61), channel_id=1, source_target_pairs={{0,1},{1,2},{2,3},{4,5},{5,6},{6,7},{8,9},{9,10},{10,11},{12,13},{... | collective-permute-start | bytes 1179656 | tf_op jit(solution)/shard_map/ppermute | solution.py:387
  74.3 12.4 %collective-permute-start.1 = (f32[6,16,8,128]{3,2,1,0:T(8,128)S(1)}, f32[6,16,8,128]{3,2,1,0:T(8,128)S(1)}, u32[]{:S(2)}, u32[]{:S(2)}) collective-permute-start(f32[6,16,8,128]{3,2,1,0:T(8,128)S(1)} %bitcast.60), channel_id=1, source_target_pairs={{1,0},{2,1},{3,2},{5,4},{6,5},{7,6},{9,8},{10,9},{11,10},{13,12},{... | collective-permute-start | bytes 1179656 | tf_op jit(solution)/shard_map/ppermute | solution.py:388

commit v6 on v5

--- a/solution.py
+++ b/solution.py
@@ -195,12 +195,22 @@
                 for step in range(STEPS):
                     image[plane + offset, step + 1] = source[plane, step]
 
-    load(lower, HALO, 0)
-    load(own, PLANES, HALO)
-    load(upper, HALO, HALO + PLANES)
-
     first_plane = bounds[0]
     end_plane = bounds[1]
+
+    def load_or_clear(source, offset, outside):
+        @pl.when(jnp.logical_not(outside))
+        def _():
+            load(source, HALO, offset)
+
+        @pl.when(outside)
+        def _():
+            for plane in range(HALO):
+                clear(image, plane + offset)
+
+    load_or_clear(lower, 0, first_plane == HALO)
+    load(own, PLANES, HALO)
+    load_or_clear(upper, HALO + PLANES, end_plane == HALO + PLANES)
 
     def along_y(source, plane, step):
         if step == 0:
@@ -384,8 +394,8 @@
     received = lax.all_to_all(sent, "shots", 0, 0, tiled=True)
     image = merge(received).reshape(PLANES, STEPS, 8, 128)
     depth_count = lax.axis_size("depth")
-    lower = lax.ppermute(image[PLANES - HALO :], "depth", [(i, i + 1) for i in range(depth_count - 1)])
-    upper = lax.ppermute(image[:HALO], "depth", [(i + 1, i) for i in range(depth_count - 1)])
+    lower = lax.ppermute(image[PLANES - HALO :], "depth", [(i, (i + 1) % depth_count) for i in range(depth_count)])
+    upper = lax.ppermute(image[:HALO], "depth", [((i + 1) % depth_count, i) for i in range(depth_count)])
     mine = lax.axis_index("shots") * owned + jnp.arange(owned)
     classes = jnp.sum(jnp.where(owner_map[None, :] == mine[:, None], dip_class[None, :], 0), axis=1)
     place = lax.axis_index("depth")

time: 99.7 us -> 95.9 us (0.962)
  starting transfers between devices: 14.1 us -> 10.3 us
    ppermute x2, starting transfers between devices: 5.86 us -> 2.09 us  [the longest x1 1.56 us: local(): lax.ppermute(image[PLANES - HALO:], 'depth', [(i, (i + 1) % depth_count)...]
  transfers between devices with their start and end apart: 3 -> 3, of which waited for: 3 -> 3; matrix products, arithmetic and copies ran while one was open for 1% -> 2% of each run, Pallas kernels for 0% -> 0%
where the time goes in v6:
time: 95.9 us; the launch traced here: 95.6 us
  waiting for transfers between devices  65.3 us (68%)
  Pallas kernels  18.3 us (19%)
  starting transfers between devices  10.3 us (11%)
  local copies, waits for them, and re-layouts  1.25 us (1%)
    all_to_all x1, waiting for transfers between devices, local(): received = lax.all_to_all(sent, 'shots', 0, 0, tiled=True)  56.9 us
    pallas_call x1, Pallas kernels, smooth(): pl.pallas_call(smooth_kernel, in_specs=[pl.BlockSpec(memory_space=pltpu.S...  12.6 us
    all_to_all x1, starting transfers between devices, local(): received = lax.all_to_all(sent, 'shots', 0, 0, tiled=True)  8.24 us
    ppermute x1, waiting for transfers between devices, local(): lax.ppermute(image[PLANES - HALO:], 'depth', [(i, (i + 1) % depth_count)...  7.22 us
    pallas_call x1, Pallas kernels, merge(): pl.pallas_call(merge_kernel, in_specs=[pl.BlockSpec(memory_space=pltpu.HB...  3.08 us
    pallas_call x1, Pallas kernels, pack(): pl.pallas_call(pack_kernel, in_specs=[hbm, hbm, hbm], out_specs=hbm, out_...  2.61 us
  transfers between devices with their start and end apart: 3, of which 3 were waited for; matrix products, arithmetic and copies ran while one was open for 2% of the time, Pallas kernels for 0%

profile of v6, /device:TPU:34, one launch (start us, length us, event | category | flops | bytes accessed | tf_op | source)
XLA Modules:
  0.0 95.6 jit_solution(12232831198021871573)
XLA Ops:
  0.0 2.6 %pack_blocks.1 = f32[32,8,4224]{2,1,0:T(8,128)} custom-call(s32[16]{0:T(128)} %aperture_hbm.1, s32[128]{0:T(128)} %owner_map_hbm.1, f32[16,8,4096]{2,1,0:T(8,128)} %partials.1), custom_call_target="tpu_custom_call" | custom-call | tf_op jit(solution)/shard_map/pack_blocks/pallas_call | solution.py:76
  2.6 8.2 %all-to-all-start = ((f32[32,8,4224]{2,1,0:T(8,128)}), f32[32,8,4224]{2,1,0:T(8,128)}, u32[]{:S(2)}, u32[]{:S(2)}) async-start(f32[32,8,4224]{2,1,0:T(8,128)} %pack_blocks.1), calls=%async_computation | async-start | bytes 8650752 | tf_op jit(solution)/shard_map/all_to_all | solution.py:394
  10.9 56.9 %all-to-all-done.received = f32[32,8,4224]{2,1,0:T(8,128)} async-done(((f32[32,8,4224]{2,1,0:T(8,128)}), f32[32,8,4224]{2,1,0:T(8,128)}, u32[]{:S(2)}, u32[]{:S(2)}) %all-to-all-start) | async-done | bytes 4325408 | tf_op jit(solution)/shard_map/all_to_all | solution.py:394
  67.8 3.1 %merge_blocks.1 = f32[1024,128]{1,0:T(8,128)S(1)} custom-call(f32[32,8,4224]{2,1,0:T(8,128)} %all-to-all-done.received), custom_call_target="tpu_custom_call" | custom-call | tf_op jit(solution)/shard_map/merge_blocks/pallas_call | solution.py:139
  70.9 1.6 %collective-permute-start = (f32[6,16,8,128]{3,2,1,0:T(8,128)S(1)}, f32[6,16,8,128]{3,2,1,0:T(8,128)S(1)}, u32[]{:S(2)}, u32[]{:S(2)}) collective-permute-start(f32[6,16,8,128]{3,2,1,0:T(8,128)S(1)} %bitcast.61), channel_id=1, source_target_pairs={{0,1},{1,2},{2,3},{3,0},{4,5},{5,6},{6,7},{7,4},{8,9},{9,10},{10,1... | collective-permute-start | bytes 1179656 | tf_op jit(solution)/shard_map/ppermute | solution.py:397
  72.5 0.5 collective-permute-start.1
  73.0 0.2 select_reduce_fusion
  73.3 0.1 copy.27
  73.4 0.1 copy.24
  73.5 0.1 copy.23
  73.6 0.1 copy.22
  73.7 0.1 copy.25
  73.8 0.1 copy.26
  73.8 0.1 copy.21
  73.9 0.1 copy.20
  74.0 0.1 copy.19
  74.1 0.1 copy.18
  74.2 0.1 stack.11
  74.3 0.1 copy.28
  74.4 0.1 pad_add_fusion.bounds
  74.5 7.2 %collective-permute-done.lower = f32[6,16,8,128]{3,2,1,0:T(8,128)S(1)} collective-permute-done((f32[6,16,8,128]{3,2,1,0:T(8,128)S(1)}, f32[6,16,8,128]{3,2,1,0:T(8,128)S(1)}, u32[]{:S(2)}, u32[]{:S(2)}) %collective-permute-start) | collective-permute-done | bytes 393248 | tf_op jit(solution)/shard_map/ppermute | solution.py:397
  81.7 1.2 %collective-permute-done.1.upper = f32[6,16,8,128]{3,2,1,0:T(8,128)S(1)} collective-permute-done((f32[6,16,8,128]{3,2,1,0:T(8,128)S(1)}, f32[6,16,8,128]{3,2,1,0:T(8,128)S(1)}, u32[]{:S(2)}, u32[]{:S(2)}) %collective-permute-start.1) | collective-permute-done | bytes 393248 | tf_op jit(solution)/shard_map/ppermute | solution.py:398
  82.9 0.1 broadcast_in_dim.29.coefs
  83.0 12.6 %smooth_image.1 = f32[4,8,4096]{2,1,0:T(8,128)} custom-call(s32[2]{0:T(128)S(1)} %pad_add_fusion.bounds, f32[10,8,128]{2,1,0:T(8,128)S(1)} %broadcast_in_dim.29.coefs, f32[6,16,8,128]{3,2,1,0:T(8,128)S(1)} %collective-permute-done.lower, f32[8,16,8,128]{3,2,1,0:T(8,128)S(1)} %bitcast.59, f32[6,16,8,128]{3,2,1,0:T(8,128)S(1)} %collective-permute-done.1.upper), custom_call_target="tpu_custom_call" | custom-call | tf_op jit(solution)/shard_map/smooth_image/pallas_call | solution.py:351
  (8 shorter events, 0.1 us)
Async XLA Ops:
  2.6 65.2 %all-to-all-start = ((f32[32,8,4224]{2,1,0:T(8,128)}), f32[32,8,4224]{2,1,0:T(8,128)}, u32[]{:S(2)}, u32[]{:S(2)}) async-start(f32[32,8,4224]{2,1,0:T(8,128)} %pack_blocks.1), calls=%async_computation | async-start | bytes 8650752 | tf_op jit(solution)/shard_map/all_to_all | solution.py:394
  10.9 62.2 %copy-start = (s32[128]{0:T(128)S(1)}, s32[128]{0:T(128)}, u32[]{:S(2)}) copy-start(s32[128]{0:T(128)} %owner_map_hbm.1) | copy-start | bytes 1540
  10.9 62.2 %copy-start.1 = (s32[128]{0:T(128)S(1)}, s32[128]{0:T(128)}, u32[]{:S(2)}) copy-start(s32[128]{0:T(128)} %param.7) | copy-start | bytes 1540
  70.9 10.8 %collective-permute-start = (f32[6,16,8,128]{3,2,1,0:T(8,128)S(1)}, f32[6,16,8,128]{3,2,1,0:T(8,128)S(1)}, u32[]{:S(2)}, u32[]{:S(2)}) collective-permute-start(f32[6,16,8,128]{3,2,1,0:T(8,128)S(1)} %bitcast.61), channel_id=1, source_target_pairs={{0,1},{1,2},{2,3},{3,0},{4,5},{5,6},{6,7},{7,4},{8,9},{9,10},{10,1... | collective-permute-start | bytes 1179656 | tf_op jit(solution)/shard_map/ppermute | solution.py:397
  72.5 10.4 %collective-permute-start.1 = (f32[6,16,8,128]{3,2,1,0:T(8,128)S(1)}, f32[6,16,8,128]{3,2,1,0:T(8,128)S(1)}, u32[]{:S(2)}, u32[]{:S(2)}) collective-permute-start(f32[6,16,8,128]{3,2,1,0:T(8,128)S(1)} %bitcast.60), channel_id=1, source_target_pairs={{1,0},{2,1},{3,2},{0,3},{5,4},{6,5},{7,6},{4,7},{9,8},{10,9},{11,1... | collective-permute-start | bytes 1179656 | tf_op jit(solution)/shard_map/ppermute | solution.py:398

commit v7 on v6

--- a/solution.py
+++ b/solution.py
@@ -26,14 +26,40 @@
     return lax.broadcasted_iota(jnp.int32, (8, 128), 0)
 
 
+def coefficients(classes):
+    tilt = 0.2 + 0.1 * (classes & 3).astype(jnp.float32)
+    azimuth = 0.3 + math.pi / 2.0 * (classes >> 2).astype(jnp.float32)
+    norm_z = jnp.cos(tilt)
+    norm_x = jnp.sin(tilt) * jnp.cos(azimuth)
+    norm_y = jnp.sin(tilt) * jnp.sin(azimuth)
+    c_zz = RATE * (1.0 - norm_z * norm_z)
+    c_xx = RATE * (1.0 - norm_x * norm_x)
+    c_yy = RATE * (1.0 - norm_y * norm_y)
+    cross = -0.5 * RATE
+    return [
+        norm_z,
+        norm_x,
+        norm_y,
+        -2.0 * (c_zz + c_xx + 2.0 * c_yy),
+        c_zz,
+        c_xx,
+        c_yy,
+        cross * norm_z * norm_x,
+        cross * norm_z * norm_y,
+        cross * norm_x * norm_y,
+    ]
+
+
 def pack_kernel(
-    aperture_hbm, owner_map_hbm, partials, out, aperture, owner_map, blocks, places, table_sems, in_sems, out_sems, place_sem
+    aperture_hbm, owner_map_hbm, dip_class_hbm, partials, out, coefs, aperture, owner_map, dip_class, owned,
+    blocks, places, table_sems, in_sems, out_sems, place_sem
 ):
     slots = partials.shape[0]
     columns = partials.shape[2]
     tables = [
         pltpu.make_async_copy(aperture_hbm, aperture, table_sems.at[0]),
         pltpu.make_async_copy(owner_map_hbm, owner_map, table_sems.at[1]),
+        pltpu.make_async_copy(dip_class_hbm, dip_class, table_sems.at[2]),
     ]
     for copy in tables:
         copy.start()
@@ -61,6 +87,28 @@
 
     labels = pltpu.make_async_copy(places, out.at[:, :, columns : columns + 128], place_sem)
     labels.start()
+
+    base = lax.axis_index("shots") * 4
+    for place in range(4):
+        owned[place] = 0
+
+    @pl.loop(0, owner_map.shape[0] // 8)
+    def _(group):
+        for k in range(8):
+            brick = group * 8 + k
+            place = owner_map[brick] - base
+
+            @pl.when(jnp.logical_and(place >= 0, place < 4))
+            def _():
+                owned[place] = dip_class[brick]
+
+    brick_of_row = rows() // 2
+    classes = jnp.full((8, 128), owned[3], jnp.int32)
+    for place in range(3):
+        classes = jnp.where(brick_of_row == place, owned[place], classes)
+    for i, value in enumerate(coefficients(classes)):
+        coefs[i] = value
+
     for slot in range(slots):
 
         @pl.when(aperture[slot] >= 0)
@@ -70,31 +118,37 @@
     labels.wait()
 
 
-def pack(aperture, owner_map, partials, owners):
+def pack(aperture, owner_map, dip_class, partials, owners):
     slots, planes, columns = partials.shape
     hbm = pl.BlockSpec(memory_space=pltpu.HBM)
     return pl.pallas_call(
         pack_kernel,
-        in_specs=[hbm, hbm, hbm],
-        out_specs=hbm,
-        out_shape=jax.ShapeDtypeStruct((owners, planes, columns + 128), jnp.float32),
+        in_specs=[hbm] * 4,
+        out_specs=[hbm, pl.BlockSpec(memory_space=pltpu.VMEM)],
+        out_shape=[
+            jax.ShapeDtypeStruct((owners, planes, columns + 128), jnp.float32),
+            jax.ShapeDtypeStruct((10, 8, 128), jnp.float32),
+        ],
         scratch_shapes=[
             pltpu.SMEM(aperture.shape, jnp.int32),
             pltpu.SMEM(owner_map.shape, jnp.int32),
+            pltpu.SMEM(dip_class.shape, jnp.int32),
+            pltpu.SMEM((4,), jnp.int32),
             pltpu.VMEM(partials.shape, jnp.float32),
             pltpu.VMEM((owners, planes, 128), jnp.float32),
-            pltpu.SemaphoreType.DMA((2,)),
+            pltpu.SemaphoreType.DMA((3,)),
             pltpu.SemaphoreType.DMA((slots,)),
             pltpu.SemaphoreType.DMA((slots,)),
             pltpu.SemaphoreType.DMA,
         ],
         compiler_params=pltpu.CompilerParams(vmem_limit_bytes=60 << 20),
         name="pack_blocks",
-    )(aperture, owner_map, partials)
-
-
-def merge_kernel(received, out, places, blocks, sums, place_sem, block_sems):
-    senders, planes, columns = blocks.shape
+    )(aperture, owner_map, dip_class, partials)
+
+
+def merge_kernel(received, out, places, sums, place_sem):
+    senders = received.shape[0]
+    columns = received.shape[2] - 128
     labels = pltpu.make_async_copy(received.at[:, 0:1, columns : columns + 128], places, place_sem)
     labels.start()
     for brick in range(4):
@@ -102,25 +156,14 @@
             sums[brick, tile] = jnp.zeros((8, 128), jnp.float32)
     labels.wait()
 
-    def block(sender):
-        return pltpu.make_async_copy(
-            received.at[sender, :, 0:columns], blocks.at[sender], block_sems.at[sender]
-        )
-
-    for sender in range(senders):
-
-        @pl.when(places[sender, 0, 0] >= 0.0)
-        def _():
-            block(sender).start()
-
-    for sender in range(senders):
+    @pl.loop(0, senders)
+    def _(sender):
         place = places[sender, 0, 0].astype(jnp.int32)
 
         @pl.when(place >= 0)
         def _():
-            block(sender).wait()
             for tile in range(TILES):
-                sums[place, tile] += blocks[sender, :, tile * 128 : tile * 128 + 128]
+                sums[place, tile] += received[sender, :, tile * 128 : tile * 128 + 128]
 
     low = lanes() < 64
     for b in range(4):
@@ -134,21 +177,19 @@
 
 
 def merge(received):
-    senders, planes, columns = received.shape
-    columns -= 128
+    senders = received.shape[0]
+    vmem = pl.BlockSpec(memory_space=pltpu.VMEM)
     return pl.pallas_call(
         merge_kernel,
-        in_specs=[pl.BlockSpec(memory_space=pltpu.HBM)],
-        out_specs=pl.BlockSpec(memory_space=pltpu.VMEM),
+        in_specs=[vmem],
+        out_specs=vmem,
         out_shape=jax.ShapeDtypeStruct((PLANES * STEPS * 8, 128), jnp.float32),
         scratch_shapes=[
             pltpu.SMEM((senders, 1, 128), jnp.float32),
-            pltpu.VMEM((senders, planes, columns), jnp.float32),
             pltpu.VMEM((4, TILES, 8, 128), jnp.float32),
             pltpu.SemaphoreType.DMA,
-            pltpu.SemaphoreType.DMA((senders,)),
         ],
-        compiler_params=pltpu.CompilerParams(vmem_limit_bytes=48 << 20),
+        compiler_params=pltpu.CompilerParams(vmem_limit_bytes=32 << 20),
         name="merge_blocks",
     )(received)
 
@@ -165,7 +206,7 @@
     return jnp.where(lanes() < 64, turned, above)
 
 
-def smooth_kernel(bounds, coefs, lower, own, upper, out, image, other, blur, slope, along, total, final):
+def smooth_kernel(coefs, lower, own, upper, out, image, other, blur, slope, along, total, final):
     column = lanes() % 64
     first_y = column == 0
     last_y = column == 63
@@ -195,8 +236,9 @@
                 for step in range(STEPS):
                     image[plane + offset, step + 1] = source[plane, step]
 
-    first_plane = bounds[0]
-    end_plane = bounds[1]
+    place = lax.axis_index("depth")
+    first_plane = HALO - place * PLANES
+    end_plane = HALO + (lax.axis_size("depth") - place) * PLANES
 
     def load_or_clear(source, offset, outside):
         @pl.when(jnp.logical_not(outside))
@@ -345,62 +387,29 @@
                 out[b, :, tile * 128 : tile * 128 + 128] = jnp.where(low_half, pltpu.roll(first, 64, 1), second)
 
 
-def smooth(bounds, coefs, lower, own, upper, interpret=False):
+def smooth(coefs, lower, own, upper, interpret=False):
     field = pltpu.VMEM((DEEP + GROUP, STEPS + 2, 8, 128), jnp.float32)
     vmem = pl.BlockSpec(memory_space=pltpu.VMEM)
     return pl.pallas_call(
         smooth_kernel,
-        in_specs=[pl.BlockSpec(memory_space=pltpu.SMEM), vmem, vmem, vmem, vmem],
+        in_specs=[vmem] * 4,
         out_specs=vmem,
         out_shape=jax.ShapeDtypeStruct((4, PLANES, STEPS * 256), jnp.float32),
         scratch_shapes=[field] * 6 + [pltpu.VMEM((PLANES * STEPS * 8, 128), jnp.float32)],
         compiler_params=pltpu.CompilerParams(vmem_limit_bytes=32 << 20),
         name="smooth_image",
         interpret=interpret,
-    )(bounds, coefs, lower, own, upper)
-
-
-def coefficients(classes):
-    tilt = 0.2 + 0.1 * (classes % 4).astype(jnp.float32)
-    azimuth = 0.3 + math.pi / 2.0 * (classes // 4).astype(jnp.float32)
-    norm_z = jnp.cos(tilt)
-    norm_x = jnp.sin(tilt) * jnp.cos(azimuth)
-    norm_y = jnp.sin(tilt) * jnp.sin(azimuth)
-    c_zz = RATE * (1.0 - norm_z * norm_z)
-    c_xx = RATE * (1.0 - norm_x * norm_x)
-    c_yy = RATE * (1.0 - norm_y * norm_y)
-    cross = -0.5 * RATE
-    values = jnp.stack(
-        [
-            norm_z,
-            norm_x,
-            norm_y,
-            -2.0 * (c_zz + c_xx + 2.0 * c_yy),
-            c_zz,
-            c_xx,
-            c_yy,
-            cross * norm_z * norm_x,
-            cross * norm_z * norm_y,
-            cross * norm_x * norm_y,
-        ]
-    )
-    return jnp.broadcast_to(jnp.repeat(values, 2, axis=1)[:, :, None], (10, 8, 128))
+    )(coefs, lower, own, upper)
 
 
 def local(partials, aperture, owner_map, dip_class):
-    senders = lax.axis_size("shots")
-    owned = owner_map.shape[0] // senders
-    sent = pack(aperture, owner_map, partials, senders)
+    sent, coefs = pack(aperture, owner_map, dip_class, partials, lax.axis_size("shots"))
     received = lax.all_to_all(sent, "shots", 0, 0, tiled=True)
     image = merge(received).reshape(PLANES, STEPS, 8, 128)
     depth_count = lax.axis_size("depth")
     lower = lax.ppermute(image[PLANES - HALO :], "depth", [(i, (i + 1) % depth_count) for i in range(depth_count)])
     upper = lax.ppermute(image[:HALO], "depth", [((i + 1) % depth_count, i) for i in range(depth_count)])
-    mine = lax.axis_index("shots") * owned + jnp.arange(owned)
-    classes = jnp.sum(jnp.where(owner_map[None, :] == mine[:, None], dip_class[None, :], 0), axis=1)
-    place = lax.axis_index("depth")
-    bounds = jnp.stack([HALO - place * PLANES, HALO + (depth_count - place) * PLANES]).astype(jnp.int32)
-    return smooth(bounds, coefficients(classes), lower, image, upper)
+    return smooth(coefs, lower, image, upper)
 
 
 def solution(mesh):

time: 95.9 us -> 91.1 us (0.950); the launches traced: 95.6 us -> 89.5 us
  blocking collectives: 0 us -> 59.8 us
  waiting for transfers between devices: 65.3 us -> 10.4 us
  starting transfers between devices: 10.3 us -> 2.09 us
  local copies, waits for them, and re-layouts: 1.25 us -> 0.06 us
  Pallas kernels: 18.3 us -> 17.2 us
    all_to_all x0 -> x1, blocking collectives: none -> 59.8 us  [local(): received = lax.all_to_all(sent, 'shots', 0, 0, tiled=True)]
    all_to_all x1 -> x0, waiting for transfers between devices: 56.9 us -> none  [local(): received = lax.all_to_all(sent, 'shots', 0, 0, tiled=True)]
    all_to_all x1 -> x0, starting transfers between devices: 8.24 us -> none  [local(): received = lax.all_to_all(sent, 'shots', 0, 0, tiled=True)]
    ppermute x1, waiting for transfers between devices: 7.22 us -> 9.16 us  [local(): lax.ppermute(image[PLANES - HALO:], 'depth', [(i, (i + 1) % depth_count)...]
    pallas_call x3, Pallas kernels: 18.3 us -> 17.2 us  [the longest x1 12.2 us: smooth(): pl.pallas_call(smooth_kernel, in_specs=[vmem] * 4, out_specs=vmem, out_sh...]
  transfers between devices with their start and end apart: 3 -> 2, of which waited for: 3 -> 2; matrix products, arithmetic and copies ran while one was open for 2% -> 0% of each run, Pallas kernels for 0% -> 0%
where the time goes in v7:
time: 91.1 us; the launch traced here: 89.5 us
  blocking collectives  59.8 us (66%)
  Pallas kernels  17.2 us (19%)
  waiting for transfers between devices  10.4 us (11%)
  starting transfers between devices  2.09 us (2%)
    all_to_all x1, blocking collectives, local(): received = lax.all_to_all(sent, 'shots', 0, 0, tiled=True)  59.8 us
    pallas_call x1, Pallas kernels, smooth(): pl.pallas_call(smooth_kernel, in_specs=[vmem] * 4, out_specs=vmem, out_sh...  12.2 us
    ppermute x1, waiting for transfers between devices, local(): lax.ppermute(image[PLANES - HALO:], 'depth', [(i, (i + 1) % depth_count)...  9.16 us
    pallas_call x1, Pallas kernels, pack(): pl.pallas_call(pack_kernel, in_specs=[hbm] * 4, out_specs=[hbm, pl.BlockS...  3.18 us
    pallas_call x1, Pallas kernels, merge(): pl.pallas_call(merge_kernel, in_specs=[vmem], out_specs=vmem, out_shape=j...  1.87 us
  transfers between devices with their start and end apart: 2, of which 2 were waited for; matrix products, arithmetic and copies ran while one was open for 0% of the time, Pallas kernels for 0%

profile of v7, /device:TPU:34, one launch (start us, length us, event | category | flops | bytes accessed | tf_op | source)
XLA Modules:
  0.0 89.5 jit_solution(7491967995104674788)
XLA Ops:
  0.0 3.2 %pack_blocks.1 = (f32[32,8,4224]{2,1,0:T(8,128)}, f32[10,8,128]{2,1,0:T(8,128)}) custom-call(s32[16]{0:T(128)} %aperture_hbm.1, s32[128]{0:T(128)} %owner_map_hbm.1, s32[128]{0:T(128)} %dip_class_hbm.1, f32[16,8,4096]{2,1,0:T(8,128)} %partials.1), custom_call_target="tpu_custom_call" | custom-call | tf_op jit(solution)/shard_map/pack_blocks/pallas_call | solution.py:124
  3.2 59.8 %all_to_all.5.received = f32[32,8,4224]{2,1,0:T(8,128)S(1)} all-to-all(f32[32,8,4224]{2,1,0:T(8,128)} %get-tuple-element.8), channel_id=1, replica_groups=mesh['shots'=32,'depth'=4] {'shots'}, dimensions={0} | all-to-all | bytes 8650752 | tf_op jit(solution)/shard_map/all_to_all | solution.py:407
  63.0 0.0 copy-start
  63.0 1.9 %merge_blocks.1 = f32[1024,128]{1,0:T(8,128)S(1)} custom-call(f32[32,8,4224]{2,1,0:T(8,128)S(1)} %all_to_all.5.received), custom_call_target="tpu_custom_call" | custom-call | tf_op jit(solution)/shard_map/merge_blocks/pallas_call | solution.py:182
  64.8 0.1 fusion
  64.9 1.6 %collective-permute-start = (f32[6,16,8,128]{3,2,1,0:T(8,128)S(1)}, f32[6,16,8,128]{3,2,1,0:T(8,128)S(1)}, u32[]{:S(2)}, u32[]{:S(2)}) collective-permute-start(f32[6,16,8,128]{3,2,1,0:T(8,128)S(1)} %bitcast.5), channel_id=1, source_target_pairs={{0,1},{1,2},{2,3},{3,0},{4,5},{5,6},{6,7},{7,4},{8,9},{9,10},{10,1... | collective-permute-start | bytes 1179656 | tf_op jit(solution)/shard_map/ppermute | solution.py:410
  66.5 0.5 collective-permute-start.1
  67.0 9.2 %collective-permute-done.lower = f32[6,16,8,128]{3,2,1,0:T(8,128)S(1)} collective-permute-done((f32[6,16,8,128]{3,2,1,0:T(8,128)S(1)}, f32[6,16,8,128]{3,2,1,0:T(8,128)S(1)}, u32[]{:S(2)}, u32[]{:S(2)}) %collective-permute-start) | collective-permute-done | bytes 393248 | tf_op jit(solution)/shard_map/ppermute | solution.py:410
  76.2 1.2 %collective-permute-done.1.upper = f32[6,16,8,128]{3,2,1,0:T(8,128)S(1)} collective-permute-done((f32[6,16,8,128]{3,2,1,0:T(8,128)S(1)}, f32[6,16,8,128]{3,2,1,0:T(8,128)S(1)}, u32[]{:S(2)}, u32[]{:S(2)}) %collective-permute-start.1) | collective-permute-done | bytes 393248 | tf_op jit(solution)/shard_map/ppermute | solution.py:411
  77.4 0.0 copy-done
  77.4 12.2 %smooth_image.1 = f32[4,8,4096]{2,1,0:T(8,128)} custom-call(f32[10,8,128]{2,1,0:T(8,128)S(1)} %copy-done, f32[6,16,8,128]{3,2,1,0:T(8,128)S(1)} %collective-permute-done.lower, f32[8,16,8,128]{3,2,1,0:T(8,128)S(1)} %bitcast.3, f32[6,16,8,128]{3,2,1,0:T(8,128)S(1)} %collective-permute-done.1.upper), custom_call_target="tpu_custom_call" | custom-call | tf_op jit(solution)/shard_map/smooth_image/pallas_call | solution.py:393
Async XLA Ops:
  63.0 14.4 %copy-start = (f32[10,8,128]{2,1,0:T(8,128)S(1)}, f32[10,8,128]{2,1,0:T(8,128)}, u32[]{:S(2)}) copy-start(f32[10,8,128]{2,1,0:T(8,128)} %get-tuple-element.7.coefs) | copy-start | bytes 122884
  64.9 11.3 %collective-permute-start = (f32[6,16,8,128]{3,2,1,0:T(8,128)S(1)}, f32[6,16,8,128]{3,2,1,0:T(8,128)S(1)}, u32[]{:S(2)}, u32[]{:S(2)}) collective-permute-start(f32[6,16,8,128]{3,2,1,0:T(8,128)S(1)} %bitcast.5), channel_id=1, source_target_pairs={{0,1},{1,2},{2,3},{3,0},{4,5},{5,6},{6,7},{7,4},{8,9},{9,10},{10,1... | collective-permute-start | bytes 1179656 | tf_op jit(solution)/shard_map/ppermute | solution.py:410
  66.5 10.9 %collective-permute-start.1 = (f32[6,16,8,128]{3,2,1,0:T(8,128)S(1)}, f32[6,16,8,128]{3,2,1,0:T(8,128)S(1)}, u32[]{:S(2)}, u32[]{:S(2)}) collective-permute-start(f32[6,16,8,128]{3,2,1,0:T(8,128)S(1)} %bitcast.4), channel_id=1, source_target_pairs={{1,0},{2,1},{3,2},{0,3},{5,4},{6,5},{7,6},{4,7},{9,8},{10,9},{11,1... | collective-permute-start | bytes 1179656 | tf_op jit(solution)/shard_map/ppermute | solution.py:411

commit v8 on v7

--- a/solution.py
+++ b/solution.py
@@ -16,6 +16,8 @@
 TINY = 1e-6
 TILES = 32
 GROUP = 2
+NEAR = 2
+KEPT = (HALO - 1, HALO, HALO + PLANES - 1, HALO + PLANES)
 
 
 def lanes():
@@ -206,7 +208,36 @@
     return jnp.where(lanes() < 64, turned, above)
 
 
-def smooth_kernel(coefs, lower, own, upper, out, image, other, blur, slope, along, total, final):
+def depth_range():
+    place = lax.axis_index("depth")
+    return HALO - place * PLANES, HALO + (lax.axis_size("depth") - place) * PLANES
+
+
+def clear(field, plane):
+    for step in range(1, STEPS + 1):
+        field[plane, step] = jnp.zeros((8, 128), jnp.float32)
+
+
+def load(field, offset, source, first, count):
+    @pl.loop(0, count // 2)
+    def _(pair):
+        for plane in (2 * pair, 2 * pair + 1):
+            for step in range(STEPS):
+                field[plane + offset, step + 1] = source[plane + first, step]
+
+
+def load_or_clear(outside, field, offset, source):
+    @pl.when(jnp.logical_not(outside))
+    def _():
+        load(field, offset, source, 0, source.shape[0])
+
+    @pl.when(outside)
+    def _():
+        for plane in range(source.shape[0]):
+            clear(field, plane + offset)
+
+
+def sweep_parts(coefs, blur, slope, along, total):
     column = lanes() % 64
     first_y = column == 0
     last_y = column == 63
@@ -219,40 +250,6 @@
 
     def blur_y(f):
         return (f + after(f)) + (f + before(f))
-
-    zero = jnp.zeros((8, 128), jnp.float32)
-
-    def clear(field, plane):
-        for step in range(1, STEPS + 1):
-            field[plane, step] = zero
-
-    for plane in (HALO - 1, HALO + PLANES):
-        clear(other, plane)
-
-    def load(source, count, offset):
-        @pl.loop(0, count // 2)
-        def _(pair):
-            for plane in (2 * pair, 2 * pair + 1):
-                for step in range(STEPS):
-                    image[plane + offset, step + 1] = source[plane, step]
-
-    place = lax.axis_index("depth")
-    first_plane = HALO - place * PLANES
-    end_plane = HALO + (lax.axis_size("depth") - place) * PLANES
-
-    def load_or_clear(source, offset, outside):
-        @pl.when(jnp.logical_not(outside))
-        def _():
-            load(source, HALO, offset)
-
-        @pl.when(outside)
-        def _():
-            for plane in range(HALO):
-                clear(image, plane + offset)
-
-    load_or_clear(lower, 0, first_plane == HALO)
-    load(own, PLANES, HALO)
-    load_or_clear(upper, HALO + PLANES, end_plane == HALO + PLANES)
 
     def along_y(source, plane, step):
         if step == 0:
@@ -275,16 +272,13 @@
     def depth_slope(deep):
         return [deep[k + 2] - deep[k] for k in range(GROUP)]
 
-    for sweep in range(ITERS):
-        source = image if sweep % 2 == 0 else other
-        target = other if sweep % 2 == 0 else image
-        margin = 2 * sweep + 1
-        start = jnp.maximum(margin, first_plane - 1)
-        stop = jnp.minimum(DEEP - margin, end_plane + 1)
-
+    def y_pass(source, plane):
+        for step in range(STEPS + 2):
+            along_y(source, plane, step)
+
+    def products(source, start, stop):
         for k in range(GROUP + 1):
-            for step in range(STEPS + 2):
-                along_y(source, start - 1 + k, step)
+            y_pass(source, start - 1 + k)
 
         @pl.loop(0, (stop - start) // GROUP)
         def _(group):
@@ -319,17 +313,7 @@
                     along[plane + k, step] = aligned
                     total[plane + k, step] = whole
 
-        for outside, edge in ((first_plane == HALO, HALO - 1), (end_plane == HALO + PLANES, HALO + PLANES)):
-
-            @pl.when(outside)
-            def _():
-                clear(along, edge)
-                clear(total, edge)
-
-        margin += 1
-        begin = jnp.maximum(margin, first_plane)
-        finish = jnp.minimum(DEEP - margin, end_plane)
-
+    def update(source, begin, finish, store):
         @pl.loop(0, (finish - begin) // GROUP)
         def _(group):
             plane = begin + group * GROUP
@@ -368,11 +352,98 @@
                         + ((tilted[step + 1][k] - tilted[step - 1][k]) + c_zy * lean[k])
                     )
                     new = now + weight * change
-                    if sweep < ITERS - 1:
-                        target[plane + k, step] = new
-                    else:
-                        base = pl.multiple_of((plane + k - HALO) * 128, 128) + (step - 1) * 8
-                        final[pl.ds(base, 8), :] = new
+                    store(plane + k, step, new)
+
+    return y_pass, products, update
+
+
+def first_kernel(coefs, lower, own, upper, out, tensors, image, blur, slope, along, total):
+    first_plane, end_plane = depth_range()
+    low_end, high_end = first_plane == HALO, end_plane == HALO + PLANES
+    _, products, update = sweep_parts(coefs, blur, slope, along, total)
+    load_or_clear(low_end, image, HALO - NEAR, lower)
+    load(image, HALO, own, 0, PLANES)
+    load_or_clear(high_end, image, HALO + PLANES, upper)
+    products(image, HALO - 1, HALO + PLANES + 1)
+    clear_outside(low_end, high_end, along, total)
+
+    def store(plane, step, new):
+        out[plane - HALO, step - 1] = new
+
+    update(image, HALO, HALO + PLANES, store)
+    for which, field in enumerate((along, total)):
+        for k, plane in enumerate(KEPT):
+            for step in range(STEPS):
+                tensors[which, k, step] = field[plane, step + 1]
+
+
+def clear_outside(low_end, high_end, along, total):
+    for outside, edge in ((low_end, HALO - 1), (high_end, HALO + PLANES)):
+
+        @pl.when(outside)
+        def _():
+            clear(along, edge)
+            clear(total, edge)
+
+
+def rest_kernel(
+    coefs, far_lower, near_lower, own, near_upper, far_upper, swept, tensors, out, image, other, blur, slope, along, total, final
+):
+    first_plane, end_plane = depth_range()
+    low_end, high_end = first_plane == HALO, end_plane == HALO + PLANES
+    y_pass, products, update = sweep_parts(coefs, blur, slope, along, total)
+    load(other, HALO, swept, 0, PLANES)
+    clear(other, HALO - 1)
+    clear(other, HALO + PLANES)
+    for which, field in enumerate((along, total)):
+        for k, plane in enumerate(KEPT):
+            for step in range(STEPS):
+                field[plane, step + 1] = tensors[which, k, step]
+
+    def keep(plane, step, new):
+        other[plane, step] = new
+
+    @pl.when(jnp.logical_not(low_end))
+    def _():
+        load(image, 0, far_lower, 0, HALO - NEAR)
+        load(image, HALO - NEAR, near_lower, 0, NEAR)
+        load(image, HALO, own, 0, NEAR)
+        products(image, 1, HALO - 1)
+        update(image, 2, HALO, keep)
+
+    @pl.when(jnp.logical_not(high_end))
+    def _():
+        top = HALO + PLANES
+        load(image, top - NEAR, own, PLANES - NEAR, NEAR)
+        load(image, top, near_upper, 0, NEAR)
+        load(image, top + NEAR, far_upper, 0, HALO - NEAR)
+        y_pass(image, top - 1)
+        products(image, top + 1, DEEP - 1)
+        update(image, top, DEEP - 2, keep)
+
+    @pl.when(low_end)
+    def _():
+        clear(image, HALO - 1)
+
+    @pl.when(high_end)
+    def _():
+        clear(image, HALO + PLANES)
+
+    for sweep in range(1, ITERS):
+        source, target = (other, image) if sweep % 2 == 1 else (image, other)
+        margin = 2 * sweep + 1
+        products(source, jnp.maximum(margin, first_plane - 1), jnp.minimum(DEEP - margin, end_plane + 1))
+        clear_outside(low_end, high_end, along, total)
+
+        def store(plane, step, new):
+            if sweep < ITERS - 1:
+                target[plane, step] = new
+            else:
+                base = pl.multiple_of((plane - HALO) * 128, 128) + (step - 1) * 8
+                final[pl.ds(base, 8), :] = new
+
+        margin += 1
+        update(source, jnp.maximum(margin, first_plane), jnp.minimum(DEEP - margin, end_plane), store)
 
     low_half = lanes() < 64
     for b in range(4):
@@ -387,29 +458,51 @@
                 out[b, :, tile * 128 : tile * 128 + 128] = jnp.where(low_half, pltpu.roll(first, 64, 1), second)
 
 
-def smooth(coefs, lower, own, upper, interpret=False):
+def smooth(coefs, image, depth_ring, interpret=False):
     field = pltpu.VMEM((DEEP + GROUP, STEPS + 2, 8, 128), jnp.float32)
     vmem = pl.BlockSpec(memory_space=pltpu.VMEM)
+    near_lower = depth_ring(image[PLANES - NEAR :], 1)
+    near_upper = depth_ring(image[:NEAR], -1)
+    middle = image[NEAR : PLANES - NEAR]
+    far_lower = depth_ring(middle, 1)
+    far_upper = depth_ring(middle, -1)
+    params = pltpu.CompilerParams(vmem_limit_bytes=32 << 20)
+    swept, tensors = pl.pallas_call(
+        first_kernel,
+        in_specs=[vmem] * 4,
+        out_specs=[vmem] * 2,
+        out_shape=[
+            jax.ShapeDtypeStruct((PLANES, STEPS, 8, 128), jnp.float32),
+            jax.ShapeDtypeStruct((2, len(KEPT), STEPS, 8, 128), jnp.float32),
+        ],
+        scratch_shapes=[field] * 5,
+        compiler_params=params,
+        cost_estimate=pl.CostEstimate(flops=20_000_000, bytes_accessed=12_000_000, transcendentals=0),
+        name="smooth_own",
+        interpret=interpret,
+    )(coefs, near_lower, image, near_upper)
     return pl.pallas_call(
-        smooth_kernel,
-        in_specs=[vmem] * 4,
+        rest_kernel,
+        in_specs=[vmem] * 8,
         out_specs=vmem,
         out_shape=jax.ShapeDtypeStruct((4, PLANES, STEPS * 256), jnp.float32),
         scratch_shapes=[field] * 6 + [pltpu.VMEM((PLANES * STEPS * 8, 128), jnp.float32)],
-        compiler_params=pltpu.CompilerParams(vmem_limit_bytes=32 << 20),
+        compiler_params=params,
         name="smooth_image",
         interpret=interpret,
-    )(coefs, lower, own, upper)
+    )(coefs, far_lower, near_lower, image, near_upper, far_upper, swept, tensors)
 
 
 def local(partials, aperture, owner_map, dip_class):
     sent, coefs = pack(aperture, owner_map, dip_class, partials, lax.axis_size("shots"))
     received = lax.all_to_all(sent, "shots", 0, 0, tiled=True)
     image = merge(received).reshape(PLANES, STEPS, 8, 128)
-    depth_count = lax.axis_size("depth")
-    lower = lax.ppermute(image[PLANES - HALO :], "depth", [(i, (i + 1) % depth_count) for i in range(depth_count)])
-    upper = lax.ppermute(image[:HALO], "depth", [((i + 1) % depth_count, i) for i in range(depth_count)])
-    return smooth(coefs, lower, image, upper)
+    count = lax.axis_size("depth")
+
+    def depth_ring(planes, way):
+        return lax.ppermute(planes, "depth", [(i, (i + way) % count) for i in range(count)])
+
+    return smooth(coefs, image, depth_ring)
 
 
 def solution(mesh):

time: 91.1 us -> 91.7 us (level)
  the two profiles are of different devices: /device:TPU:34 before, /device:TPU:0 now
where the time goes in v8:
time: 91.7 us; the launch traced here: 91.4 us
  blocking collectives  61.2 us (67%)
  Pallas kernels  15.1 us (16%)
  waiting for transfers between devices  8.72 us (10%)
  starting transfers between devices  6.21 us (7%)
    all_to_all x1, blocking collectives, local(): received = lax.all_to_all(sent, 'shots', 0, 0, tiled=True)  61.2 us
    ppermute x4, waiting for transfers between devices, depth_ring(): lax.ppermute(planes, 'depth', [(i, (i + way) % count) for i in range(coun...  8.72 us
    pallas_call x1, Pallas kernels, smooth(): pl.pallas_call(rest_kernel, in_specs=[vmem] * 8, out_specs=vmem, out_shap...  8.11 us
    ppermute x4, starting transfers between devices, depth_ring(): lax.ppermute(planes, 'depth', [(i, (i + way) % count) for i in range(coun...  6.21 us
    pallas_call x1, Pallas kernels, pack(): pl.pallas_call(pack_kernel, in_specs=[hbm] * 4, out_specs=[hbm, pl.BlockS...  3.2 us
    pallas_call x1, Pallas kernels, smooth(): pl.pallas_call(first_kernel, in_specs=[vmem] * 4, out_specs=[vmem] * 2, o...  2.03 us
  transfers between devices with their start and end apart: 4, of which 1 were waited for; matrix products, arithmetic and copies ran while one was open for 0% of the time, Pallas kernels for 2%

profile of v8, /device:TPU:0, one launch (start us, length us, event | category | flops | bytes accessed | tf_op | source)
XLA Modules:
  0.0 91.4 jit_solution(5167734617650291114)
XLA Ops:
  0.0 3.2 %pack_blocks.1 = (f32[32,8,4224]{2,1,0:T(8,128)}, f32[10,8,128]{2,1,0:T(8,128)}) custom-call(s32[16]{0:T(128)} %aperture_hbm.1, s32[128]{0:T(128)} %owner_map_hbm.1, s32[128]{0:T(128)} %dip_class_hbm.1, f32[16,8,4096]{2,1,0:T(8,128)} %partials.1), custom_call_target="tpu_custom_call" | custom-call | tf_op jit(solution)/shard_map/pack_blocks/pallas_call | solution.py:126
  3.2 61.2 %all_to_all.5.received = f32[32,8,4224]{2,1,0:T(8,128)S(1)} all-to-all(f32[32,8,4224]{2,1,0:T(8,128)} %get-tuple-element.10), channel_id=1, replica_groups=mesh['shots'=32,'depth'=4] {'shots'}, dimensions={0} | all-to-all | bytes 8650752 | tf_op jit(solution)/shard_map/all_to_all | solution.py:498
  64.4 0.0 copy-start
  64.4 1.8 %merge_blocks.1 = f32[1024,128]{1,0:T(8,128)S(1)} custom-call(f32[32,8,4224]{2,1,0:T(8,128)S(1)} %all_to_all.5.received), custom_call_target="tpu_custom_call" | custom-call | tf_op jit(solution)/shard_map/merge_blocks/pallas_call | solution.py:184
  66.3 2.8 %collective-permute-start.3 = (f32[4,16,8,128]{3,2,1,0:T(8,128)S(1)}, f32[4,16,8,128]{3,2,1,0:T(8,128)S(1)}, u32[]{:S(2)}, u32[]{:S(2)}) collective-permute-start(f32[4,16,8,128]{3,2,1,0:T(8,128)S(1)} %bitcast.6), channel_id=1, source_target_pairs={{0,3},{1,0},{2,1},{3,2},{4,7},{5,4},{6,5},{7,6},{8,11},{9,8},{10,9... | collective-permute-start | bytes 786440 | tf_op jit(solution)/shard_map/ppermute | solution.py:503
  69.1 0.0 collective-permute-start
  69.1 0.8 collective-permute-start.1
  70.0 2.6 %collective-permute-start.2 = (f32[2,16,8,128]{3,2,1,0:T(8,128)S(1)}, f32[2,16,8,128]{3,2,1,0:T(8,128)S(1)}, u32[]{:S(2)}, u32[]{:S(2)}) collective-permute-start(f32[2,16,8,128]{3,2,1,0:T(8,128)S(1)} %bitcast.8), channel_id=1, source_target_pairs={{0,3},{1,0},{2,1},{3,2},{4,7},{5,4},{6,5},{7,6},{8,11},{9,8},{10,9... | collective-permute-start | bytes 393224 | tf_op jit(solution)/shard_map/ppermute | solution.py:503
  72.5 8.7 %collective-permute-done.1.lower.near_lower = f32[2,16,8,128]{3,2,1,0:T(8,128)S(1)} collective-permute-done((f32[2,16,8,128]{3,2,1,0:T(8,128)S(1)}, f32[2,16,8,128]{3,2,1,0:T(8,128)S(1)}, u32[]{:S(2)}, u32[]{:S(2)}) %collective-permute-start.1) | collective-permute-done | bytes 131104 | tf_op jit(solution)/shard_map/ppermute | solution.py:503
  81.2 0.0 collective-permute-done.2.upper.near_upper
  81.2 0.0 copy-done
  81.2 2.0 %smooth_own.1 = (f32[8,16,8,128]{3,2,1,0:T(8,128)S(1)}, f32[2,4,16,8,128]{4,3,2,1,0:T(8,128)S(1)}) custom-call(f32[10,8,128]{2,1,0:T(8,128)S(1)} %copy-done, f32[2,16,8,128]{3,2,1,0:T(8,128)S(1)} %collective-permute-done.1.lower.near_lower, f32[8,16,8,128]{3,2,1,0:T(8,128)S(1)} %bitcast.4, f32[2,16,8,128]{3,2,1,0:T(8,128)S(1)} %collective-permute-done.2.upper.near_upper), custom_call_target="tpu_custom_call" | custom-call | flops 20000000 | bytes 12000000 | tf_op jit(solution)/shard_map/smooth_own/pallas_call | solution.py:470
  83.3 0.0 collective-permute-done.3.far_upper
  83.3 0.0 collective-permute-done.far_lower
  83.3 8.1 %smooth_image.1 = f32[4,8,4096]{2,1,0:T(8,128)} custom-call(f32[10,8,128]{2,1,0:T(8,128)S(1)} %copy-done, f32[4,16,8,128]{3,2,1,0:T(8,128)S(1)} %collective-permute-done.far_lower, f32[2,16,8,128]{3,2,1,0:T(8,128)S(1)} %collective-permute-done.1.lower.near_lower, f32[8,16,8,128]{3,2,1,0:T(8,128)S(1)} %bitcast.5, ...), custom_call_target="tpu_custom_call" | custom-call | tf_op jit(solution)/shard_map/smooth_image/pallas_call | solution.py:484
  (2 shorter events, 0.0 us)
Async XLA Ops:
  64.4 16.8 %copy-start = (f32[10,8,128]{2,1,0:T(8,128)S(1)}, f32[10,8,128]{2,1,0:T(8,128)}, u32[]{:S(2)}) copy-start(f32[10,8,128]{2,1,0:T(8,128)} %get-tuple-element.9.coefs) | copy-start | bytes 122884
  66.3 17.0 %collective-permute-start.3 = (f32[4,16,8,128]{3,2,1,0:T(8,128)S(1)}, f32[4,16,8,128]{3,2,1,0:T(8,128)S(1)}, u32[]{:S(2)}, u32[]{:S(2)}) collective-permute-start(f32[4,16,8,128]{3,2,1,0:T(8,128)S(1)} %bitcast.6), channel_id=1, source_target_pairs={{0,3},{1,0},{2,1},{3,2},{4,7},{5,4},{6,5},{7,6},{8,11},{9,8},{10,9... | collective-permute-start | bytes 786440 | tf_op jit(solution)/shard_map/ppermute | solution.py:503
  69.1 14.2 %collective-permute-start = (f32[4,16,8,128]{3,2,1,0:T(8,128)S(1)}, f32[4,16,8,128]{3,2,1,0:T(8,128)S(1)}, u32[]{:S(2)}, u32[]{:S(2)}) collective-permute-start(f32[4,16,8,128]{3,2,1,0:T(8,128)S(1)} %bitcast.7), channel_id=1, source_target_pairs={{0,1},{1,2},{2,3},{3,0},{4,5},{5,6},{6,7},{7,4},{8,9},{9,10},{10,1... | collective-permute-start | bytes 786440 | tf_op jit(solution)/shard_map/ppermute | solution.py:503
  69.1 12.1 %collective-permute-start.1 = (f32[2,16,8,128]{3,2,1,0:T(8,128)S(1)}, f32[2,16,8,128]{3,2,1,0:T(8,128)S(1)}, u32[]{:S(2)}, u32[]{:S(2)}) collective-permute-start(f32[2,16,8,128]{3,2,1,0:T(8,128)S(1)} %bitcast.9), channel_id=1, source_target_pairs={{0,1},{1,2},{2,3},{3,0},{4,5},{5,6},{6,7},{7,4},{8,9},{9,10},{10,1... | collective-permute-start | bytes 393224 | tf_op jit(solution)/shard_map/ppermute | solution.py:503
  70.0 11.3 %collective-permute-start.2 = (f32[2,16,8,128]{3,2,1,0:T(8,128)S(1)}, f32[2,16,8,128]{3,2,1,0:T(8,128)S(1)}, u32[]{:S(2)}, u32[]{:S(2)}) collective-permute-start(f32[2,16,8,128]{3,2,1,0:T(8,128)S(1)} %bitcast.8), channel_id=1, source_target_pairs={{0,3},{1,0},{2,1},{3,2},{4,7},{5,4},{6,5},{7,6},{8,11},{9,8},{10,9... | collective-permute-start | bytes 393224 | tf_op jit(solution)/shard_map/ppermute | solution.py:503

commit v9 on v7

--- a/solution.py
+++ b/solution.py
@@ -97,10 +97,7 @@
         for k in range(8):
             brick = group * 8 + k
             place = owner_map[brick] - base
-
-            @pl.when(jnp.logical_and(place >= 0, place < 4))
-            def _():
-                owned[place] = dip_class[brick]
+            owned[jnp.where(jnp.logical_and(place >= 0, place < 4), place, 4)] = dip_class[brick]
 
     brick_of_row = rows() // 2
     classes = jnp.full((8, 128), owned[3], jnp.int32)
@@ -133,7 +130,7 @@
             pltpu.SMEM(aperture.shape, jnp.int32),
             pltpu.SMEM(owner_map.shape, jnp.int32),
             pltpu.SMEM(dip_class.shape, jnp.int32),
-            pltpu.SMEM((4,), jnp.int32),
+            pltpu.SMEM((8,), jnp.int32),
             pltpu.VMEM(partials.shape, jnp.float32),
             pltpu.VMEM((owners, planes, 128), jnp.float32),
             pltpu.SemaphoreType.DMA((3,)),
@@ -151,9 +148,12 @@
     columns = received.shape[2] - 128
     labels = pltpu.make_async_copy(received.at[:, 0:1, columns : columns + 128], places, place_sem)
     labels.start()
-    for brick in range(4):
+
+    @pl.loop(0, 4)
+    def _(brick):
         for tile in range(TILES):
             sums[brick, tile] = jnp.zeros((8, 128), jnp.float32)
+
     labels.wait()
 
     @pl.loop(0, senders)
@@ -166,7 +166,9 @@
                 sums[place, tile] += received[sender, :, tile * 128 : tile * 128 + 128]
 
     low = lanes() < 64
-    for b in range(4):
+
+    @pl.loop(0, 4)
+    def _(b):
         for upper in range(2):
             for k in range(8):
                 even = sums[b, upper * 16 + k]
@@ -206,7 +208,7 @@
     return jnp.where(lanes() < 64, turned, above)
 
 
-def smooth_kernel(coefs, lower, own, upper, out, image, other, blur, slope, along, total, final):
+def smooth_kernel(coefs, lower, own, upper, out, fresh, image, blur, slope, along, total, final):
     column = lanes() % 64
     first_y = column == 0
     last_y = column == 63
@@ -225,16 +227,13 @@
     def clear(field, plane):
         for step in range(1, STEPS + 1):
             field[plane, step] = zero
-
-    for plane in (HALO - 1, HALO + PLANES):
-        clear(other, plane)
 
     def load(source, count, offset):
         @pl.loop(0, count // 2)
         def _(pair):
             for plane in (2 * pair, 2 * pair + 1):
                 for step in range(STEPS):
-                    image[plane + offset, step + 1] = source[plane, step]
+                    fresh[plane + offset, step + 1] = source[plane, step]
 
     place = lax.axis_index("depth")
     first_plane = HALO - place * PLANES
@@ -247,22 +246,22 @@
 
         @pl.when(outside)
         def _():
-            for plane in range(HALO):
-                clear(image, plane + offset)
+            @pl.loop(0, HALO)
+            def _(plane):
+                clear(fresh, plane + offset)
 
     load_or_clear(lower, 0, first_plane == HALO)
     load(own, PLANES, HALO)
     load_or_clear(upper, HALO + PLANES, end_plane == HALO + PLANES)
 
-    def along_y(source, plane, step):
+    def along_y(plane, step):
         if step == 0:
-            cells = left_edge(source[plane, STEPS])
+            cells = left_edge(fresh[plane, STEPS])
         elif step == STEPS + 1:
-            cells = right_edge(source[plane, 1])
+            cells = right_edge(fresh[plane, 1])
         else:
-            cells = source[plane, step]
-        if step in (0, STEPS + 1):
-            source[plane, step] = cells
+            cells = fresh[plane, step]
+        image[plane, step] = cells
         up, down = after(cells), before(cells)
         blur[plane, step] = (cells + cells) + (up + down)
         slope[plane, step] = up - down
@@ -275,16 +274,16 @@
     def depth_slope(deep):
         return [deep[k + 2] - deep[k] for k in range(GROUP)]
 
-    for sweep in range(ITERS):
-        source = image if sweep % 2 == 0 else other
-        target = other if sweep % 2 == 0 else image
+    @pl.loop(0, ITERS)
+    def _(sweep):
         margin = 2 * sweep + 1
         start = jnp.maximum(margin, first_plane - 1)
         stop = jnp.minimum(DEEP - margin, end_plane + 1)
 
-        for k in range(GROUP + 1):
+        @pl.loop(0, GROUP + 1)
+        def _(k):
             for step in range(STEPS + 2):
-                along_y(source, start - 1 + k, step)
+                along_y(start - 1 + k, step)
 
         @pl.loop(0, (stop - start) // GROUP)
         def _(group):
@@ -295,7 +294,7 @@
 
             def prepare(step):
                 for k in range(GROUP):
-                    along_y(source, plane + GROUP + k, step)
+                    along_y(plane + GROUP + k, step)
                 flat[step], deep = depth_blur(blur, plane, step)
                 steep[step] = depth_slope(deep)
                 wide[step], _ = depth_blur(slope, plane, step)
@@ -326,7 +325,7 @@
                 clear(along, edge)
                 clear(total, edge)
 
-        margin += 1
+        margin = margin + 1
         begin = jnp.maximum(margin, first_plane)
         finish = jnp.minimum(DEEP - margin, end_plane)
 
@@ -343,7 +342,7 @@
                         cells[STEPS + 1] = [right_edge(f) for f in depth_blur(field, plane, 1)[0]]
                     elif step <= STEPS:
                         cells[step], _ = depth_blur(field, plane, step)
-                deep[step] = [source[plane - 1 + k, step] for k in range(GROUP + 2)]
+                deep[step] = [image[plane - 1 + k, step] for k in range(GROUP + 2)]
                 steep = depth_slope(deep[step])
                 tilted[step] = [c_zx * steep[k] + c_xy * slope[plane + k, step] for k in range(GROUP)]
 
@@ -368,14 +367,17 @@
                         + ((tilted[step + 1][k] - tilted[step - 1][k]) + c_zy * lean[k])
                     )
                     new = now + weight * change
-                    if sweep < ITERS - 1:
-                        target[plane + k, step] = new
-                    else:
-                        base = pl.multiple_of((plane + k - HALO) * 128, 128) + (step - 1) * 8
-                        final[pl.ds(base, 8), :] = new
+                    fresh[plane + k, step] = new
+
+    @pl.loop(0, PLANES)
+    def _(plane):
+        for step in range(STEPS):
+            final[pl.ds(pl.multiple_of(plane * 128, 128) + step * 8, 8), :] = fresh[plane + HALO, step + 1]
 
     low_half = lanes() < 64
-    for b in range(4):
+
+    @pl.loop(0, 4)
+    def _(b):
         for half in range(2):
             for k in range(8):
                 base = k * 16 + b * 2 + half

time: 91.1 us -> 92.1 us (1.011)
  Pallas kernels: 17.2 us -> 18.5 us
where the time goes in v9:
time: 92.1 us; the launch traced here: 90.6 us
  blocking collectives  59.6 us (65%)
  Pallas kernels  18.5 us (20%)
  waiting for transfers between devices  10.4 us (11%)
  starting transfers between devices  2.09 us (2%)
    all_to_all x1, blocking collectives, local(): received = lax.all_to_all(sent, 'shots', 0, 0, tiled=True)  59.6 us
    pallas_call x1, Pallas kernels, smooth(): pl.pallas_call(smooth_kernel, in_specs=[vmem] * 4, out_specs=vmem, out_sh...  13.1 us
    ppermute x1, waiting for transfers between devices, local(): lax.ppermute(image[PLANES - HALO:], 'depth', [(i, (i + 1) % depth_count)...  9.14 us
    pallas_call x1, Pallas kernels, pack(): pl.pallas_call(pack_kernel, in_specs=[hbm] * 4, out_specs=[hbm, pl.BlockS...  3.34 us
    pallas_call x1, Pallas kernels, merge(): pl.pallas_call(merge_kernel, in_specs=[vmem], out_specs=vmem, out_shape=j...  2.07 us
  transfers between devices with their start and end apart: 2, of which 2 were waited for; matrix products, arithmetic and copies ran while one was open for 0% of the time, Pallas kernels for 0%

profile of v9, /device:TPU:34, one launch (start us, length us, event | category | flops | bytes accessed | tf_op | source)
XLA Modules:
  0.0 90.6 jit_solution(12858935355752083883)
XLA Ops:
  0.0 3.3 %pack_blocks.1 = (f32[32,8,4224]{2,1,0:T(8,128)}, f32[10,8,128]{2,1,0:T(8,128)}) custom-call(s32[16]{0:T(128)} %aperture_hbm.1, s32[128]{0:T(128)} %owner_map_hbm.1, s32[128]{0:T(128)} %dip_class_hbm.1, f32[16,8,4096]{2,1,0:T(8,128)} %partials.1), custom_call_target="tpu_custom_call" | custom-call | tf_op jit(solution)/shard_map/pack_blocks/pallas_call | solution.py:121
  3.3 59.6 %all_to_all.5.received = f32[32,8,4224]{2,1,0:T(8,128)S(1)} all-to-all(f32[32,8,4224]{2,1,0:T(8,128)} %get-tuple-element.8), channel_id=1, replica_groups=mesh['shots'=32,'depth'=4] {'shots'}, dimensions={0} | all-to-all | bytes 8650752 | tf_op jit(solution)/shard_map/all_to_all | solution.py:409
  63.0 0.0 copy-start
  63.0 2.1 %merge_blocks.1 = f32[1024,128]{1,0:T(8,128)S(1)} custom-call(f32[32,8,4224]{2,1,0:T(8,128)S(1)} %all_to_all.5.received), custom_call_target="tpu_custom_call" | custom-call | tf_op jit(solution)/shard_map/merge_blocks/pallas_call | solution.py:184
  65.0 0.1 fusion
  65.1 1.6 %collective-permute-start = (f32[6,16,8,128]{3,2,1,0:T(8,128)S(1)}, f32[6,16,8,128]{3,2,1,0:T(8,128)S(1)}, u32[]{:S(2)}, u32[]{:S(2)}) collective-permute-start(f32[6,16,8,128]{3,2,1,0:T(8,128)S(1)} %bitcast.5), channel_id=1, source_target_pairs={{0,1},{1,2},{2,3},{3,0},{4,5},{5,6},{6,7},{7,4},{8,9},{9,10},{10,1... | collective-permute-start | bytes 1179656 | tf_op jit(solution)/shard_map/ppermute | solution.py:412
  66.7 0.5 collective-permute-start.1
  67.2 9.1 %collective-permute-done.lower = f32[6,16,8,128]{3,2,1,0:T(8,128)S(1)} collective-permute-done((f32[6,16,8,128]{3,2,1,0:T(8,128)S(1)}, f32[6,16,8,128]{3,2,1,0:T(8,128)S(1)}, u32[]{:S(2)}, u32[]{:S(2)}) %collective-permute-start) | collective-permute-done | bytes 393248 | tf_op jit(solution)/shard_map/ppermute | solution.py:412
  76.3 1.2 %collective-permute-done.1.upper = f32[6,16,8,128]{3,2,1,0:T(8,128)S(1)} collective-permute-done((f32[6,16,8,128]{3,2,1,0:T(8,128)S(1)}, f32[6,16,8,128]{3,2,1,0:T(8,128)S(1)}, u32[]{:S(2)}, u32[]{:S(2)}) %collective-permute-start.1) | collective-permute-done | bytes 393248 | tf_op jit(solution)/shard_map/ppermute | solution.py:413
  77.5 0.0 copy-done
  77.5 13.1 %smooth_image.1 = f32[4,8,4096]{2,1,0:T(8,128)} custom-call(f32[10,8,128]{2,1,0:T(8,128)S(1)} %copy-done, f32[6,16,8,128]{3,2,1,0:T(8,128)S(1)} %collective-permute-done.lower, f32[8,16,8,128]{3,2,1,0:T(8,128)S(1)} %bitcast.3, f32[6,16,8,128]{3,2,1,0:T(8,128)S(1)} %collective-permute-done.1.upper), custom_call_target="tpu_custom_call" | custom-call | tf_op jit(solution)/shard_map/smooth_image/pallas_call | solution.py:395
Async XLA Ops:
  63.0 14.6 %copy-start = (f32[10,8,128]{2,1,0:T(8,128)S(1)}, f32[10,8,128]{2,1,0:T(8,128)}, u32[]{:S(2)}) copy-start(f32[10,8,128]{2,1,0:T(8,128)} %get-tuple-element.7.coefs) | copy-start | bytes 122884
  65.1 11.2 %collective-permute-start = (f32[6,16,8,128]{3,2,1,0:T(8,128)S(1)}, f32[6,16,8,128]{3,2,1,0:T(8,128)S(1)}, u32[]{:S(2)}, u32[]{:S(2)}) collective-permute-start(f32[6,16,8,128]{3,2,1,0:T(8,128)S(1)} %bitcast.5), channel_id=1, source_target_pairs={{0,1},{1,2},{2,3},{3,0},{4,5},{5,6},{6,7},{7,4},{8,9},{9,10},{10,1... | collective-permute-start | bytes 1179656 | tf_op jit(solution)/shard_map/ppermute | solution.py:412
  66.7 10.9 %collective-permute-start.1 = (f32[6,16,8,128]{3,2,1,0:T(8,128)S(1)}, f32[6,16,8,128]{3,2,1,0:T(8,128)S(1)}, u32[]{:S(2)}, u32[]{:S(2)}) collective-permute-start(f32[6,16,8,128]{3,2,1,0:T(8,128)S(1)} %bitcast.4), channel_id=1, source_target_pairs={{1,0},{2,1},{3,2},{0,3},{5,4},{6,5},{7,6},{4,7},{9,8},{10,9},{11,1... | collective-permute-start | bytes 1179656 | tf_op jit(solution)/shard_map/ppermute | solution.py:413

commit v10 on v7

--- a/solution.py
+++ b/solution.py
@@ -16,6 +16,7 @@
 TINY = 1e-6
 TILES = 32
 GROUP = 2
+PITCH = STEPS * 8 + 8
 
 
 def lanes():
@@ -146,7 +147,7 @@
     )(aperture, owner_map, dip_class, partials)
 
 
-def merge_kernel(received, out, places, sums, place_sem):
+def merge_kernel(received, out, places, sums, spread, place_sem):
     senders = received.shape[0]
     columns = received.shape[2] - 128
     labels = pltpu.make_async_copy(received.at[:, 0:1, columns : columns + 128], places, place_sem)
@@ -172,8 +173,11 @@
                 even = sums[b, upper * 16 + k]
                 odd = sums[b, upper * 16 + 8 + k]
                 base = k * 16 + b * 2 + upper
-                out[pl.ds(base, 8, stride=128), :] = jnp.where(low, even, pltpu.roll(odd, 64, 1))
-                out[pl.ds(base + 8, 8, stride=128), :] = jnp.where(low, pltpu.roll(even, 64, 1), odd)
+                spread[pl.ds(base, 8, stride=PITCH), :] = jnp.where(low, even, pltpu.roll(odd, 64, 1))
+                spread[pl.ds(base + 8, 8, stride=PITCH), :] = jnp.where(low, pltpu.roll(even, 64, 1), odd)
+
+    for plane in range(PLANES):
+        out[plane * STEPS * 8 : (plane + 1) * STEPS * 8, :] = spread[plane * PITCH : plane * PITCH + STEPS * 8, :]
 
 
 def merge(received):
@@ -187,6 +191,7 @@
         scratch_shapes=[
             pltpu.SMEM((senders, 1, 128), jnp.float32),
             pltpu.VMEM((4, TILES, 8, 128), jnp.float32),
+            pltpu.VMEM((PLANES * PITCH, 128), jnp.float32),
             pltpu.SemaphoreType.DMA,
         ],
         compiler_params=pltpu.CompilerParams(vmem_limit_bytes=32 << 20),
@@ -371,7 +376,7 @@
                     if sweep < ITERS - 1:
                         target[plane + k, step] = new
                     else:
-                        base = pl.multiple_of((plane + k - HALO) * 128, 128) + (step - 1) * 8
+                        base = pl.multiple_of((plane + k - HALO) * PITCH, 8) + (step - 1) * 8
                         final[pl.ds(base, 8), :] = new
 
     low_half = lanes() < 64
@@ -379,8 +384,8 @@
         for half in range(2):
             for k in range(8):
                 base = k * 16 + b * 2 + half
-                first = final[pl.ds(base, 8, stride=128), :]
-                second = final[pl.ds(base + 8, 8, stride=128), :]
+                first = final[pl.ds(base, 8, stride=PITCH), :]
+                second = final[pl.ds(base + 8, 8, stride=PITCH), :]
                 tile = half * 16 + k
                 out[b, :, tile * 128 : tile * 128 + 128] = jnp.where(low_half, first, pltpu.roll(second, 64, 1))
                 tile += 8
@@ -395,7 +400,7 @@
         in_specs=[vmem] * 4,
         out_specs=vmem,
         out_shape=jax.ShapeDtypeStruct((4, PLANES, STEPS * 256), jnp.float32),
-        scratch_shapes=[field] * 6 + [pltpu.VMEM((PLANES * STEPS * 8, 128), jnp.float32)],
+        scratch_shapes=[field] * 6 + [pltpu.VMEM((PLANES * PITCH, 128), jnp.float32)],
         compiler_params=pltpu.CompilerParams(vmem_limit_bytes=32 << 20),
         name="smooth_image",
         interpret=interpret,

time: 91.1 us -> 90.7 us (level)
  no operation moved by 1% of the time
where the time goes in v10:
time: 90.7 us; the launch traced here: 89.2 us
  blocking collectives  59.8 us (66%)
  Pallas kernels  16.9 us (19%)
  waiting for transfers between devices  10.3 us (11%)
  starting transfers between devices  2.09 us (2%)
    all_to_all x1, blocking collectives, local(): received = lax.all_to_all(sent, 'shots', 0, 0, tiled=True)  59.8 us
    pallas_call x1, Pallas kernels, smooth(): pl.pallas_call(smooth_kernel, in_specs=[vmem] * 4, out_specs=vmem, out_sh...  12 us
    ppermute x1, waiting for transfers between devices, local(): lax.ppermute(image[PLANES - HALO:], 'depth', [(i, (i + 1) % depth_count)...  9.13 us
    pallas_call x1, Pallas kernels, pack(): pl.pallas_call(pack_kernel, in_specs=[hbm] * 4, out_specs=[hbm, pl.BlockS...  3.18 us
  transfers between devices with their start and end apart: 2, of which 2 were waited for; matrix products, arithmetic and copies ran while one was open for 0% of the time, Pallas kernels for 0%

profile of v10, /device:TPU:34, one launch (start us, length us, event | category | flops | bytes accessed | tf_op | source)
XLA Modules:
  0.0 89.2 jit_solution(1701149009160672495)
XLA Ops:
  0.0 3.2 %pack_blocks.1 = (f32[32,8,4224]{2,1,0:T(8,128)}, f32[10,8,128]{2,1,0:T(8,128)}) custom-call(s32[16]{0:T(128)} %aperture_hbm.1, s32[128]{0:T(128)} %owner_map_hbm.1, s32[128]{0:T(128)} %dip_class_hbm.1, f32[16,8,4096]{2,1,0:T(8,128)} %partials.1), custom_call_target="tpu_custom_call" | custom-call | tf_op jit(solution)/shard_map/pack_blocks/pallas_call | solution.py:125
  3.2 59.8 %all_to_all.5.received = f32[32,8,4224]{2,1,0:T(8,128)S(1)} all-to-all(f32[32,8,4224]{2,1,0:T(8,128)} %get-tuple-element.8), channel_id=1, replica_groups=mesh['shots'=32,'depth'=4] {'shots'}, dimensions={0} | all-to-all | bytes 8650752 | tf_op jit(solution)/shard_map/all_to_all | solution.py:412
  63.0 0.0 copy-start
  63.0 1.8 %merge_blocks.1 = f32[1024,128]{1,0:T(8,128)S(1)} custom-call(f32[32,8,4224]{2,1,0:T(8,128)S(1)} %all_to_all.5.received), custom_call_target="tpu_custom_call" | custom-call | tf_op jit(solution)/shard_map/merge_blocks/pallas_call | solution.py:186
  64.7 0.1 fusion
  64.8 1.6 %collective-permute-start = (f32[6,16,8,128]{3,2,1,0:T(8,128)S(1)}, f32[6,16,8,128]{3,2,1,0:T(8,128)S(1)}, u32[]{:S(2)}, u32[]{:S(2)}) collective-permute-start(f32[6,16,8,128]{3,2,1,0:T(8,128)S(1)} %bitcast.5), channel_id=1, source_target_pairs={{0,1},{1,2},{2,3},{3,0},{4,5},{5,6},{6,7},{7,4},{8,9},{9,10},{10,1... | collective-permute-start | bytes 1179656 | tf_op jit(solution)/shard_map/ppermute | solution.py:415
  66.4 0.5 collective-permute-start.1
  66.9 9.1 %collective-permute-done.lower = f32[6,16,8,128]{3,2,1,0:T(8,128)S(1)} collective-permute-done((f32[6,16,8,128]{3,2,1,0:T(8,128)S(1)}, f32[6,16,8,128]{3,2,1,0:T(8,128)S(1)}, u32[]{:S(2)}, u32[]{:S(2)}) %collective-permute-start) | collective-permute-done | bytes 393248 | tf_op jit(solution)/shard_map/ppermute | solution.py:415
  76.0 1.2 %collective-permute-done.1.upper = f32[6,16,8,128]{3,2,1,0:T(8,128)S(1)} collective-permute-done((f32[6,16,8,128]{3,2,1,0:T(8,128)S(1)}, f32[6,16,8,128]{3,2,1,0:T(8,128)S(1)}, u32[]{:S(2)}, u32[]{:S(2)}) %collective-permute-start.1) | collective-permute-done | bytes 393248 | tf_op jit(solution)/shard_map/ppermute | solution.py:416
  77.2 0.0 copy-done
  77.2 12.0 %smooth_image.1 = f32[4,8,4096]{2,1,0:T(8,128)} custom-call(f32[10,8,128]{2,1,0:T(8,128)S(1)} %copy-done, f32[6,16,8,128]{3,2,1,0:T(8,128)S(1)} %collective-permute-done.lower, f32[8,16,8,128]{3,2,1,0:T(8,128)S(1)} %bitcast.3, f32[6,16,8,128]{3,2,1,0:T(8,128)S(1)} %collective-permute-done.1.upper), custom_call_target="tpu_custom_call" | custom-call | tf_op jit(solution)/shard_map/smooth_image/pallas_call | solution.py:398
Async XLA Ops:
  63.0 14.3 %copy-start = (f32[10,8,128]{2,1,0:T(8,128)S(1)}, f32[10,8,128]{2,1,0:T(8,128)}, u32[]{:S(2)}) copy-start(f32[10,8,128]{2,1,0:T(8,128)} %get-tuple-element.7.coefs) | copy-start | bytes 122884
  64.8 11.2 %collective-permute-start = (f32[6,16,8,128]{3,2,1,0:T(8,128)S(1)}, f32[6,16,8,128]{3,2,1,0:T(8,128)S(1)}, u32[]{:S(2)}, u32[]{:S(2)}) collective-permute-start(f32[6,16,8,128]{3,2,1,0:T(8,128)S(1)} %bitcast.5), channel_id=1, source_target_pairs={{0,1},{1,2},{2,3},{3,0},{4,5},{5,6},{6,7},{7,4},{8,9},{9,10},{10,1... | collective-permute-start | bytes 1179656 | tf_op jit(solution)/shard_map/ppermute | solution.py:415
  66.4 10.9 %collective-permute-start.1 = (f32[6,16,8,128]{3,2,1,0:T(8,128)S(1)}, f32[6,16,8,128]{3,2,1,0:T(8,128)S(1)}, u32[]{:S(2)}, u32[]{:S(2)}) collective-permute-start(f32[6,16,8,128]{3,2,1,0:T(8,128)S(1)} %bitcast.4), channel_id=1, source_target_pairs={{1,0},{2,1},{3,2},{0,3},{5,4},{6,5},{7,6},{4,7},{9,8},{10,9},{11,1... | collective-permute-start | bytes 1179656 | tf_op jit(solution)/shard_map/ppermute | solution.py:416

commit v11 on v10

--- a/solution.py
+++ b/solution.py
@@ -231,9 +231,6 @@
         for step in range(1, STEPS + 1):
             field[plane, step] = zero
 
-    for plane in (HALO - 1, HALO + PLANES):
-        clear(other, plane)
-
     def load(source, count, offset):
         @pl.loop(0, count // 2)
         def _(pair):
@@ -242,8 +239,8 @@
                     image[plane + offset, step + 1] = source[plane, step]
 
     place = lax.axis_index("depth")
-    first_plane = HALO - place * PLANES
-    end_plane = HALO + (lax.axis_size("depth") - place) * PLANES
+    low_end = place == 0
+    high_end = place == lax.axis_size("depth") - 1
 
     def load_or_clear(source, offset, outside):
         @pl.when(jnp.logical_not(outside))
@@ -255,9 +252,9 @@
             for plane in range(HALO):
                 clear(image, plane + offset)
 
-    load_or_clear(lower, 0, first_plane == HALO)
+    load_or_clear(lower, 0, low_end)
     load(own, PLANES, HALO)
-    load_or_clear(upper, HALO + PLANES, end_plane == HALO + PLANES)
+    load_or_clear(upper, HALO + PLANES, high_end)
 
     def along_y(source, plane, step):
         if step == 0:
@@ -280,12 +277,19 @@
     def depth_slope(deep):
         return [deep[k + 2] - deep[k] for k in range(GROUP)]
 
+    def clear_outside(*fields):
+        for outside, edge in ((low_end, HALO - 1), (high_end, HALO + PLANES)):
+
+            @pl.when(outside)
+            def _():
+                for field in fields:
+                    clear(field, edge)
+
     for sweep in range(ITERS):
         source = image if sweep % 2 == 0 else other
         target = other if sweep % 2 == 0 else image
         margin = 2 * sweep + 1
-        start = jnp.maximum(margin, first_plane - 1)
-        stop = jnp.minimum(DEEP - margin, end_plane + 1)
+        start, stop = margin, DEEP - margin
 
         for k in range(GROUP + 1):
             for step in range(STEPS + 2):
@@ -324,16 +328,10 @@
                     along[plane + k, step] = aligned
                     total[plane + k, step] = whole
 
-        for outside, edge in ((first_plane == HALO, HALO - 1), (end_plane == HALO + PLANES, HALO + PLANES)):
-
-            @pl.when(outside)
-            def _():
-                clear(along, edge)
-                clear(total, edge)
+        clear_outside(along, total)
 
         margin += 1
-        begin = jnp.maximum(margin, first_plane)
-        finish = jnp.minimum(DEEP - margin, end_plane)
+        begin, finish = margin, DEEP - margin
 
         @pl.loop(0, (finish - begin) // GROUP)
         def _(group):
@@ -379,6 +377,9 @@
                         base = pl.multiple_of((plane + k - HALO) * PITCH, 8) + (step - 1) * 8
                         final[pl.ds(base, 8), :] = new
 
+        if sweep < ITERS - 1:
+            clear_outside(target)
+
     low_half = lanes() < 64
     for b in range(4):
         for half in range(2):

time: 90.7 us -> 88.6 us (0.977)
  the two profiles are of different devices: /device:TPU:34 before, /device:TPU:1 now
where the time goes in v11:
time: 88.6 us; the launch traced here: 88.4 us
  blocking collectives  62.1 us (70%)
  Pallas kernels  14.6 us (16%)
  waiting for transfers between devices  8.89 us (10%)
  starting transfers between devices  2.75 us (3%)
    all_to_all x1, blocking collectives, local(): received = lax.all_to_all(sent, 'shots', 0, 0, tiled=True)  62.1 us
    pallas_call x1, Pallas kernels, smooth(): pl.pallas_call(smooth_kernel, in_specs=[vmem] * 4, out_specs=vmem, out_sh...  9.54 us
    ppermute x1, waiting for transfers between devices, local(): lax.ppermute(image[PLANES - HALO:], 'depth', [(i, (i + 1) % depth_count)...  8.88 us
    pallas_call x1, Pallas kernels, pack(): pl.pallas_call(pack_kernel, in_specs=[hbm] * 4, out_specs=[hbm, pl.BlockS...  3.33 us
  transfers between devices with their start and end apart: 2, of which 1 were waited for; matrix products, arithmetic and copies ran while one was open for 0% of the time, Pallas kernels for 0%

profile of v11, /device:TPU:1, one launch (start us, length us, event | category | flops | bytes accessed | tf_op | source)
XLA Modules:
  0.0 88.4 jit_solution(11715981575859659512)
XLA Ops:
  0.0 3.3 %pack_blocks.1 = (f32[32,8,4224]{2,1,0:T(8,128)}, f32[10,8,128]{2,1,0:T(8,128)}) custom-call(s32[16]{0:T(128)} %aperture_hbm.1, s32[128]{0:T(128)} %owner_map_hbm.1, s32[128]{0:T(128)} %dip_class_hbm.1, f32[16,8,4096]{2,1,0:T(8,128)} %partials.1), custom_call_target="tpu_custom_call" | custom-call | tf_op jit(solution)/shard_map/pack_blocks/pallas_call | solution.py:125
  3.3 62.1 %all_to_all.5.received = f32[32,8,4224]{2,1,0:T(8,128)S(1)} all-to-all(f32[32,8,4224]{2,1,0:T(8,128)} %get-tuple-element.8), channel_id=1, replica_groups=mesh['shots'=32,'depth'=4] {'shots'}, dimensions={0} | all-to-all | bytes 8650752 | tf_op jit(solution)/shard_map/all_to_all | solution.py:413
  65.4 0.0 copy-start
  65.4 1.7 %merge_blocks.1 = f32[1024,128]{1,0:T(8,128)S(1)} custom-call(f32[32,8,4224]{2,1,0:T(8,128)S(1)} %all_to_all.5.received), custom_call_target="tpu_custom_call" | custom-call | tf_op jit(solution)/shard_map/merge_blocks/pallas_call | solution.py:186
  67.2 0.1 fusion
  67.2 1.3 %collective-permute-start = (f32[6,16,8,128]{3,2,1,0:T(8,128)S(1)}, f32[6,16,8,128]{3,2,1,0:T(8,128)S(1)}, u32[]{:S(2)}, u32[]{:S(2)}) collective-permute-start(f32[6,16,8,128]{3,2,1,0:T(8,128)S(1)} %bitcast.5), channel_id=1, source_target_pairs={{0,1},{1,2},{2,3},{3,0},{4,5},{5,6},{6,7},{7,4},{8,9},{9,10},{10,1... | collective-permute-start | bytes 1179656 | tf_op jit(solution)/shard_map/ppermute | solution.py:416
  68.5 1.5 %collective-permute-start.1 = (f32[6,16,8,128]{3,2,1,0:T(8,128)S(1)}, f32[6,16,8,128]{3,2,1,0:T(8,128)S(1)}, u32[]{:S(2)}, u32[]{:S(2)}) collective-permute-start(f32[6,16,8,128]{3,2,1,0:T(8,128)S(1)} %bitcast.4), channel_id=1, source_target_pairs={{1,0},{2,1},{3,2},{0,3},{5,4},{6,5},{7,6},{4,7},{9,8},{10,9},{11,1... | collective-permute-start | bytes 1179656 | tf_op jit(solution)/shard_map/ppermute | solution.py:417
  70.0 8.9 %collective-permute-done.lower = f32[6,16,8,128]{3,2,1,0:T(8,128)S(1)} collective-permute-done((f32[6,16,8,128]{3,2,1,0:T(8,128)S(1)}, f32[6,16,8,128]{3,2,1,0:T(8,128)S(1)}, u32[]{:S(2)}, u32[]{:S(2)}) %collective-permute-start) | collective-permute-done | bytes 393248 | tf_op jit(solution)/shard_map/ppermute | solution.py:416
  78.8 0.0 collective-permute-done.1.upper
  78.8 0.0 copy-done
  78.8 9.5 %smooth_image.1 = f32[4,8,4096]{2,1,0:T(8,128)} custom-call(f32[10,8,128]{2,1,0:T(8,128)S(1)} %copy-done, f32[6,16,8,128]{3,2,1,0:T(8,128)S(1)} %collective-permute-done.lower, f32[8,16,8,128]{3,2,1,0:T(8,128)S(1)} %bitcast.3, f32[6,16,8,128]{3,2,1,0:T(8,128)S(1)} %collective-permute-done.1.upper), custom_call_target="tpu_custom_call" | custom-call | tf_op jit(solution)/shard_map/smooth_image/pallas_call | solution.py:399
Async XLA Ops:
  65.4 13.4 %copy-start = (f32[10,8,128]{2,1,0:T(8,128)S(1)}, f32[10,8,128]{2,1,0:T(8,128)}, u32[]{:S(2)}) copy-start(f32[10,8,128]{2,1,0:T(8,128)} %get-tuple-element.7.coefs) | copy-start | bytes 122884
  67.2 11.6 %collective-permute-start = (f32[6,16,8,128]{3,2,1,0:T(8,128)S(1)}, f32[6,16,8,128]{3,2,1,0:T(8,128)S(1)}, u32[]{:S(2)}, u32[]{:S(2)}) collective-permute-start(f32[6,16,8,128]{3,2,1,0:T(8,128)S(1)} %bitcast.5), channel_id=1, source_target_pairs={{0,1},{1,2},{2,3},{3,0},{4,5},{5,6},{6,7},{7,4},{8,9},{9,10},{10,1... | collective-permute-start | bytes 1179656 | tf_op jit(solution)/shard_map/ppermute | solution.py:416
  68.5 10.4 %collective-permute-start.1 = (f32[6,16,8,128]{3,2,1,0:T(8,128)S(1)}, f32[6,16,8,128]{3,2,1,0:T(8,128)S(1)}, u32[]{:S(2)}, u32[]{:S(2)}) collective-permute-start(f32[6,16,8,128]{3,2,1,0:T(8,128)S(1)} %bitcast.4), channel_id=1, source_target_pairs={{1,0},{2,1},{3,2},{0,3},{5,4},{6,5},{7,6},{4,7},{9,8},{10,9},{11,1... | collective-permute-start | bytes 1179656 | tf_op jit(solution)/shard_map/ppermute | solution.py:417

commit v12 on v11

--- a/solution.py
+++ b/solution.py
@@ -75,6 +75,17 @@
     def block(slot, owner):
         return pltpu.make_async_copy(blocks.at[slot], out.at[owner, :, 0:columns], out_sems.at[slot])
 
+    base = lax.axis_index("shots") * 4
+    for place in range(4):
+        owned[place] = 0
+
+    @pl.loop(0, owner_map.shape[0] // 8)
+    def _(group):
+        for k in range(8):
+            brick = group * 8 + k
+            place = owner_map[brick] - base
+            owned[jnp.where(jnp.logical_and(place >= 0, place < 4), place, 4)] = dip_class[brick]
+
     for slot in range(slots):
         fetches[slot].wait()
         brick = aperture[slot]
@@ -88,20 +99,6 @@
 
     labels = pltpu.make_async_copy(places, out.at[:, :, columns : columns + 128], place_sem)
     labels.start()
-
-    base = lax.axis_index("shots") * 4
-    for place in range(4):
-        owned[place] = 0
-
-    @pl.loop(0, owner_map.shape[0] // 8)
-    def _(group):
-        for k in range(8):
-            brick = group * 8 + k
-            place = owner_map[brick] - base
-
-            @pl.when(jnp.logical_and(place >= 0, place < 4))
-            def _():
-                owned[place] = dip_class[brick]
 
     brick_of_row = rows() // 2
     classes = jnp.full((8, 128), owned[3], jnp.int32)
@@ -134,7 +131,7 @@
             pltpu.SMEM(aperture.shape, jnp.int32),
             pltpu.SMEM(owner_map.shape, jnp.int32),
             pltpu.SMEM(dip_class.shape, jnp.int32),
-            pltpu.SMEM((4,), jnp.int32),
+            pltpu.SMEM((8,), jnp.int32),
             pltpu.VMEM(partials.shape, jnp.float32),
             pltpu.VMEM((owners, planes, 128), jnp.float32),
             pltpu.SemaphoreType.DMA((3,)),
@@ -211,7 +208,7 @@
     return jnp.where(lanes() < 64, turned, above)
 
 
-def smooth_kernel(coefs, lower, own, upper, out, image, other, blur, slope, along, total, final):
+def smooth_kernel(coefs, lower, own, upper, out, image, other, blur, slope, along, total, final, bricks, out_sems):
     column = lanes() % 64
     first_y = column == 0
     last_y = column == 63
@@ -381,6 +378,7 @@
             clear_outside(target)
 
     low_half = lanes() < 64
+    copies = [pltpu.make_async_copy(bricks.at[b], out.at[b], out_sems.at[b]) for b in range(4)]
     for b in range(4):
         for half in range(2):
             for k in range(8):
@@ -388,9 +386,12 @@
                 first = final[pl.ds(base, 8, stride=PITCH), :]
                 second = final[pl.ds(base + 8, 8, stride=PITCH), :]
                 tile = half * 16 + k
-                out[b, :, tile * 128 : tile * 128 + 128] = jnp.where(low_half, first, pltpu.roll(second, 64, 1))
+                bricks[b, :, tile * 128 : tile * 128 + 128] = jnp.where(low_half, first, pltpu.roll(second, 64, 1))
                 tile += 8
-                out[b, :, tile * 128 : tile * 128 + 128] = jnp.where(low_half, pltpu.roll(first, 64, 1), second)
+                bricks[b, :, tile * 128 : tile * 128 + 128] = jnp.where(low_half, pltpu.roll(first, 64, 1), second)
+        copies[b].start()
+    for copy in copies:
+        copy.wait()
 
 
 def smooth(coefs, lower, own, upper, interpret=False):
@@ -399,9 +400,14 @@
     return pl.pallas_call(
         smooth_kernel,
         in_specs=[vmem] * 4,
-        out_specs=vmem,
+        out_specs=pl.BlockSpec(memory_space=pltpu.HBM),
         out_shape=jax.ShapeDtypeStruct((4, PLANES, STEPS * 256), jnp.float32),
-        scratch_shapes=[field] * 6 + [pltpu.VMEM((PLANES * PITCH, 128), jnp.float32)],
+        scratch_shapes=[field] * 6
+        + [
+            pltpu.VMEM((PLANES * PITCH, 128), jnp.float32),
+            pltpu.VMEM((4, PLANES, STEPS * 256), jnp.float32),
+            pltpu.SemaphoreType.DMA((4,)),
+        ],
         compiler_params=pltpu.CompilerParams(vmem_limit_bytes=32 << 20),
         name="smooth_image",
         interpret=interpret,

time: 88.6 us -> 88.8 us (level)
  no operation moved by 1% of the time
where the time goes in v12:
time: 88.8 us; the launch traced here: 88.6 us
  blocking collectives  62.2 us (70%)
  Pallas kernels  14.7 us (17%)
  waiting for transfers between devices  8.86 us (10%)
  starting transfers between devices  2.75 us (3%)
    all_to_all x1, blocking collectives, local(): received = lax.all_to_all(sent, 'shots', 0, 0, tiled=True)  62.2 us
    pallas_call x1, Pallas kernels, smooth(): pl.pallas_call(smooth_kernel, in_specs=[vmem] * 4, out_specs=pl.BlockSpec...  9.46 us
    ppermute x1, waiting for transfers between devices, local(): lax.ppermute(image[PLANES - HALO:], 'depth', [(i, (i + 1) % depth_count)...  8.86 us
    pallas_call x1, Pallas kernels, pack(): pl.pallas_call(pack_kernel, in_specs=[hbm] * 4, out_specs=[hbm, pl.BlockS...  3.52 us
  transfers between devices with their start and end apart: 2, of which 1 were waited for; matrix products, arithmetic and copies ran while one was open for 0% of the time, Pallas kernels for 0%

profile of v12, /device:TPU:1, one launch (start us, length us, event | category | flops | bytes accessed | tf_op | source)
XLA Modules:
  0.0 88.6 jit_solution(17961802766939140464)
XLA Ops:
  0.0 3.5 %pack_blocks.1 = (f32[32,8,4224]{2,1,0:T(8,128)}, f32[10,8,128]{2,1,0:T(8,128)}) custom-call(s32[16]{0:T(128)} %aperture_hbm.1, s32[128]{0:T(128)} %owner_map_hbm.1, s32[128]{0:T(128)} %dip_class_hbm.1, f32[16,8,4096]{2,1,0:T(8,128)} %partials.1), custom_call_target="tpu_custom_call" | custom-call | tf_op jit(solution)/shard_map/pack_blocks/pallas_call | solution.py:122
  3.5 62.2 %all_to_all.5.received = f32[32,8,4224]{2,1,0:T(8,128)S(1)} all-to-all(f32[32,8,4224]{2,1,0:T(8,128)} %get-tuple-element.8), channel_id=1, replica_groups=mesh['shots'=32,'depth'=4] {'shots'}, dimensions={0} | all-to-all | bytes 8650752 | tf_op jit(solution)/shard_map/all_to_all | solution.py:419
  65.7 0.0 copy-start
  65.7 1.7 %merge_blocks.1 = f32[1024,128]{1,0:T(8,128)S(1)} custom-call(f32[32,8,4224]{2,1,0:T(8,128)S(1)} %all_to_all.5.received), custom_call_target="tpu_custom_call" | custom-call | tf_op jit(solution)/shard_map/merge_blocks/pallas_call | solution.py:183
  67.4 0.1 fusion
  67.5 1.3 %collective-permute-start = (f32[6,16,8,128]{3,2,1,0:T(8,128)S(1)}, f32[6,16,8,128]{3,2,1,0:T(8,128)S(1)}, u32[]{:S(2)}, u32[]{:S(2)}) collective-permute-start(f32[6,16,8,128]{3,2,1,0:T(8,128)S(1)} %bitcast.5), channel_id=1, source_target_pairs={{0,1},{1,2},{2,3},{3,0},{4,5},{5,6},{6,7},{7,4},{8,9},{9,10},{10,1... | collective-permute-start | bytes 1179656 | tf_op jit(solution)/shard_map/ppermute | solution.py:422
  68.8 1.5 %collective-permute-start.1 = (f32[6,16,8,128]{3,2,1,0:T(8,128)S(1)}, f32[6,16,8,128]{3,2,1,0:T(8,128)S(1)}, u32[]{:S(2)}, u32[]{:S(2)}) collective-permute-start(f32[6,16,8,128]{3,2,1,0:T(8,128)S(1)} %bitcast.4), channel_id=1, source_target_pairs={{1,0},{2,1},{3,2},{0,3},{5,4},{6,5},{7,6},{4,7},{9,8},{10,9},{11,1... | collective-permute-start | bytes 1179656 | tf_op jit(solution)/shard_map/ppermute | solution.py:423
  70.2 8.9 %collective-permute-done.lower = f32[6,16,8,128]{3,2,1,0:T(8,128)S(1)} collective-permute-done((f32[6,16,8,128]{3,2,1,0:T(8,128)S(1)}, f32[6,16,8,128]{3,2,1,0:T(8,128)S(1)}, u32[]{:S(2)}, u32[]{:S(2)}) %collective-permute-start) | collective-permute-done | bytes 393248 | tf_op jit(solution)/shard_map/ppermute | solution.py:422
  79.1 0.0 collective-permute-done.1.upper
  79.1 0.0 copy-done
  79.1 9.5 %smooth_image.1 = f32[4,8,4096]{2,1,0:T(8,128)} custom-call(f32[10,8,128]{2,1,0:T(8,128)S(1)} %copy-done, f32[6,16,8,128]{3,2,1,0:T(8,128)S(1)} %collective-permute-done.lower, f32[8,16,8,128]{3,2,1,0:T(8,128)S(1)} %bitcast.3, f32[6,16,8,128]{3,2,1,0:T(8,128)S(1)} %collective-permute-done.1.upper), custom_call_target="tpu_custom_call" | custom-call | tf_op jit(solution)/shard_map/smooth_image/pallas_call | solution.py:400
Async XLA Ops:
  65.7 13.4 %copy-start = (f32[10,8,128]{2,1,0:T(8,128)S(1)}, f32[10,8,128]{2,1,0:T(8,128)}, u32[]{:S(2)}) copy-start(f32[10,8,128]{2,1,0:T(8,128)} %get-tuple-element.7.coefs) | copy-start | bytes 122884
  67.5 11.6 %collective-permute-start = (f32[6,16,8,128]{3,2,1,0:T(8,128)S(1)}, f32[6,16,8,128]{3,2,1,0:T(8,128)S(1)}, u32[]{:S(2)}, u32[]{:S(2)}) collective-permute-start(f32[6,16,8,128]{3,2,1,0:T(8,128)S(1)} %bitcast.5), channel_id=1, source_target_pairs={{0,1},{1,2},{2,3},{3,0},{4,5},{5,6},{6,7},{7,4},{8,9},{9,10},{10,1... | collective-permute-start | bytes 1179656 | tf_op jit(solution)/shard_map/ppermute | solution.py:422
  68.8 10.3 %collective-permute-start.1 = (f32[6,16,8,128]{3,2,1,0:T(8,128)S(1)}, f32[6,16,8,128]{3,2,1,0:T(8,128)S(1)}, u32[]{:S(2)}, u32[]{:S(2)}) collective-permute-start(f32[6,16,8,128]{3,2,1,0:T(8,128)S(1)} %bitcast.4), channel_id=1, source_target_pairs={{1,0},{2,1},{3,2},{0,3},{5,4},{6,5},{7,6},{4,7},{9,8},{10,9},{11,1... | collective-permute-start | bytes 1179656 | tf_op jit(solution)/shard_map/ppermute | solution.py:423

commit v13 on v12

--- a/solution.py
+++ b/solution.py
@@ -28,11 +28,20 @@
 
 
 def coefficients(classes):
-    tilt = 0.2 + 0.1 * (classes & 3).astype(jnp.float32)
-    azimuth = 0.3 + math.pi / 2.0 * (classes >> 2).astype(jnp.float32)
-    norm_z = jnp.cos(tilt)
-    norm_x = jnp.sin(tilt) * jnp.cos(azimuth)
-    norm_y = jnp.sin(tilt) * jnp.sin(azimuth)
+    tilts = [0.2 + 0.1 * i for i in range(4)]
+    azimuths = [0.3 + math.pi / 2.0 * i for i in range(2)]
+
+    def pick(index, values):
+        chosen = jnp.full(index.shape, values[-1], jnp.float32)
+        for i, value in enumerate(values[:-1]):
+            chosen = jnp.where(index == i, jnp.float32(value), chosen)
+        return chosen
+
+    tilt, azimuth = classes & 3, classes >> 2
+    lean = pick(tilt, [math.sin(angle) for angle in tilts])
+    norm_z = pick(tilt, [math.cos(angle) for angle in tilts])
+    norm_x = lean * pick(azimuth, [math.cos(angle) for angle in azimuths])
+    norm_y = lean * pick(azimuth, [math.sin(angle) for angle in azimuths])
     c_zz = RATE * (1.0 - norm_z * norm_z)
     c_xx = RATE * (1.0 - norm_x * norm_x)
     c_yy = RATE * (1.0 - norm_y * norm_y)

time: 88.8 us -> 88.8 us (level)
  no operation moved by 1% of the time
where the time goes in v13:
time: 88.8 us; the launch traced here: 88.5 us
  blocking collectives  62.5 us (70%)
  Pallas kernels  14.4 us (16%)
  waiting for transfers between devices  8.88 us (10%)
  starting transfers between devices  2.75 us (3%)
    all_to_all x1, blocking collectives, local(): received = lax.all_to_all(sent, 'shots', 0, 0, tiled=True)  62.5 us
    pallas_call x1, Pallas kernels, smooth(): pl.pallas_call(smooth_kernel, in_specs=[vmem] * 4, out_specs=pl.BlockSpec...  9.46 us
    ppermute x1, waiting for transfers between devices, local(): lax.ppermute(image[PLANES - HALO:], 'depth', [(i, (i + 1) % depth_count)...  8.87 us
    pallas_call x1, Pallas kernels, pack(): pl.pallas_call(pack_kernel, in_specs=[hbm] * 4, out_specs=[hbm, pl.BlockS...  3.24 us
  transfers between devices with their start and end apart: 2, of which 1 were waited for; matrix products, arithmetic and copies ran while one was open for 0% of the time, Pallas kernels for 0%

profile of v13, /device:TPU:1, one launch (start us, length us, event | category | flops | bytes accessed | tf_op | source)
XLA Modules:
  0.0 88.5 jit_solution(8920013376816985964)
XLA Ops:
  0.0 3.2 %pack_blocks.1 = (f32[32,8,4224]{2,1,0:T(8,128)}, f32[10,8,128]{2,1,0:T(8,128)}) custom-call(s32[16]{0:T(128)} %aperture_hbm.1, s32[128]{0:T(128)} %owner_map_hbm.1, s32[128]{0:T(128)} %dip_class_hbm.1, f32[16,8,4096]{2,1,0:T(8,128)} %partials.1), custom_call_target="tpu_custom_call" | custom-call | tf_op jit(solution)/shard_map/pack_blocks/pallas_call | solution.py:131
  3.2 62.5 %all_to_all.5.received = f32[32,8,4224]{2,1,0:T(8,128)S(1)} all-to-all(f32[32,8,4224]{2,1,0:T(8,128)} %get-tuple-element.8), channel_id=1, replica_groups=mesh['shots'=32,'depth'=4] {'shots'}, dimensions={0} | all-to-all | bytes 8650752 | tf_op jit(solution)/shard_map/all_to_all | solution.py:428
  65.7 0.0 copy-start
  65.7 1.7 %merge_blocks.1 = f32[1024,128]{1,0:T(8,128)S(1)} custom-call(f32[32,8,4224]{2,1,0:T(8,128)S(1)} %all_to_all.5.received), custom_call_target="tpu_custom_call" | custom-call | tf_op jit(solution)/shard_map/merge_blocks/pallas_call | solution.py:192
  67.4 0.1 fusion
  67.5 1.3 %collective-permute-start = (f32[6,16,8,128]{3,2,1,0:T(8,128)S(1)}, f32[6,16,8,128]{3,2,1,0:T(8,128)S(1)}, u32[]{:S(2)}, u32[]{:S(2)}) collective-permute-start(f32[6,16,8,128]{3,2,1,0:T(8,128)S(1)} %bitcast.5), channel_id=1, source_target_pairs={{0,1},{1,2},{2,3},{3,0},{4,5},{5,6},{6,7},{7,4},{8,9},{9,10},{10,1... | collective-permute-start | bytes 1179656 | tf_op jit(solution)/shard_map/ppermute | solution.py:431
  68.7 1.5 %collective-permute-start.1 = (f32[6,16,8,128]{3,2,1,0:T(8,128)S(1)}, f32[6,16,8,128]{3,2,1,0:T(8,128)S(1)}, u32[]{:S(2)}, u32[]{:S(2)}) collective-permute-start(f32[6,16,8,128]{3,2,1,0:T(8,128)S(1)} %bitcast.4), channel_id=1, source_target_pairs={{1,0},{2,1},{3,2},{0,3},{5,4},{6,5},{7,6},{4,7},{9,8},{10,9},{11,1... | collective-permute-start | bytes 1179656 | tf_op jit(solution)/shard_map/ppermute | solution.py:432
  70.2 8.9 %collective-permute-done.lower = f32[6,16,8,128]{3,2,1,0:T(8,128)S(1)} collective-permute-done((f32[6,16,8,128]{3,2,1,0:T(8,128)S(1)}, f32[6,16,8,128]{3,2,1,0:T(8,128)S(1)}, u32[]{:S(2)}, u32[]{:S(2)}) %collective-permute-start) | collective-permute-done | bytes 393248 | tf_op jit(solution)/shard_map/ppermute | solution.py:431
  79.1 0.0 collective-permute-done.1.upper
  79.1 0.0 copy-done
  79.1 9.5 %smooth_image.1 = f32[4,8,4096]{2,1,0:T(8,128)} custom-call(f32[10,8,128]{2,1,0:T(8,128)S(1)} %copy-done, f32[6,16,8,128]{3,2,1,0:T(8,128)S(1)} %collective-permute-done.lower, f32[8,16,8,128]{3,2,1,0:T(8,128)S(1)} %bitcast.3, f32[6,16,8,128]{3,2,1,0:T(8,128)S(1)} %collective-permute-done.1.upper), custom_call_target="tpu_custom_call" | custom-call | tf_op jit(solution)/shard_map/smooth_image/pallas_call | solution.py:409
Async XLA Ops:
  65.7 13.4 %copy-start = (f32[10,8,128]{2,1,0:T(8,128)S(1)}, f32[10,8,128]{2,1,0:T(8,128)}, u32[]{:S(2)}) copy-start(f32[10,8,128]{2,1,0:T(8,128)} %get-tuple-element.7.coefs) | copy-start | bytes 122884
  67.5 11.6 %collective-permute-start = (f32[6,16,8,128]{3,2,1,0:T(8,128)S(1)}, f32[6,16,8,128]{3,2,1,0:T(8,128)S(1)}, u32[]{:S(2)}, u32[]{:S(2)}) collective-permute-start(f32[6,16,8,128]{3,2,1,0:T(8,128)S(1)} %bitcast.5), channel_id=1, source_target_pairs={{0,1},{1,2},{2,3},{3,0},{4,5},{5,6},{6,7},{7,4},{8,9},{9,10},{10,1... | collective-permute-start | bytes 1179656 | tf_op jit(solution)/shard_map/ppermute | solution.py:431
  68.7 10.3 %collective-permute-start.1 = (f32[6,16,8,128]{3,2,1,0:T(8,128)S(1)}, f32[6,16,8,128]{3,2,1,0:T(8,128)S(1)}, u32[]{:S(2)}, u32[]{:S(2)}) collective-permute-start(f32[6,16,8,128]{3,2,1,0:T(8,128)S(1)} %bitcast.4), channel_id=1, source_target_pairs={{1,0},{2,1},{3,2},{0,3},{5,4},{6,5},{7,6},{4,7},{9,8},{10,9},{11,1... | collective-permute-start | bytes 1179656 | tf_op jit(solution)/shard_map/ppermute | solution.py:432

commit v14 on v12

--- a/solution.py
+++ b/solution.py
@@ -52,7 +52,7 @@
 
 
 def pack_kernel(
-    aperture_hbm, owner_map_hbm, dip_class_hbm, partials, out, coefs, aperture, owner_map, dip_class, owned,
+    aperture_hbm, owner_map_hbm, partials, out, aperture, owner_map,
     blocks, places, table_sems, in_sems, out_sems, place_sem
 ):
     slots = partials.shape[0]
@@ -60,7 +60,6 @@
     tables = [
         pltpu.make_async_copy(aperture_hbm, aperture, table_sems.at[0]),
         pltpu.make_async_copy(owner_map_hbm, owner_map, table_sems.at[1]),
-        pltpu.make_async_copy(dip_class_hbm, dip_class, table_sems.at[2]),
     ]
     for copy in tables:
         copy.start()
@@ -75,6 +74,61 @@
     def block(slot, owner):
         return pltpu.make_async_copy(blocks.at[slot], out.at[owner, :, 0:columns], out_sems.at[slot])
 
+    for slot in range(slots):
+        fetches[slot].wait()
+        brick = aperture[slot]
+
+        @pl.when(brick >= 0)
+        def _():
+            row = owner_map[brick]
+            owner = row // 4
+            block(slot, owner).start()
+            places[owner] = jnp.full((8, 128), row % 4, jnp.int32).astype(jnp.float32)
+
+    labels = pltpu.make_async_copy(places, out.at[:, :, columns : columns + 128], place_sem)
+    labels.start()
+
+    for slot in range(slots):
+
+        @pl.when(aperture[slot] >= 0)
+        def _():
+            block(slot, 0).wait()
+
+    labels.wait()
+
+
+def pack(aperture, owner_map, partials, owners):
+    slots, planes, columns = partials.shape
+    hbm = pl.BlockSpec(memory_space=pltpu.HBM)
+    return pl.pallas_call(
+        pack_kernel,
+        in_specs=[hbm] * 3,
+        out_specs=hbm,
+        out_shape=jax.ShapeDtypeStruct((owners, planes, columns + 128), jnp.float32),
+        scratch_shapes=[
+            pltpu.SMEM(aperture.shape, jnp.int32),
+            pltpu.SMEM(owner_map.shape, jnp.int32),
+            pltpu.VMEM(partials.shape, jnp.float32),
+            pltpu.VMEM((owners, planes, 128), jnp.float32),
+            pltpu.SemaphoreType.DMA((2,)),
+            pltpu.SemaphoreType.DMA((slots,)),
+            pltpu.SemaphoreType.DMA((slots,)),
+            pltpu.SemaphoreType.DMA,
+        ],
+        compiler_params=pltpu.CompilerParams(vmem_limit_bytes=60 << 20),
+        name="pack_blocks",
+    )(aperture, owner_map, partials)
+
+
+def factors_kernel(owner_map_hbm, dip_class_hbm, merged, coefs, owner_map, dip_class, owned, table_sems):
+    tables = [
+        pltpu.make_async_copy(owner_map_hbm, owner_map, table_sems.at[0]),
+        pltpu.make_async_copy(dip_class_hbm, dip_class, table_sems.at[1]),
+    ]
+    for copy in tables:
+        copy.start()
+    for copy in tables:
+        copy.wait()
     base = lax.axis_index("shots") * 4
     for place in range(4):
         owned[place] = 0
@@ -86,20 +140,6 @@
             place = owner_map[brick] - base
             owned[jnp.where(jnp.logical_and(place >= 0, place < 4), place, 4)] = dip_class[brick]
 
-    for slot in range(slots):
-        fetches[slot].wait()
-        brick = aperture[slot]
-
-        @pl.when(brick >= 0)
-        def _():
-            row = owner_map[brick]
-            owner = row // 4
-            block(slot, owner).start()
-            places[owner] = jnp.full((8, 128), row % 4, jnp.int32).astype(jnp.float32)
-
-    labels = pltpu.make_async_copy(places, out.at[:, :, columns : columns + 128], place_sem)
-    labels.start()
-
     brick_of_row = rows() // 2
     classes = jnp.full((8, 128), owned[3], jnp.int32)
     for place in range(3):
@@ -107,41 +147,24 @@
     for i, value in enumerate(coefficients(classes)):
         coefs[i] = value
 
-    for slot in range(slots):
-
-        @pl.when(aperture[slot] >= 0)
-        def _():
-            block(slot, 0).wait()
-
-    labels.wait()
-
-
-def pack(aperture, owner_map, dip_class, partials, owners):
-    slots, planes, columns = partials.shape
+
+def factors(owner_map, dip_class, merged):
     hbm = pl.BlockSpec(memory_space=pltpu.HBM)
+    vmem = pl.BlockSpec(memory_space=pltpu.VMEM)
     return pl.pallas_call(
-        pack_kernel,
-        in_specs=[hbm] * 4,
-        out_specs=[hbm, pl.BlockSpec(memory_space=pltpu.VMEM)],
-        out_shape=[
-            jax.ShapeDtypeStruct((owners, planes, columns + 128), jnp.float32),
-            jax.ShapeDtypeStruct((10, 8, 128), jnp.float32),
-        ],
+        factors_kernel,
+        in_specs=[hbm, hbm, vmem],
+        out_specs=vmem,
+        out_shape=jax.ShapeDtypeStruct((10, 8, 128), jnp.float32),
         scratch_shapes=[
-            pltpu.SMEM(aperture.shape, jnp.int32),
             pltpu.SMEM(owner_map.shape, jnp.int32),
             pltpu.SMEM(dip_class.shape, jnp.int32),
             pltpu.SMEM((8,), jnp.int32),
-            pltpu.VMEM(partials.shape, jnp.float32),
-            pltpu.VMEM((owners, planes, 128), jnp.float32),
-            pltpu.SemaphoreType.DMA((3,)),
-            pltpu.SemaphoreType.DMA((slots,)),
-            pltpu.SemaphoreType.DMA((slots,)),
-            pltpu.SemaphoreType.DMA,
+            pltpu.SemaphoreType.DMA((2,)),
         ],
-        compiler_params=pltpu.CompilerParams(vmem_limit_bytes=60 << 20),
-        name="pack_blocks",
-    )(aperture, owner_map, dip_class, partials)
+        compiler_params=pltpu.CompilerParams(vmem_limit_bytes=56 << 20),
+        name="update_factors",
+    )(owner_map, dip_class, merged)
 
 
 def merge_kernel(received, out, places, sums, spread, place_sem):
@@ -415,12 +438,13 @@
 
 
 def local(partials, aperture, owner_map, dip_class):
-    sent, coefs = pack(aperture, owner_map, dip_class, partials, lax.axis_size("shots"))
+    sent = pack(aperture, owner_map, partials, lax.axis_size("shots"))
     received = lax.all_to_all(sent, "shots", 0, 0, tiled=True)
     image = merge(received).reshape(PLANES, STEPS, 8, 128)
     depth_count = lax.axis_size("depth")
     lower = lax.ppermute(image[PLANES - HALO :], "depth", [(i, (i + 1) % depth_count) for i in range(depth_count)])
     upper = lax.ppermute(image[:HALO], "depth", [((i + 1) % depth_count, i) for i in range(depth_count)])
+    coefs = factors(owner_map, dip_class, image[0, 0])
     return smooth(coefs, lower, image, upper)
 
 

time: 88.8 us -> 88.4 us (level)
  waiting for transfers between devices: 8.86 us -> 5.83 us
  local copies, waits for them, and re-layouts: 0.06 us -> 1.42 us
  Pallas kernels: 14.7 us -> 15.9 us
    ppermute x1, waiting for transfers between devices: 8.86 us -> 5.83 us  [local(): lax.ppermute(image[PLANES - HALO:], 'depth', [(i, (i + 1) % depth_count)...]
    pallas_call x1 -> x2, Pallas kernels: 3.52 us -> 5.02 us  [the longest x1 2.57 us: pack(): pl.pallas_call(pack_kernel, in_specs=[hbm] * 3, out_specs=hbm, out_shape=...]
  transfers between devices with their start and end apart: 2 -> 2, of which waited for: 1 -> 1; matrix products, arithmetic and copies ran while one was open for 0% -> 1% of each run, Pallas kernels for 0% -> 3%
where the time goes in v14:
time: 88.4 us; the launch traced here: 88.2 us
  blocking collectives  62.3 us (70%)
  Pallas kernels  15.9 us (18%)
  waiting for transfers between devices  5.83 us (7%)
  starting transfers between devices  2.75 us (3%)
  local copies, waits for them, and re-layouts  1.42 us (2%)
    all_to_all x1, blocking collectives, local(): received = lax.all_to_all(sent, 'shots', 0, 0, tiled=True)  62.3 us
    pallas_call x1, Pallas kernels, smooth(): pl.pallas_call(smooth_kernel, in_specs=[vmem] * 4, out_specs=pl.BlockSpec...  9.16 us
    ppermute x1, waiting for transfers between devices, local(): lax.ppermute(image[PLANES - HALO:], 'depth', [(i, (i + 1) % depth_count)...  5.83 us
    pallas_call x1, Pallas kernels, pack(): pl.pallas_call(pack_kernel, in_specs=[hbm] * 3, out_specs=hbm, out_shape=...  2.57 us
    pallas_call x1, Pallas kernels, factors(): pl.pallas_call(factors_kernel, in_specs=[hbm, hbm, vmem], out_specs=vmem,...  2.44 us
  transfers between devices with their start and end apart: 2, of which 1 were waited for; matrix products, arithmetic and copies ran while one was open for 1% of the time, Pallas kernels for 3%

profile of v14, /device:TPU:1, one launch (start us, length us, event | category | flops | bytes accessed | tf_op | source)
XLA Modules:
  0.0 88.2 jit_solution(6518783847253934283)
XLA Ops:
  0.0 2.6 %pack_blocks.1 = f32[32,8,4224]{2,1,0:T(8,128)} custom-call(s32[16]{0:T(128)} %aperture_hbm.1, s32[128]{0:T(128)} %owner_map_hbm.3, f32[16,8,4096]{2,1,0:T(8,128)} %partials.1), custom_call_target="tpu_custom_call" | custom-call | tf_op jit(solution)/shard_map/pack_blocks/pallas_call | solution.py:103
  2.6 62.3 %all_to_all.5.received = f32[32,8,4224]{2,1,0:T(8,128)S(1)} all-to-all(f32[32,8,4224]{2,1,0:T(8,128)} %pack_blocks.1), channel_id=1, replica_groups=mesh['shots'=32,'depth'=4] {'shots'}, dimensions={0} | all-to-all | bytes 8650752 | tf_op jit(solution)/shard_map/all_to_all | solution.py:442
  64.8 1.7 %merge_blocks.1 = f32[1024,128]{1,0:T(8,128)S(1)} custom-call(f32[32,8,4224]{2,1,0:T(8,128)S(1)} %all_to_all.5.received), custom_call_target="tpu_custom_call" | custom-call | tf_op jit(solution)/shard_map/merge_blocks/pallas_call | solution.py:206
  66.5 0.1 fusion
  66.6 1.3 %collective-permute-start = (f32[6,16,8,128]{3,2,1,0:T(8,128)S(1)}, f32[6,16,8,128]{3,2,1,0:T(8,128)S(1)}, u32[]{:S(2)}, u32[]{:S(2)}) collective-permute-start(f32[6,16,8,128]{3,2,1,0:T(8,128)S(1)} %bitcast.8), channel_id=1, source_target_pairs={{0,1},{1,2},{2,3},{3,0},{4,5},{5,6},{6,7},{7,4},{8,9},{9,10},{10,1... | collective-permute-start | bytes 1179656 | tf_op jit(solution)/shard_map/ppermute | solution.py:445
  67.9 1.5 %collective-permute-start.1 = (f32[6,16,8,128]{3,2,1,0:T(8,128)S(1)}, f32[6,16,8,128]{3,2,1,0:T(8,128)S(1)}, u32[]{:S(2)}, u32[]{:S(2)}) collective-permute-start(f32[6,16,8,128]{3,2,1,0:T(8,128)S(1)} %bitcast.7), channel_id=1, source_target_pairs={{1,0},{2,1},{3,2},{0,3},{5,4},{6,5},{7,6},{4,7},{9,8},{10,9},{11,1... | collective-permute-start | bytes 1179656 | tf_op jit(solution)/shard_map/ppermute | solution.py:446
  69.4 0.6 slice_bitcast_fusion.merged
  69.9 2.4 %update_factors.1.coefs = f32[10,8,128]{2,1,0:T(8,128)} custom-call(s32[128]{0:T(128)} %owner_map_hbm.3, s32[128]{0:T(128)} %dip_class_hbm.1, f32[8,128]{1,0:T(8,128)} %slice_bitcast_fusion.merged), custom_call_target="tpu_custom_call" | custom-call | tf_op jit(solution)/shard_map/update_factors/pallas_call | solution.py:154
  72.4 5.8 %collective-permute-done.lower = f32[6,16,8,128]{3,2,1,0:T(8,128)S(1)} collective-permute-done((f32[6,16,8,128]{3,2,1,0:T(8,128)S(1)}, f32[6,16,8,128]{3,2,1,0:T(8,128)S(1)}, u32[]{:S(2)}, u32[]{:S(2)}) %collective-permute-start) | collective-permute-done | bytes 393248 | tf_op jit(solution)/shard_map/ppermute | solution.py:445
  78.2 0.0 collective-permute-done.1.upper
  78.2 0.0 copy-start
  78.2 0.8 copy-done
  79.0 9.2 %smooth_image.1 = f32[4,8,4096]{2,1,0:T(8,128)} custom-call(f32[10,8,128]{2,1,0:T(8,128)S(1)} %copy-done, f32[6,16,8,128]{3,2,1,0:T(8,128)S(1)} %collective-permute-done.lower, f32[8,16,8,128]{3,2,1,0:T(8,128)S(1)} %bitcast.6, f32[6,16,8,128]{3,2,1,0:T(8,128)S(1)} %collective-permute-done.1.upper), custom_call_target="tpu_custom_call" | custom-call | tf_op jit(solution)/shard_map/smooth_image/pallas_call | solution.py:423
Async XLA Ops:
  66.6 11.6 %collective-permute-start = (f32[6,16,8,128]{3,2,1,0:T(8,128)S(1)}, f32[6,16,8,128]{3,2,1,0:T(8,128)S(1)}, u32[]{:S(2)}, u32[]{:S(2)}) collective-permute-start(f32[6,16,8,128]{3,2,1,0:T(8,128)S(1)} %bitcast.8), channel_id=1, source_target_pairs={{0,1},{1,2},{2,3},{3,0},{4,5},{5,6},{6,7},{7,4},{8,9},{9,10},{10,1... | collective-permute-start | bytes 1179656 | tf_op jit(solution)/shard_map/ppermute | solution.py:445
  67.9 10.3 %collective-permute-start.1 = (f32[6,16,8,128]{3,2,1,0:T(8,128)S(1)}, f32[6,16,8,128]{3,2,1,0:T(8,128)S(1)}, u32[]{:S(2)}, u32[]{:S(2)}) collective-permute-start(f32[6,16,8,128]{3,2,1,0:T(8,128)S(1)} %bitcast.7), channel_id=1, source_target_pairs={{1,0},{2,1},{3,2},{0,3},{5,4},{6,5},{7,6},{4,7},{9,8},{10,9},{11,1... | collective-permute-start | bytes 1179656 | tf_op jit(solution)/shard_map/ppermute | solution.py:446
  78.2 0.8 copy-start
